TPU v7x, 32 devices: a whole 2x2x4 slice. The times are simulated.
32 devices in a mesh: grp: 8 (over y, x, core), fsdp: 4 (over z).
Axes of the slice: x: 2, y: 2, z: 4, core: 2. Of those that a mesh axis runs over, the one named last changes fastest.
Arguments:
- inputs: bfloat16 [8192, 8192], P(('grp', 'fsdp')), may hold values from -6 to 6
- upstream: bfloat16 [8192, 1024], P(('grp', 'fsdp')), may hold values from -12 to 12
- value_weight: bfloat16 [8192, 1024], P('fsdp'), may hold values from -0.0625 to 0.0625
- adapter_in: bfloat16 [8192, 8], replicated, may hold values from -0.0625 to 0.0625
- adapter_out: bfloat16 [8, 1024], replicated, may hold values from -0.1875 to 0.1875
- sign_seed: int32 [1], replicated, may hold values from 0 to 1073741823
Outputs:
- input_grads: bfloat16 [8192, 8192], P(('grp', 'fsdp'))
- features: float32 [32, 4096], P(('grp', 'fsdp'))
- mean_grad: float32 [73728], P('fsdp')
All inputs are finite; a program needn't handle non-finite values.
Results may differ from a plain program's by a relative error of at most 0.005.
Values may be sent and summed in bfloat16 or wider, within the bound.
No kernel may reach another device: no remote copies, remote signals or barrier semaphores. Data moves between devices by JAX's collectives and lax.ppermute only.
A program may use at most 128 MiB of HBM per device.

v0:
```python
import math

import jax
import jax.numpy as jnp
from jax import lax
from jax.sharding import PartitionSpec as P

PROJ = 4096


lowrank_scale_factor = 2.0


def contract_last(left, right):
    return lax.dot_general(
        left, right, (((1,), (1,)), ((), ())), preferred_element_type=jnp.float32
    )


def leading_contraction(left, right):
    return lax.dot_general(
        left, right, (((0,), (0,)), ((), ())), preferred_element_type=jnp.float32
    )


def make_signs(start, count, width, seed_value):
    rows = start + lax.broadcasted_iota(jnp.int32, (count, 1), 0)
    columns = lax.broadcasted_iota(jnp.int32, (1, width), 1)
    mixed = rows * -1640531535 + columns * -2048144789 + seed_value * 668265263
    mixed = mixed ^ mixed >> 15 & 131071
    mixed = mixed * -1028477387
    mixed = mixed ^ mixed >> 13 & 524287
    return (1 - 2 * (mixed >> 16 & 1)).astype(jnp.bfloat16)


def per_device(inputs, upstream, value_weight, adapter_in, adapter_out, sign_seed):
    passed_along = contract_last(upstream, adapter_out)
    adapter_expanded = adapter_in.astype(jnp.float32)
    col_count = value_weight.shape[0]
    adapter_slice = lax.dynamic_slice_in_dim(
        adapter_expanded, lax.axis_index("fsdp") * col_count, col_count, 0
    )
    piece = lax.all_gather(upstream, "fsdp", axis=0, tiled=True)
    main_part = contract_last(piece, value_weight)
    piece_through = contract_last(piece, adapter_out)
    lowrank_portion = jnp.dot(
        lowrank_scale_factor * piece_through, adapter_slice.T, precision=lax.Precision.HIGHEST
    )
    columns = (main_part + lowrank_portion).astype(jnp.bfloat16)
    input_grads = lax.all_to_all(columns, "fsdp", split_axis=0, concat_axis=1, tiled=True)
    rescaled_values = (lowrank_scale_factor * passed_along).astype(jnp.bfloat16)
    rank_reduced = jnp.dot(inputs, adapter_in, preferred_element_type=jnp.float32).astype(
        jnp.bfloat16
    )
    grad_in = leading_contraction(inputs, rescaled_values)
    output_gradient = lowrank_scale_factor * leading_contraction(rank_reduced, upstream)
    flat = jnp.concatenate([grad_in.reshape(-1), output_gradient.reshape(-1)]).astype(jnp.bfloat16)
    groups = lax.axis_size("fsdp")
    slice_len = flat.shape[0] // groups
    received = lax.all_to_all(
        flat.reshape(groups, slice_len), "fsdp", split_axis=0, concat_axis=0, tiled=True
    )
    block = math.gcd(slice_len, 512)
    first_row = lax.axis_index("fsdp") * slice_len
    seed_value = sign_seed[0]

    def add_block(block_index, total):
        offset = block_index * block
        part = lax.dynamic_slice_in_dim(received, offset, block, 1)
        signs = make_signs(first_row + offset, block, PROJ, seed_value)
        return total + jnp.dot(part, signs, preferred_element_type=jnp.float32)

    partial_feats = lax.fori_loop(
        0, slice_len // block, add_block, jnp.zeros((groups, PROJ), jnp.float32)
    )
    raw = lax.psum_scatter(partial_feats, "fsdp", scatter_dimension=0, tiled=True)
    features = raw * lax.rsqrt(jnp.mean(raw * raw, axis=1, keepdims=True) + 1e-06)
    local_total = jnp.sum(received.astype(jnp.float32), axis=0)
    mean_grad = lax.psum(local_total, "grp") / (lax.axis_size("grp") * groups)
    return (input_grads, features, mean_grad)


def solution(mesh):
    return jax.shard_map(
        per_device,
        mesh=mesh,
        in_specs=(
            P(("grp", "fsdp"), None),
            P(("grp", "fsdp"), None),
            P("fsdp", None),
            P(),
            P(),
            P(),
        ),
        out_specs=(P(("grp", "fsdp"), None), P(("grp", "fsdp"), None), P("fsdp")),
        check_vma=False,
    )
```

profile of v0, /device:TPU:0, one launch (start us, length us, event | category | flops | bytes accessed | tf_op | source)
XLA Modules:
  0.0 264.7 jit_solution(8746733007855314452)
XLA Ops:
  15.5 3.7 %fusion.22 = bf16[1,8,8,128]{3,2,1,0:T(8,128)(2,1)S(1)} fusion(bf16[256,1024]{1,0:T(8,128)(2,1)S(1)} %copy-done.1, bf16[256,8192]{1,0:T(8,128)(2,1)} %param.8, bf16[8192,8]{0,1:T(8,128)(2,1)S(1)} %copy-done), kind=kOutput, calls=%fused_computation.30 | convolution fusion | flops 37767168 | bytes 4866048 | tf_op jit(solution)/shard_map/dot_general | solution.py:21
  22.0 6.3 %all-to-all-start.1 = ((bf16[4,2,9216]{2,1,0:T(2,128)(2,1)}), bf16[4,2,9216]{2,1,0:T(2,128)(2,1)S(1)}, u32[]{:S(2)}, u32[]{:S(2)}) async-start(bf16[4,2,9216]{2,1,0:T(2,128)(2,1)} %reshape.59), calls=%async_computation.1 | async-start | bytes 294912 | tf_op jit(solution)/shard_map/all_to_all | solution.py:60
  29.6 9.3 %all-to-all-done.1 = bf16[4,2,9216]{2,1,0:T(2,128)(2,1)S(1)} async-done(((bf16[4,2,9216]{2,1,0:T(2,128)(2,1)}), bf16[4,2,9216]{2,1,0:T(2,128)(2,1)S(1)}, u32[]{:S(2)}, u32[]{:S(2)}) %all-to-all-start.1) | async-done | bytes 147488 | tf_op jit(solution)/shard_map/all_to_all | solution.py:60
  39.9 22.3 %all-gather.2.cloned.1.call-done = bf16[1024,1024]{1,0:T(8,128)(2,1)} async-done(((bf16[256,1024]{1,0:T(8,128)(2,1)}), bf16[1024,1024]{1,0:T(8,128)(2,1)}) %all-gather.2.cloned.1.call-update) | async-done | bytes 2097168 | tf_op jit(solution)/shard_map/all_gather | solution.py:43
  64.5 7.0 %fusion.28 = f32[1024,2048]{1,0:T(8,128)S(1)} fusion(bf16[1024,1024]{1,0:T(8,128)(2,1)} %all-gather.2.cloned.1.call-done, bf16[2048,1024]{1,0:T(8,128)(2,1)} %param.10), kind=kOutput, calls=%fused_computation.45 | convolution fusion | flops 4294967296 | bytes 14680064 | tf_op jit(solution)/shard_map/dot_general | solution.py:15
  71.5 5.5 %add_convert_fusion = bf16[1024,2048]{1,0:T(8,128)(2,1)} fusion(f32[1024,2048]{1,0:T(8,128)S(1)} %fusion.28, f32[1024,8]{0,1:T(8,128)S(1)} %convolution_multiply_fusion, bf16[8192,8]{0,1:T(8,128)(2,1)S(1)} %copy-done, s32[]{:T(128)S(6)} %select_n.12), kind=kOutput, calls=%fused_computation.26 | convolution fusion | flops 205520896 | bytes 12648452 | tf_op jit(solution)/shard_map/dot_general | solution.py:46
  77.0 4.8 %all-to-all-start = ((bf16[4,256,2048]{2,1,0:T(8,128)(2,1)}), bf16[4,256,2048]{2,1,0:T(8,128)(2,1)}, u32[]{:S(2)}, u32[]{:S(2)}) async-start(bf16[4,256,2048]{2,1,0:T(8,128)(2,1)} %bitcast.27), calls=%async_computation | async-start | bytes 8388608 | tf_op jit(solution)/shard_map/all_to_all | solution.py:50
  82.1 129.8 %while.16 = (s32[]{:T(128)}, f32[4,4096]{1,0:T(4,128)S(1)}, bf16[4,18432]{1,0:T(4,128)(2,1)S(1)}, s32[]{:T(128)}, s32[]{:T(128)}, /*index=5*/s32[]{:T(128)}, s32[]{:T(128)}, s32[]{:T(128)}, s32[]{:T(128)}) while((s32[]{:T(128)}, f32[4,4096]{1,0:T(4,128)S(1)}, bf16[4,18432]{1,0:T(4,128)(2,1)S(1)}, s32[]{:T(128)}, s32[]{:T(128)}, ...), condition=%wide.region_1.0_spmd.clone, body=%wide.region_0.0_spmd.clone.sunk | while | flops 46175240 | bytes 172205 | solution.py:73
  82.1 3.6 %convolution_add_fusion.2 = f32[4,4096]{1,0:T(4,128)S(1)} fusion(s32[]{:T(128)} %get-tuple-element.215, s32[4096]{0:T(1024)S(1)} %iota_multiply_fusion.2, s32[512]{0:T(512)S(1)} %add_multiply_fusion.2, f32[4,4096]{1,0:T(4,128)S(1)} %get-tuple-element.203, pred[]{:T(512)S(6)} %compare.3, bf16[4,18432]{1,0:T(4,128)(2,1)S(1)} %get-tuple-element.213, ...), kind=kOutput, calls=%fused_computation.1.clone.1 | convolution fusion | flops 46170112 | bytes 153609 | tf_op jit(solution)/shard_map/while/body/eval_jaxpr/dot_general | solution.py:71
  85.7 3.6 %convolution_add_fusion.2 = f32[4,4096]{1,0:T(4,128)S(1)} fusion(s32[]{:T(128)} %get-tuple-element.215, s32[4096]{0:T(1024)S(1)} %iota_multiply_fusion.2, s32[512]{0:T(512)S(1)} %add_multiply_fusion.2, f32[4,4096]{1,0:T(4,128)S(1)} %get-tuple-element.203, pred[]{:T(512)S(6)} %compare.3, bf16[4,18432]{1,0:T(4,128)(2,1)S(1)} %get-tuple-element.213, ...), kind=kOutput, calls=%fused_computation.1.clone.1 | convolution fusion | flops 46170112 | bytes 153609 | tf_op jit(solution)/shard_map/while/body/eval_jaxpr/dot_general | solution.py:71
  89.3 3.6 %convolution_add_fusion.2 = f32[4,4096]{1,0:T(4,128)S(1)} fusion(s32[]{:T(128)} %get-tuple-element.215, s32[4096]{0:T(1024)S(1)} %iota_multiply_fusion.2, s32[512]{0:T(512)S(1)} %add_multiply_fusion.2, f32[4,4096]{1,0:T(4,128)S(1)} %get-tuple-element.203, pred[]{:T(512)S(6)} %compare.3, bf16[4,18432]{1,0:T(4,128)(2,1)S(1)} %get-tuple-element.213, ...), kind=kOutput, calls=%fused_computation.1.clone.1 | convolution fusion | flops 46170112 | bytes 153609 | tf_op jit(solution)/shard_map/while/body/eval_jaxpr/dot_general | solution.py:71
  92.9 3.6 %convolution_add_fusion.2 = f32[4,4096]{1,0:T(4,128)S(1)} fusion(s32[]{:T(128)} %get-tuple-element.215, s32[4096]{0:T(1024)S(1)} %iota_multiply_fusion.2, s32[512]{0:T(512)S(1)} %add_multiply_fusion.2, f32[4,4096]{1,0:T(4,128)S(1)} %get-tuple-element.203, pred[]{:T(512)S(6)} %compare.3, bf16[4,18432]{1,0:T(4,128)(2,1)S(1)} %get-tuple-element.213, ...), kind=kOutput, calls=%fused_computation.1.clone.1 | convolution fusion | flops 46170112 | bytes 153609 | tf_op jit(solution)/shard_map/while/body/eval_jaxpr/dot_general | solution.py:71
  96.5 3.6 %convolution_add_fusion.2 = f32[4,4096]{1,0:T(4,128)S(1)} fusion(s32[]{:T(128)} %get-tuple-element.215, s32[4096]{0:T(1024)S(1)} %iota_multiply_fusion.2, s32[512]{0:T(512)S(1)} %add_multiply_fusion.2, f32[4,4096]{1,0:T(4,128)S(1)} %get-tuple-element.203, pred[]{:T(512)S(6)} %compare.3, bf16[4,18432]{1,0:T(4,128)(2,1)S(1)} %get-tuple-element.213, ...), kind=kOutput, calls=%fused_computation.1.clone.1 | convolution fusion | flops 46170112 | bytes 153609 | tf_op jit(solution)/shard_map/while/body/eval_jaxpr/dot_general | solution.py:71
  100.1 3.6 %convolution_add_fusion.2 = f32[4,4096]{1,0:T(4,128)S(1)} fusion(s32[]{:T(128)} %get-tuple-element.215, s32[4096]{0:T(1024)S(1)} %iota_multiply_fusion.2, s32[512]{0:T(512)S(1)} %add_multiply_fusion.2, f32[4,4096]{1,0:T(4,128)S(1)} %get-tuple-element.203, pred[]{:T(512)S(6)} %compare.3, bf16[4,18432]{1,0:T(4,128)(2,1)S(1)} %get-tuple-element.213, ...), kind=kOutput, calls=%fused_computation.1.clone.1 | convolution fusion | flops 46170112 | bytes 153609 | tf_op jit(solution)/shard_map/while/body/eval_jaxpr/dot_general | solution.py:71
  103.7 3.6 %convolution_add_fusion.2 = f32[4,4096]{1,0:T(4,128)S(1)} fusion(s32[]{:T(128)} %get-tuple-element.215, s32[4096]{0:T(1024)S(1)} %iota_multiply_fusion.2, s32[512]{0:T(512)S(1)} %add_multiply_fusion.2, f32[4,4096]{1,0:T(4,128)S(1)} %get-tuple-element.203, pred[]{:T(512)S(6)} %compare.3, bf16[4,18432]{1,0:T(4,128)(2,1)S(1)} %get-tuple-element.213, ...), kind=kOutput, calls=%fused_computation.1.clone.1 | convolution fusion | flops 46170112 | bytes 153609 | tf_op jit(solution)/shard_map/while/body/eval_jaxpr/dot_general | solution.py:71
  107.3 3.6 %convolution_add_fusion.2 = f32[4,4096]{1,0:T(4,128)S(1)} fusion(s32[]{:T(128)} %get-tuple-element.215, s32[4096]{0:T(1024)S(1)} %iota_multiply_fusion.2, s32[512]{0:T(512)S(1)} %add_multiply_fusion.2, f32[4,4096]{1,0:T(4,128)S(1)} %get-tuple-element.203, pred[]{:T(512)S(6)} %compare.3, bf16[4,18432]{1,0:T(4,128)(2,1)S(1)} %get-tuple-element.213, ...), kind=kOutput, calls=%fused_computation.1.clone.1 | convolution fusion | flops 46170112 | bytes 153609 | tf_op jit(solution)/shard_map/while/body/eval_jaxpr/dot_general | solution.py:71
  110.9 3.6 %convolution_add_fusion.2 = f32[4,4096]{1,0:T(4,128)S(1)} fusion(s32[]{:T(128)} %get-tuple-element.215, s32[4096]{0:T(1024)S(1)} %iota_multiply_fusion.2, s32[512]{0:T(512)S(1)} %add_multiply_fusion.2, f32[4,4096]{1,0:T(4,128)S(1)} %get-tuple-element.203, pred[]{:T(512)S(6)} %compare.3, bf16[4,18432]{1,0:T(4,128)(2,1)S(1)} %get-tuple-element.213, ...), kind=kOutput, calls=%fused_computation.1.clone.1 | convolution fusion | flops 46170112 | bytes 153609 | tf_op jit(solution)/shard_map/while/body/eval_jaxpr/dot_general | solution.py:71
  114.5 3.6 %convolution_add_fusion.2 = f32[4,4096]{1,0:T(4,128)S(1)} fusion(s32[]{:T(128)} %get-tuple-element.215, s32[4096]{0:T(1024)S(1)} %iota_multiply_fusion.2, s32[512]{0:T(512)S(1)} %add_multiply_fusion.2, f32[4,4096]{1,0:T(4,128)S(1)} %get-tuple-element.203, pred[]{:T(512)S(6)} %compare.3, bf16[4,18432]{1,0:T(4,128)(2,1)S(1)} %get-tuple-element.213, ...), kind=kOutput, calls=%fused_computation.1.clone.1 | convolution fusion | flops 46170112 | bytes 153609 | tf_op jit(solution)/shard_map/while/body/eval_jaxpr/dot_general | solution.py:71
  118.2 3.6 %convolution_add_fusion.2 = f32[4,4096]{1,0:T(4,128)S(1)} fusion(s32[]{:T(128)} %get-tuple-element.215, s32[4096]{0:T(1024)S(1)} %iota_multiply_fusion.2, s32[512]{0:T(512)S(1)} %add_multiply_fusion.2, f32[4,4096]{1,0:T(4,128)S(1)} %get-tuple-element.203, pred[]{:T(512)S(6)} %compare.3, bf16[4,18432]{1,0:T(4,128)(2,1)S(1)} %get-tuple-element.213, ...), kind=kOutput, calls=%fused_computation.1.clone.1 | convolution fusion | flops 46170112 | bytes 153609 | tf_op jit(solution)/shard_map/while/body/eval_jaxpr/dot_general | solution.py:71
  121.8 3.6 %convolution_add_fusion.2 = f32[4,4096]{1,0:T(4,128)S(1)} fusion(s32[]{:T(128)} %get-tuple-element.215, s32[4096]{0:T(1024)S(1)} %iota_multiply_fusion.2, s32[512]{0:T(512)S(1)} %add_multiply_fusion.2, f32[4,4096]{1,0:T(4,128)S(1)} %get-tuple-element.203, pred[]{:T(512)S(6)} %compare.3, bf16[4,18432]{1,0:T(4,128)(2,1)S(1)} %get-tuple-element.213, ...), kind=kOutput, calls=%fused_computation.1.clone.1 | convolution fusion | flops 46170112 | bytes 153609 | tf_op jit(solution)/shard_map/while/body/eval_jaxpr/dot_general | solution.py:71
  125.4 3.6 %convolution_add_fusion.2 = f32[4,4096]{1,0:T(4,128)S(1)} fusion(s32[]{:T(128)} %get-tuple-element.215, s32[4096]{0:T(1024)S(1)} %iota_multiply_fusion.2, s32[512]{0:T(512)S(1)} %add_multiply_fusion.2, f32[4,4096]{1,0:T(4,128)S(1)} %get-tuple-element.203, pred[]{:T(512)S(6)} %compare.3, bf16[4,18432]{1,0:T(4,128)(2,1)S(1)} %get-tuple-element.213, ...), kind=kOutput, calls=%fused_computation.1.clone.1 | convolution fusion | flops 46170112 | bytes 153609 | tf_op jit(solution)/shard_map/while/body/eval_jaxpr/dot_general | solution.py:71
  168.6 3.6 %convolution_add_fusion.2 = f32[4,4096]{1,0:T(4,128)S(1)} fusion(s32[]{:T(128)} %get-tuple-element.215, s32[4096]{0:T(1024)S(1)} %iota_multiply_fusion.2, s32[512]{0:T(512)S(1)} %add_multiply_fusion.2, f32[4,4096]{1,0:T(4,128)S(1)} %get-tuple-element.203, pred[]{:T(512)S(6)} %compare.3, bf16[4,18432]{1,0:T(4,128)(2,1)S(1)} %get-tuple-element.213, ...), kind=kOutput, calls=%fused_computation.1.clone.1 | convolution fusion | flops 46170112 | bytes 153609 | tf_op jit(solution)/shard_map/while/body/eval_jaxpr/dot_general | solution.py:71
  214.1 33.5 %all-reduce.6.cloned.1.call-done = f32[4,4096]{1,0:T(4,128)} async-done(((f32[4,4096]{1,0:T(4,128)}), f32[4,4096]{1,0:T(4,128)}) %all-reduce.6.cloned.1.call-update) | async-done | bytes 65552
  252.4 4.8 %copy.18 = bf16[4,32,8,2048]{3,2,0,1:T(8,128)(2,1)} copy(bf16[4,32,8,2048]{3,2,1,0:T(8,128)(2,1)} %bitcast.6) | data formatting | bytes 8388608 | tf_op jit(solution)/shard_map/all_to_all | solution.py:50
  (129 shorter events, 100.0 us)
Async XLA Ops:
  8.0 7.5 %copy-start = (bf16[8192,8]{0,1:T(8,128)(2,1)S(1)}, bf16[8192,8]{0,1:T(8,128)(2,1)}, u32[]{:S(2)}) copy-start(bf16[8192,8]{0,1:T(8,128)(2,1)} %param.11) | copy-start | bytes 393220
  8.0 21.0 %copy-start.4 = (u32[32]{0:T(128)S(1)}, u32[32]{0:T(128)}, u32[]{:S(2)}) copy-start(u32[32]{0:T(128)} %constant.152) | copy-start | bytes 388
  8.0 7.4 %copy-start.1 = (bf16[256,1024]{1,0:T(8,128)(2,1)S(1)}, bf16[256,1024]{1,0:T(8,128)(2,1)}, u32[]{:S(2)}) copy-start(bf16[256,1024]{1,0:T(8,128)(2,1)} %param.9) | copy-start | bytes 1572868
  8.0 54.2 %all-gather.2.cloned.1.call-start = ((), (), s32[]{:S(2)}) async-start(), calls=%async_computation.2 | async-start | bytes 2621440 | tf_op jit(solution)/shard_map/all_gather | solution.py:43
  8.8 53.5 %copy-start.2 = (bf16[8,1024]{1,0:T(8,128)(2,1)S(1)}, bf16[8,1024]{1,0:T(8,128)(2,1)}, u32[]{:S(2)}) copy-start(bf16[8,1024]{1,0:T(8,128)(2,1)} %param.12) | copy-start | bytes 49156
  22.0 16.8 %all-to-all-start.1 = ((bf16[4,2,9216]{2,1,0:T(2,128)(2,1)}), bf16[4,2,9216]{2,1,0:T(2,128)(2,1)S(1)}, u32[]{:S(2)}, u32[]{:S(2)}) async-start(bf16[4,2,9216]{2,1,0:T(2,128)(2,1)} %reshape.59), calls=%async_computation.1 | async-start | bytes 294912 | tf_op jit(solution)/shard_map/all_to_all | solution.py:60
  28.4 184.2 %all-reduce.4.cloned.1.call-start = ((), (), s32[]{:S(2)}) async-start(), calls=%async_computation.3 | async-start | bytes 147456 | tf_op jit(solution)/shard_map/psum | solution.py:79
  77.0 175.5 %all-to-all-start = ((bf16[4,256,2048]{2,1,0:T(8,128)(2,1)}), bf16[4,256,2048]{2,1,0:T(8,128)(2,1)}, u32[]{:S(2)}, u32[]{:S(2)}) async-start(bf16[4,256,2048]{2,1,0:T(8,128)(2,1)} %bitcast.27), calls=%async_computation | async-start | bytes 8388608 | tf_op jit(solution)/shard_map/all_to_all | solution.py:50
  81.8 165.7 %all-reduce.6.cloned.1.call-start = ((), (), s32[]{:S(2)}) async-start(), calls=%async_computation.4 | async-start | bytes 131072
  211.9 0.6 copy-start.3
Sparse Core Ops, SparseCore 0:
  10.4 51.7 all-gather.1
Sparse Core Ops, SparseCore 1:
  40.0 49.6 all-reduce.3
  212.6 34.9 all-reduce.5
where the time goes:
time: 265 us
  matrix products  151 us (57%)
  waiting for transfers between devices  65.8 us (25%)
  between operations  16.9 us (6%)
  starting transfers between devices  11.4 us (4%)
  local copies, waits for them, and re-layouts  10.6 us (4%)
  other arithmetic  8.5 us (3%)
    dot_general x36, matrix products, add_block(): return total + jnp.dot(part, signs, preferred_element_type=jnp.float32)  129 us
    unnamed x4, waiting for transfers between devices  34.2 us
    all_gather x1, waiting for transfers between devices, per_device(): piece = lax.all_gather(upstream, 'fsdp', axis=0, tiled=True)  22.3 us
    all_to_all x1, waiting for transfers between devices, per_device(): lax.all_to_all(flat.reshape(groups, slice_len), 'fsdp', split_axis=0, con...  9.26 us
    dot_general x2, matrix products, contract_last(): lax.dot_general(left, right, (((1,), (1,)), ((), ())), preferred_element_...  9.25 us
    dot_general x2, matrix products, leading_contraction(): lax.dot_general(left, right, (((0,), (0,)), ((), ())), preferred_element_...  7.15 us
    all_to_all x1, starting transfers between devices, per_device(): lax.all_to_all(flat.reshape(groups, slice_len), 'fsdp', split_axis=0, con...  6.32 us
    dot_general x1, matrix products, per_device(): jnp.dot(lowrank_scale_factor * piece_through, adapter_slice.T, precision=...  5.48 us
  transfers between devices with their start and end apart: 5, of which 3 were waited for; matrix products, arithmetic and copies ran while one was open for 62% of the time, Pallas kernels for 0%

commit v1 on v0

v1 whole, which is shorter than its diff:
```python
import math

import jax
import jax.numpy as jnp
from jax import lax
from jax.sharding import PartitionSpec as P

PROJ = 4096

lowrank_scale_factor = 2.0


def contract_last(left, right):
    return lax.dot_general(
        left, right, (((1,), (1,)), ((), ())), preferred_element_type=jnp.float32
    )


def leading_contraction(left, right):
    return lax.dot_general(
        left, right, (((0,), (0,)), ((), ())), preferred_element_type=jnp.float32
    )


def make_signs(start, count, width, seed_value):
    rows = start + lax.broadcasted_iota(jnp.int32, (count, 1), 0)
    columns = lax.broadcasted_iota(jnp.int32, (1, width), 1)
    mixed = rows * -1640531535 + columns * -2048144789 + seed_value * 668265263
    mixed = mixed ^ lax.shift_right_logical(mixed, 15)
    mixed = mixed * 181057748
    mixed = mixed ^ lax.shift_left(mixed, 13)
    return jnp.where(mixed < 0, -1.0, 1.0).astype(jnp.bfloat16)


def per_device(inputs, upstream, value_weight, adapter_in, adapter_out, sign_seed):
    both = ("fsdp", "grp")
    groups = lax.axis_size("fsdp")
    members = lax.axis_size("grp")
    passed_along = contract_last(upstream, adapter_out)
    adapter_expanded = adapter_in.astype(jnp.float32)
    col_count = value_weight.shape[0]
    adapter_slice = lax.dynamic_slice_in_dim(
        adapter_expanded, lax.axis_index("fsdp") * col_count, col_count, 0
    )
    piece = lax.all_gather(upstream, "fsdp", axis=0, tiled=True)
    main_part = contract_last(piece, value_weight)
    piece_through = contract_last(piece, adapter_out)
    lowrank_portion = jnp.dot(
        lowrank_scale_factor * piece_through, adapter_slice.T, precision=lax.Precision.HIGHEST
    )
    columns = (main_part + lowrank_portion).astype(jnp.bfloat16)
    input_grads = lax.all_to_all(columns, "fsdp", split_axis=0, concat_axis=1, tiled=True)

    rescaled_values = (lowrank_scale_factor * passed_along).astype(jnp.bfloat16)
    rank_reduced = jnp.dot(inputs, adapter_in, preferred_element_type=jnp.float32).astype(
        jnp.bfloat16
    )
    grad_in = leading_contraction(inputs, rescaled_values)
    output_gradient = lowrank_scale_factor * leading_contraction(rank_reduced, upstream)
    flat = jnp.concatenate([grad_in.reshape(-1), output_gradient.reshape(-1)]).astype(jnp.bfloat16)
    devices = groups * members
    slice_len = flat.shape[0] // devices
    received = lax.all_to_all(
        flat.reshape(devices, slice_len), both, split_axis=0, concat_axis=0, tiled=True
    )
    local_total = jnp.sum(received.astype(jnp.float32), axis=0) / devices
    mean_grad = lax.all_to_all(
        jnp.broadcast_to(local_total, (members, slice_len)), "grp", split_axis=0, concat_axis=0, tiled=True
    ).reshape(-1)

    first_row = (lax.axis_index("fsdp") * members + lax.axis_index("grp")) * slice_len
    signs = make_signs(first_row, slice_len, PROJ, sign_seed[0])
    partial_feats = jnp.dot(received, signs, preferred_element_type=jnp.float32)
    parts = lax.all_to_all(partial_feats, both, split_axis=0, concat_axis=0, tiled=True)
    raw = jnp.sum(parts, axis=0, keepdims=True)
    features = raw * lax.rsqrt(jnp.mean(raw * raw, axis=1, keepdims=True) + 1e-06)
    return (input_grads, features, mean_grad)


def solution(mesh):
    return jax.shard_map(
        per_device,
        mesh=mesh,
        in_specs=(
            P(("grp", "fsdp"), None),
            P(("grp", "fsdp"), None),
            P("fsdp", None),
            P(),
            P(),
            P(),
        ),
        out_specs=(P(("grp", "fsdp"), None), P(("grp", "fsdp"), None), P("fsdp")),
        check_vma=False,
    )
```

time: 265 us -> 189 us (0.71)
  matrix products: 151 us -> 33 us
  waiting for transfers between devices: 65.8 us -> 105 us
  starting transfers between devices: 11.4 us -> 19.5 us
  other arithmetic: 8.5 us -> 3.14 us
    dot_general x36 -> x1, matrix products: 129 us -> 12.6 us  [per_device(): partial_feats = jnp.dot(received, signs, preferred_element_type=jnp.float32)]
    all_to_all x1, waiting for transfers between devices: 0.01 us -> 91.3 us  [per_device(): lax.all_to_all(columns, 'fsdp', split_axis=0, concat_axis=1, tiled=True)]
    unnamed x4 -> x1, waiting for transfers between devices: 34.2 us -> 0.68 us
    all_gather x1, waiting for transfers between devices: 22.3 us -> 0.02 us  [per_device(): piece = lax.all_gather(upstream, 'fsdp', axis=0, tiled=True)]
    all_to_all x1 -> x3, starting transfers between devices: 6.32 us -> 14.7 us  [the longest x1 7.3 us: per_device(): lax.all_to_all(flat.reshape(devices, slice_len), both, split_axis=0, conc...]
    all_to_all x1 -> x3, waiting for transfers between devices: 9.26 us -> 13.3 us  [the longest x1 11.1 us: per_device(): lax.all_to_all(flat.reshape(devices, slice_len), both, split_axis=0, conc...]
  transfers between devices with their start and end apart: 5 -> 5, of which waited for: 3 -> 3; matrix products, arithmetic and copies ran while one was open for 62% -> 23% of each run, Pallas kernels for 0% -> 0%
where the time goes in v1:
time: 189 us; the launch traced here: 188 us
  waiting for transfers between devices  105 us (56%)
  matrix products  33 us (17%)
  starting transfers between devices  19.5 us (10%)
  between operations  15.6 us (8%)
  local copies, waits for them, and re-layouts  12 us (6%)
  other arithmetic  3.14 us (2%)
    all_to_all x1, waiting for transfers between devices, per_device(): lax.all_to_all(columns, 'fsdp', split_axis=0, concat_axis=1, tiled=True)  91.3 us
    dot_general x1, matrix products, per_device(): partial_feats = jnp.dot(received, signs, preferred_element_type=jnp.float32)  12.6 us
    all_to_all x1, waiting for transfers between devices, per_device(): lax.all_to_all(flat.reshape(devices, slice_len), both, split_axis=0, conc...  11.1 us
    dot_general x2, matrix products, contract_last(): lax.dot_general(left, right, (((1,), (1,)), ((), ())), preferred_element_...  7.8 us
    all_to_all x1, starting transfers between devices, per_device(): lax.all_to_all(flat.reshape(devices, slice_len), both, split_axis=0, conc...  7.3 us
    dot_general x2, matrix products, leading_contraction(): lax.dot_general(left, right, (((0,), (0,)), ((), ())), preferred_element_...  7.15 us
    dot_general x1, matrix products, per_device(): jnp.dot(lowrank_scale_factor * piece_through, adapter_slice.T, precision=...  5.47 us
    all_to_all x1, starting transfers between devices, per_device(): lax.all_to_all(columns, 'fsdp', split_axis=0, concat_axis=1, tiled=True)  4.84 us
  transfers between devices with their start and end apart: 5, of which 3 were waited for; matrix products, arithmetic and copies ran while one was open for 23% of the time, Pallas kernels for 0%

profile of v1, /device:TPU:0, one launch (start us, length us, event | category | flops | bytes accessed | tf_op | source)
XLA Modules:
  0.0 188.5 jit_solution(8914029964665227998)
XLA Ops:
  7.2 0.7 all-gather.2.cloned.1.call-update
  7.9 3.5 %fusion.3 = bf16[8192,8]{0,1:T(8,128)(2,1)S(1)} fusion(bf16[256,8192]{1,0:T(8,128)(2,1)} %param.6, bf16[256,1024]{1,0:T(8,128)(2,1)} %param.7, bf16[8,1024]{1,0:T(8,128)(2,1)} %param.10), kind=kOutput, calls=%fused_computation.7 | convolution fusion | flops 37818368 | bytes 4866048 | tf_op jit(solution)/shard_map/dot_general | solution.py:20
  11.4 1.0 copy.13
  12.4 2.2 %reshape.78 = bf16[65536]{0:T(1024)(128)(2,1)S(1)} reshape(bf16[8192,8]{1,0:T(8,128)(2,1)S(1)} %copy.13) | data formatting | bytes 262144 | tf_op jit(solution)/shard_map/reshape | solution.py:60
  14.6 3.7 %fusion.6 = bf16[1,8,8,128]{3,2,1,0:T(8,128)(2,1)S(1)} fusion(bf16[256,1024]{1,0:T(8,128)(2,1)S(1)} %copy-done.1, bf16[256,8192]{1,0:T(8,128)(2,1)} %param.6, bf16[8192,8]{0,1:T(8,128)(2,1)S(1)} %copy-done), kind=kOutput, calls=%fused_computation.13 | convolution fusion | flops 37767168 | bytes 4866048 | tf_op jit(solution)/shard_map/dot_general | solution.py:20
  18.9 1.5 reduce.2
  20.4 0.7 reshape.81
  21.1 7.3 %all-to-all-start.1 = ((bf16[32,2,1152]{2,1,0:T(2,128)(2,1)}), bf16[32,2,1152]{2,1,0:T(2,128)(2,1)S(1)}, u32[]{:S(2)}, u32[]{:S(2)}) async-start(bf16[32,2,1152]{2,1,0:T(2,128)(2,1)} %reshape.81), calls=%async_computation.1 | async-start | bytes 294912 | tf_op jit(solution)/shard_map/all_to_all | solution.py:63
  29.1 11.1 %all-to-all-done.1 = bf16[32,2,1152]{2,1,0:T(2,128)(2,1)S(1)} async-done(((bf16[32,2,1152]{2,1,0:T(2,128)(2,1)}), bf16[32,2,1152]{2,1,0:T(2,128)(2,1)S(1)}, u32[]{:S(2)}, u32[]{:S(2)}) %all-to-all-start.1) | async-done | bytes 147488 | tf_op jit(solution)/shard_map/all_to_all | solution.py:63
  40.3 0.7 broadcast_in_dim.15
  41.0 3.7 %all-to-all-start.3 = ((f32[8,1,2304]{2,1,0:T(1,128)}), f32[8,1,2304]{2,1,0:T(1,128)S(1)}, u32[]{:S(2)}, u32[]{:S(2)}) async-start(f32[8,1,2304]{2,1,0:T(1,128)} %broadcast_in_dim.15), calls=%async_computation.3 | async-start | bytes 147456 | tf_op jit(solution)/shard_map/all_to_all | solution.py:67
  44.6 12.6 %fusion.4 = f32[32,1,4096]{2,0,1:T(8,128)S(1)} fusion(s32[]{:T(128)} %bitcast.3, s32[4096]{0:T(1024)S(1)} %iota_multiply_fusion, s32[2304]{0:T(1024)S(1)} %add_multiply_fusion, bf16[32,1,2304]{2,1,0:T(2,128)(2,1)S(1)} %reshape.82), kind=kOutput, calls=%fused_computation.9 | convolution fusion | flops 698351616 | bytes 697348 | tf_op jit(solution)/shard_map/dot_general | solution.py:73
  57.2 1.3 copy.15
  58.6 3.7 %all-to-all-start.2 = ((f32[32,1,4096]{2,1,0:T(1,128)}), f32[32,1,4096]{2,1,0:T(1,128)S(1)}, u32[]{:S(2)}, u32[]{:S(2)}) async-start(f32[32,1,4096]{2,1,0:T(1,128)} %copy.15), calls=%async_computation.2 | async-start | bytes 1048576 | tf_op jit(solution)/shard_map/all_to_all | solution.py:74
  62.3 7.2 %fusion.20 = f32[1024,2048]{1,0:T(8,128)S(1)} fusion(bf16[1024,1024]{1,0:T(8,128)(2,1)} %all-gather.2.cloned.1.call-done, bf16[2048,1024]{1,0:T(8,128)(2,1)} %param.8), kind=kOutput, calls=%fused_computation.37 | convolution fusion | flops 4294967296 | bytes 14680064 | tf_op jit(solution)/shard_map/dot_general | solution.py:14
  69.5 0.6 convolution_multiply_fusion
  70.2 5.5 %add_convert_fusion = bf16[1024,2048]{1,0:T(8,128)(2,1)} fusion(f32[1024,2048]{1,0:T(8,128)S(1)} %fusion.20, f32[1024,8]{0,1:T(8,128)S(1)} %convolution_multiply_fusion, bf16[8192,8]{0,1:T(8,128)(2,1)S(1)} %copy-done, s32[]{:T(128)S(6)} %select_n.7), kind=kOutput, calls=%fused_computation.8 | convolution fusion | flops 205520896 | bytes 12648452 | tf_op jit(solution)/shard_map/dot_general | solution.py:48
  75.6 2.2 %all-to-all-done.2 = f32[32,1,4096]{2,1,0:T(1,128)S(1)} async-done(((f32[32,1,4096]{2,1,0:T(1,128)}), f32[32,1,4096]{2,1,0:T(1,128)S(1)}, u32[]{:S(2)}, u32[]{:S(2)}) %all-to-all-start.2) | async-done | bytes 524320 | tf_op jit(solution)/shard_map/all_to_all | solution.py:74
  77.8 4.8 %all-to-all-start = ((bf16[4,256,2048]{2,1,0:T(8,128)(2,1)}), bf16[4,256,2048]{2,1,0:T(8,128)(2,1)}, u32[]{:S(2)}, u32[]{:S(2)}) async-start(bf16[4,256,2048]{2,1,0:T(8,128)(2,1)} %bitcast.31), calls=%async_computation | async-start | bytes 8388608 | tf_op jit(solution)/shard_map/all_to_all | solution.py:52
  83.0 0.6 multiply_reduce_fusion
  84.3 0.6 broadcast_multiply_fusion
  84.9 91.3 %all-to-all-done = bf16[4,256,2048]{2,1,0:T(8,128)(2,1)} async-done(((bf16[4,256,2048]{2,1,0:T(8,128)(2,1)}), bf16[4,256,2048]{2,1,0:T(8,128)(2,1)}, u32[]{:S(2)}, u32[]{:S(2)}) %all-to-all-start) | async-done | bytes 4194336 | tf_op jit(solution)/shard_map/all_to_all | solution.py:52
  176.2 4.8 %copy.17 = bf16[4,32,8,2048]{3,2,0,1:T(8,128)(2,1)} copy(bf16[4,32,8,2048]{3,2,1,0:T(8,128)(2,1)} %bitcast.8) | data formatting | bytes 8388608 | tf_op jit(solution)/shard_map/all_to_all | solution.py:52
  181.0 0.6 copy.28
  (21 shorter events, 1.2 us)
Async XLA Ops:
  7.2 7.4 %copy-start = (bf16[8192,8]{0,1:T(8,128)(2,1)S(1)}, bf16[8192,8]{0,1:T(8,128)(2,1)}, u32[]{:S(2)}) copy-start(bf16[8192,8]{0,1:T(8,128)(2,1)} %param.9) | copy-start | bytes 393220
  7.2 7.4 %copy-start.1 = (bf16[256,1024]{1,0:T(8,128)(2,1)S(1)}, bf16[256,1024]{1,0:T(8,128)(2,1)}, u32[]{:S(2)}) copy-start(bf16[256,1024]{1,0:T(8,128)(2,1)} %param.7) | copy-start | bytes 1572868
  7.2 55.1 %all-gather.2.cloned.1.call-start = ((), (), s32[]{:S(2)}) async-start(), calls=%async_computation.4 | async-start | bytes 2621440 | tf_op jit(solution)/shard_map/all_gather | solution.py:45
  21.1 19.0 %all-to-all-start.1 = ((bf16[32,2,1152]{2,1,0:T(2,128)(2,1)}), bf16[32,2,1152]{2,1,0:T(2,128)(2,1)S(1)}, u32[]{:S(2)}, u32[]{:S(2)}) async-start(bf16[32,2,1152]{2,1,0:T(2,128)(2,1)} %reshape.81), calls=%async_computation.1 | async-start | bytes 294912 | tf_op jit(solution)/shard_map/all_to_all | solution.py:63
  41.0 17.6 %all-to-all-start.3 = ((f32[8,1,2304]{2,1,0:T(1,128)}), f32[8,1,2304]{2,1,0:T(1,128)S(1)}, u32[]{:S(2)}, u32[]{:S(2)}) async-start(f32[8,1,2304]{2,1,0:T(1,128)} %broadcast_in_dim.15), calls=%async_computation.3 | async-start | bytes 147456 | tf_op jit(solution)/shard_map/all_to_all | solution.py:67
  58.6 19.3 %all-to-all-start.2 = ((f32[32,1,4096]{2,1,0:T(1,128)}), f32[32,1,4096]{2,1,0:T(1,128)S(1)}, u32[]{:S(2)}, u32[]{:S(2)}) async-start(f32[32,1,4096]{2,1,0:T(1,128)} %copy.15), calls=%async_computation.2 | async-start | bytes 1048576 | tf_op jit(solution)/shard_map/all_to_all | solution.py:74
  62.3 7.2 %copy-start.3 = (bf16[8,1024]{1,0:T(8,128)(2,1)S(1)}, bf16[8,1024]{1,0:T(8,128)(2,1)}, u32[]{:S(2)}) copy-start(bf16[8,1024]{1,0:T(8,128)(2,1)} %param.10) | copy-start | bytes 49156
  62.3 7.2 %copy-start.2 = (bf16[1024,1024]{1,0:T(8,128)(2,1)S(1)}, bf16[1024,1024]{1,0:T(8,128)(2,1)}, u32[]{:S(2)}) copy-start(bf16[1024,1024]{1,0:T(8,128)(2,1)} %all-gather.2.cloned.1.call-done) | copy-start | bytes 6291460
  77.8 98.4 %all-to-all-start = ((bf16[4,256,2048]{2,1,0:T(8,128)(2,1)}), bf16[4,256,2048]{2,1,0:T(8,128)(2,1)}, u32[]{:S(2)}, u32[]{:S(2)}) async-start(bf16[4,256,2048]{2,1,0:T(8,128)(2,1)} %bitcast.31), calls=%async_computation | async-start | bytes 8388608 | tf_op jit(solution)/shard_map/all_to_all | solution.py:52
Sparse Core Ops, SparseCore 0:
  9.6 51.7 all-gather.1

commit v2 on v1

--- a/solution.py
+++ b/solution.py
@@ -1,8 +1,10 @@
-import math
+import functools
 
 import jax
 import jax.numpy as jnp
 from jax import lax
+from jax.experimental import pallas as pl
+from jax.experimental.pallas import tpu as pltpu
 from jax.sharding import PartitionSpec as P
 
 PROJ = 4096
@@ -32,25 +34,201 @@
     return jnp.where(mixed < 0, -1.0, 1.0).astype(jnp.bfloat16)
 
 
+def split_pair(tokens, adapter_out):
+    through = lowrank_scale_factor * contract_last(tokens, adapter_out)
+    high = through.astype(jnp.bfloat16)
+    low = (through - high.astype(jnp.float32)).astype(jnp.bfloat16)
+    return jnp.concatenate([high, low], axis=1)
+
+
+def own_kernel(up_ref, weight_ref, double_ref, out_adapter_ref, out_ref, pair_ref):
+    @pl.when(pl.program_id(0) == 0)
+    def _():
+        pair_ref[...] = split_pair(up_ref[...], out_adapter_ref[...])
+
+    total = contract_last(up_ref[...], weight_ref[...])
+    total += contract_last(pair_ref[...], double_ref[...])
+    out_ref[...] = total.astype(out_ref.dtype)
+
+
+def own_columns(upstream, weight, double, adapter_out):
+    tokens, depth = upstream.shape
+    columns = weight.shape[0]
+    block = min(512, columns)
+    rank2 = double.shape[1]
+    return pl.pallas_call(
+        own_kernel,
+        grid=(columns // block,),
+        in_specs=[
+            pl.BlockSpec((tokens, depth), lambda i: (0, 0)),
+            pl.BlockSpec((block, depth), lambda i: (i, 0)),
+            pl.BlockSpec((block, rank2), lambda i: (i, 0)),
+            pl.BlockSpec(adapter_out.shape, lambda i: (0, 0)),
+        ],
+        out_specs=pl.BlockSpec((tokens, block), lambda i: (0, i)),
+        out_shape=jax.ShapeDtypeStruct((tokens, columns), jnp.bfloat16),
+        scratch_shapes=[pltpu.VMEM((tokens, rank2), jnp.bfloat16)],
+        cost_estimate=pl.CostEstimate(
+            flops=2 * tokens * depth * columns,
+            bytes_accessed=2 * (tokens * depth + columns * depth + tokens * columns),
+            transcendentals=0,
+        ),
+    )(upstream, weight, double, adapter_out)
+
+
+def pair_kernel(even_ref, odd_ref, out_adapter_ref, even_pair_ref, odd_pair_ref):
+    even_pair_ref[0] = split_pair(even_ref[0], out_adapter_ref[...])
+    odd_pair_ref[0] = split_pair(odd_ref[0], out_adapter_ref[...])
+
+
+def plane_pairs(even, odd, adapter_out):
+    chips, tokens, depth = even.shape
+    rank2 = 2 * adapter_out.shape[0]
+    block = pl.BlockSpec((1, tokens, depth), lambda i: (i, 0, 0))
+    pairs = pl.BlockSpec((1, tokens, rank2), lambda i: (i, 0, 0))
+    shape = jax.ShapeDtypeStruct((chips, tokens, rank2), jnp.bfloat16)
+    return pl.pallas_call(
+        pair_kernel,
+        grid=(chips,),
+        in_specs=[block, block, pl.BlockSpec(adapter_out.shape, lambda i: (0, 0))],
+        out_specs=[pairs, pairs],
+        out_shape=[shape, shape],
+        cost_estimate=pl.CostEstimate(
+            flops=4 * chips * tokens * depth * 128, bytes_accessed=4 * chips * tokens * depth, transcendentals=0
+        ),
+    )(even, odd, adapter_out)
+
+
+def piece_kernel(member_ref, even_ref, odd_ref, even_pair_ref, odd_pair_ref, weight_ref, double_ref, out_ref):
+    core = lax.rem(member_ref[0], 2)
+    for place, tokens, pair in ((core, even_ref, even_pair_ref), (1 - core, odd_ref, odd_pair_ref)):
+        total = contract_last(tokens[0], weight_ref[...])
+        total += contract_last(pair[0], double_ref[...])
+        out_ref[0, place] = total.astype(out_ref.dtype)
+
+
+def piece_columns(member, even, odd, even_pair, odd_pair, weight, double):
+    chips, tokens, depth = even.shape
+    width = weight.shape[0]
+    rank2 = double.shape[1]
+    block = pl.BlockSpec((1, tokens, depth), lambda i, m: (i, 0, 0))
+    pairs = pl.BlockSpec((1, tokens, rank2), lambda i, m: (i, 0, 0))
+    return pl.pallas_call(
+        piece_kernel,
+        grid_spec=pltpu.PrefetchScalarGridSpec(
+            num_scalar_prefetch=1,
+            grid=(chips,),
+            in_specs=[
+                block,
+                block,
+                pairs,
+                pairs,
+                pl.BlockSpec((width, depth), lambda i, m: (0, 0)),
+                pl.BlockSpec((width, rank2), lambda i, m: (0, 0)),
+            ],
+            out_specs=pl.BlockSpec(
+                (1, 2, tokens, width), lambda i, m: (lax.bitwise_xor(i, lax.div(m[0], 2)), 0, 0, 0)
+            ),
+        ),
+        out_shape=jax.ShapeDtypeStruct((chips, 2, tokens, width), jnp.bfloat16),
+        cost_estimate=pl.CostEstimate(
+            flops=4 * chips * tokens * depth * width,
+            bytes_accessed=4 * chips * tokens * (depth + width),
+            transcendentals=0,
+        ),
+    )(member, even, odd, even_pair, odd_pair, weight, double)
+
+
+def assemble_kernel(groups, shifts, place_ref, own_ref, *refs):
+    pieces, out_ref, sem = refs[: len(shifts)], refs[len(shifts)], refs[len(shifts) + 1]
+    members, tokens, width = pieces[0].shape
+    columns = own_ref.shape[1]
+    me = place_ref[0]
+    copies = [
+        pltpu.make_async_copy(
+            own_ref, out_ref.at[:, pl.ds(pl.multiple_of(me * columns, columns), columns)], sem.at[0]
+        )
+    ]
+    for index, (shift, piece) in enumerate(zip(shifts, pieces)):
+        shard = lax.rem(me + groups - shift, groups)
+        for member in range(members):
+            start = pl.multiple_of(shard * columns + member * width, width)
+            copies.append(
+                pltpu.make_async_copy(
+                    piece.at[member], out_ref.at[:, pl.ds(start, width)], sem.at[1 + index * members + member]
+                )
+            )
+    for copy in copies:
+        copy.start()
+    for copy in copies:
+        copy.wait()
+
+
+def assemble(place, own, pieces, shifts, groups):
+    tokens, columns = own.shape
+    members, _, width = pieces[0].shape
+    if width % 128:
+        blocks = [own] + [jnp.swapaxes(p, 0, 1).reshape(tokens, columns) for p in pieces]
+        order = [0] * groups
+        for index, shift in enumerate((0,) + tuple(shifts)):
+            order[shift] = index
+        stacked = jnp.stack([blocks[i] for i in order])
+        picked = jnp.take(stacked, (place[0] - jnp.arange(groups)) % groups, axis=0)
+        return jnp.swapaxes(picked, 0, 1).reshape(tokens, groups * columns)
+    anywhere = pl.BlockSpec(memory_space=pl.ANY)
+    return pl.pallas_call(
+        functools.partial(assemble_kernel, groups, shifts),
+        grid_spec=pltpu.PrefetchScalarGridSpec(
+            num_scalar_prefetch=1,
+            grid=(),
+            in_specs=[anywhere] * (1 + len(pieces)),
+            out_specs=anywhere,
+            scratch_shapes=[pltpu.SemaphoreType.DMA((1 + len(pieces) * members,))],
+        ),
+        out_shape=jax.ShapeDtypeStruct((tokens, groups * columns), jnp.bfloat16),
+    )(place, own, *pieces)
+
+
+def input_gradients(upstream, value_weight, adapter_in, adapter_out):
+    groups, members = lax.axis_size("fsdp"), lax.axis_size("grp")
+    place, member = lax.axis_index("fsdp"), lax.axis_index("grp")
+    columns = value_weight.shape[0]
+    width = columns // members
+    tokens, depth = upstream.shape
+    double = jnp.concatenate([adapter_in, adapter_in], axis=1)
+
+    slice_own = lax.dynamic_slice_in_dim(value_weight, member * width, width, 0)
+    shifts = sorted(range(1, groups), key=lambda s: (min(s, groups - s), s))
+    weights = [
+        lax.ppermute(slice_own, "fsdp", [(i, (i + s) % groups) for i in range(groups)]) for s in shifts
+    ]
+    even = jnp.stack(
+        [upstream]
+        + [lax.ppermute(upstream, "grp", [(i, i ^ m) for i in range(members)]) for m in range(2, members, 2)]
+    )
+    odd = lax.ppermute(even, "grp", [(i, i ^ 1) for i in range(members)])
+    even_pair, odd_pair = plane_pairs(even, odd, adapter_out)
+
+    own = own_columns(
+        upstream, value_weight, lax.dynamic_slice_in_dim(double, place * columns, columns, 0), adapter_out
+    )
+    pieces = []
+    for shift, weight in zip(shifts, weights):
+        shard = lax.rem(place + groups - shift, groups)
+        part = lax.dynamic_slice_in_dim(double, shard * columns + member * width, width, 0)
+        piece = piece_columns(member.reshape(1), even, odd, even_pair, odd_pair, weight, part)
+        piece = piece.reshape(members, tokens, width)
+        pieces.append(lax.all_to_all(piece, "grp", split_axis=0, concat_axis=0, tiled=True))
+    return assemble(place.reshape(1), own, pieces, shifts, groups)
+
+
 def per_device(inputs, upstream, value_weight, adapter_in, adapter_out, sign_seed):
     both = ("fsdp", "grp")
     groups = lax.axis_size("fsdp")
     members = lax.axis_size("grp")
+    input_grads = input_gradients(upstream, value_weight, adapter_in, adapter_out)
+
     passed_along = contract_last(upstream, adapter_out)
-    adapter_expanded = adapter_in.astype(jnp.float32)
-    col_count = value_weight.shape[0]
-    adapter_slice = lax.dynamic_slice_in_dim(
-        adapter_expanded, lax.axis_index("fsdp") * col_count, col_count, 0
-    )
-    piece = lax.all_gather(upstream, "fsdp", axis=0, tiled=True)
-    main_part = contract_last(piece, value_weight)
-    piece_through = contract_last(piece, adapter_out)
-    lowrank_portion = jnp.dot(
-        lowrank_scale_factor * piece_through, adapter_slice.T, precision=lax.Precision.HIGHEST
-    )
-    columns = (main_part + lowrank_portion).astype(jnp.bfloat16)
-    input_grads = lax.all_to_all(columns, "fsdp", split_axis=0, concat_axis=1, tiled=True)
-
     rescaled_values = (lowrank_scale_factor * passed_along).astype(jnp.bfloat16)
     rank_reduced = jnp.dot(inputs, adapter_in, preferred_element_type=jnp.float32).astype(
         jnp.bfloat16

time: 189 us -> 280 us (1.48)
  Pallas kernels: 0 us -> 154 us
  waiting for transfers between devices: 105 us -> 48 us
  starting transfers between devices: 19.5 us -> 34.7 us
  between operations: 15.6 us -> 2.24 us
  matrix products: 33 us -> 19.7 us
  local copies, waits for them, and re-layouts: 12 us -> 15 us
    pallas_call x0 -> x6, Pallas kernels: none -> 154 us  [the longest x1 128 us: assemble(): pl.pallas_call(functools.partial(assemble_kernel, groups, shifts), grid_s...]
    all_to_all x1 -> x3, waiting for transfers between devices: 91.3 us -> 6.6 us  [input_gradients(): lax.all_to_all(piece, 'grp', split_axis=0, concat_axis=0, tiled=True)]
    ppermute x0 -> x7, waiting for transfers between devices: none -> 26.9 us  [the longest x3 26.9 us: input_gradients(): lax.ppermute(slice_own, 'fsdp', [(i, (i + s) % groups) for i in range(gro...]
    dot_general x3 -> x0, matrix products: 13.3 us -> none  [the longest x2 7.8 us: contract_last(): lax.dot_general(left, right, (((1,), (1,)), ((), ())), preferred_element_...]
    ppermute x0 -> x7, starting transfers between devices: none -> 10.3 us  [the longest x3 5.49 us: input_gradients(): lax.ppermute(slice_own, 'fsdp', [(i, (i + s) % groups) for i in range(gro...]
    all_to_all x1 -> x3, starting transfers between devices: 4.84 us -> 11.3 us  [input_gradients(): lax.all_to_all(piece, 'grp', split_axis=0, concat_axis=0, tiled=True)]
    unnamed x12 -> x25, local copies, waits for them, and re-layouts: 1.48 us -> 7.33 us
    all_to_all x1 -> x0, local copies, waits for them, and re-layouts: 4.79 us -> none  [per_device(): lax.all_to_all(columns, 'fsdp', split_axis=0, concat_axis=1, tiled=True)]
  transfers between devices with their start and end apart: 5 -> 13, of which waited for: 3 -> 5; matrix products, arithmetic and copies ran while one was open for 23% -> 13% of each run, Pallas kernels for 0% -> 9%
where the time goes in v2:
time: 280 us; the launch traced here: 279 us
  Pallas kernels  154 us (55%)
  waiting for transfers between devices  48 us (17%)
  starting transfers between devices  34.7 us (12%)
  matrix products  19.7 us (7%)
  local copies, waits for them, and re-layouts  15 us (5%)
  other arithmetic  4.75 us (2%)
    pallas_call x1, Pallas kernels, assemble(): pl.pallas_call(functools.partial(assemble_kernel, groups, shifts), grid_s...  128 us
    ppermute x3, waiting for transfers between devices, input_gradients(): lax.ppermute(slice_own, 'fsdp', [(i, (i + s) % groups) for i in range(gro...  26.9 us
    pallas_call x3, Pallas kernels, piece_columns(): pl.pallas_call(piece_kernel, grid_spec=pltpu.PrefetchScalarGridSpec(num_s...  15.8 us
    dot_general x1, matrix products, per_device(): partial_feats = jnp.dot(received, signs, preferred_element_type=jnp.float32)  12.6 us
    all_to_all x3, starting transfers between devices, input_gradients(): lax.all_to_all(piece, 'grp', split_axis=0, concat_axis=0, tiled=True)  11.3 us
    all_to_all x1, waiting for transfers between devices, per_device(): lax.all_to_all(flat.reshape(devices, slice_len), both, split_axis=0, conc...  9.72 us
    unnamed x25, local copies, waits for them, and re-layouts  7.33 us
    dot_general x2, matrix products, leading_contraction(): lax.dot_general(left, right, (((0,), (0,)), ((), ())), preferred_element_...  7.15 us
  transfers between devices with their start and end apart: 13, of which 5 were waited for; matrix products, arithmetic and copies ran while one was open for 13% of the time, Pallas kernels for 9%

profile of v2, /device:TPU:0, one launch (start us, length us, event | category | flops | bytes accessed | tf_op | source)
XLA Modules:
  0.0 278.8 jit_solution(2151036878665209604)
XLA Ops:
  0.6 3.0 %collective-permute-start = (bf16[256,1024]{1,0:T(8,128)(2,1)}, bf16[256,1024]{1,0:T(8,128)(2,1)}, u32[]{:S(2)}, u32[]{:S(2)}) collective-permute-start(bf16[256,1024]{1,0:T(8,128)(2,1)} %up_ref.1), channel_id=1, source_target_pairs={{0,8},{4,12},{8,0},{12,4},{16,24},{20,28},{24,16},{28,20},{1,9},{5... | collective-permute-start | bytes 1572872 | tf_op jit(solution)/shard_map/ppermute | solution.py:207
  5.2 1.9 constant_dynamic-slice_fusion.3
  7.1 3.0 %collective-permute-start.6 = (bf16[256,1024]{1,0:T(8,128)(2,1)}, bf16[256,1024]{1,0:T(8,128)(2,1)}, u32[]{:S(2)}, u32[]{:S(2)}) collective-permute-start(bf16[256,1024]{1,0:T(8,128)(2,1)} %constant_dynamic-slice_fusion.3), channel_id=1, source_target_pairs={{0,2},{1,3},{2,0},{3,1},{4,6},{5,7},{6,4},{7,5},{8,10},{9,11},{10,... | collective-permute-start | bytes 1572872 | tf_op jit(solution)/shard_map/ppermute | solution.py:203
  10.1 3.5 %fusion.3 = bf16[8192,8]{0,1:T(8,128)(2,1)S(1)} fusion(bf16[256,8192]{1,0:T(8,128)(2,1)} %param.6, bf16[256,1024]{1,0:T(8,128)(2,1)} %up_ref.1, bf16[8,1024]{1,0:T(8,128)(2,1)} %out_adapter_ref.3), kind=kOutput, calls=%fused_computation.7 | convolution fusion | flops 37818368 | bytes 4866048 | tf_op jit(solution)/shard_map/dot_general | solution.py:22
  14.6 2.1 reshape.97
  16.8 3.7 %fusion.6 = bf16[1,8,8,128]{3,2,1,0:T(8,128)(2,1)S(1)} fusion(bf16[256,1024]{1,0:T(8,128)(2,1)S(1)} %copy-done.1, bf16[256,8192]{1,0:T(8,128)(2,1)} %param.6, bf16[8192,8]{0,1:T(8,128)(2,1)S(1)} %copy-done.5), kind=kOutput, calls=%fused_computation.12 | convolution fusion | flops 37767168 | bytes 4866048 | tf_op jit(solution)/shard_map/dot_general | solution.py:22
  23.2 3.8 %all-to-all-start.3 = ((bf16[32,2,1152]{2,1,0:T(2,128)(2,1)}), bf16[32,2,1152]{2,1,0:T(2,128)(2,1)S(1)}, u32[]{:S(2)}, u32[]{:S(2)}) async-start(bf16[32,2,1152]{2,1,0:T(2,128)(2,1)} %reshape.100), calls=%async_computation.3 | async-start | bytes 294912 | tf_op jit(solution)/shard_map/all_to_all | solution.py:241
  27.8 9.7 %all-to-all-done.3 = bf16[32,2,1152]{2,1,0:T(2,128)(2,1)S(1)} async-done(((bf16[32,2,1152]{2,1,0:T(2,128)(2,1)}), bf16[32,2,1152]{2,1,0:T(2,128)(2,1)S(1)}, u32[]{:S(2)}, u32[]{:S(2)}) %all-to-all-start.3) | async-done | bytes 147488 | tf_op jit(solution)/shard_map/all_to_all | solution.py:241
  38.3 3.5 %all-to-all-start.5 = ((f32[8,1,2304]{2,1,0:T(1,128)}), f32[8,1,2304]{2,1,0:T(1,128)S(1)}, u32[]{:S(2)}, u32[]{:S(2)}) async-start(f32[8,1,2304]{2,1,0:T(1,128)} %broadcast_in_dim.15), calls=%async_computation.5 | async-start | bytes 147456 | tf_op jit(solution)/shard_map/all_to_all | solution.py:245
  43.8 12.6 %fusion.4 = f32[32,1,4096]{2,0,1:T(8,128)S(1)} fusion(s32[]{:T(128)} %bitcast.10, s32[4096]{0:T(1024)S(1)} %iota_multiply_fusion, s32[2304]{0:T(1024)S(1)} %add_multiply_fusion, bf16[32,1,2304]{2,1,0:T(2,128)(2,1)S(1)} %reshape.101), kind=kOutput, calls=%fused_computation.8 | convolution fusion | flops 698351616 | bytes 697348 | tf_op jit(solution)/shard_map/dot_general | solution.py:251
  57.8 5.7 %all-to-all-start.4 = ((f32[32,1,4096]{2,1,0:T(1,128)}), f32[32,1,4096]{2,1,0:T(1,128)S(1)}, u32[]{:S(2)}, u32[]{:S(2)}) async-start(f32[32,1,4096]{2,1,0:T(1,128)} %copy.20), calls=%async_computation.4 | async-start | bytes 1048576 | tf_op jit(solution)/shard_map/all_to_all | solution.py:252
  64.3 4.7 %shard_map.86 = (bf16[4,256,16]{2,1,0:T(8,128)(2,1)}, bf16[4,256,16]{2,1,0:T(8,128)(2,1)}) custom-call(bf16[4,256,1024]{2,1,0:T(8,128)(2,1)} %copy-done, bf16[4,256,1024]{2,1,0:T(8,128)(2,1)} %collective-permute-done.3.odd_ref, bf16[8,1024]{1,0:T(8,128)(2,1)} %out_adapter_ref.3), custom_call_target="tpu_custom_call" | custom-call | flops 536870912 | bytes 4194304 | tf_op jit(solution)/shard_map/pallas_call | solution.py:90
  69.0 5.3 %shard_map.89 = bf16[4,2,256,256]{3,2,1,0:T(8,128)(2,1)} custom-call(s32[1]{0:T(128)} %bitcast.1.member_ref, bf16[4,256,1024]{2,1,0:T(8,128)(2,1)} %copy-done, bf16[4,256,1024]{2,1,0:T(8,128)(2,1)} %collective-permute-done.3.odd_ref, bf16[4,256,16]{2,1,0:T(8,128)(2,1)} %get-tuple-element.5.even_pair_ref, bf16[4,256,16]{2,1,0:T(8,128)(2,1)} %get-tuple-element.6.odd_pair_ref, ...), custom_call_target="tpu_custom_call" | custom-call | flops 1073741824 | bytes 5242880 | tf_op jit(solution)/shard_map/pallas_call | solution.py:116
  74.3 4.7 %all-to-all-done.4 = f32[32,1,4096]{2,1,0:T(1,128)S(1)} async-done(((f32[32,1,4096]{2,1,0:T(1,128)}), f32[32,1,4096]{2,1,0:T(1,128)S(1)}, u32[]{:S(2)}, u32[]{:S(2)}) %all-to-all-start.4) | async-done | bytes 524320 | tf_op jit(solution)/shard_map/all_to_all | solution.py:252
  79.1 3.6 %all-to-all-start.2 = ((bf16[8,256,256]{2,1,0:T(8,128)(2,1)}), bf16[8,256,256]{2,1,0:T(8,128)(2,1)S(1)}, u32[]{:S(2)}, u32[]{:S(2)}) async-start(bf16[8,256,256]{2,1,0:T(8,128)(2,1)} %bitcast.34), calls=%async_computation.2 | async-start | bytes 2097152 | tf_op jit(solution)/shard_map/all_to_all | solution.py:221
  84.5 12.5 %collective-permute-done.5.weight_ref = bf16[256,1024]{1,0:T(8,128)(2,1)S(1)} collective-permute-done((bf16[256,1024]{1,0:T(8,128)(2,1)}, bf16[256,1024]{1,0:T(8,128)(2,1)S(1)}, u32[]{:S(2)}, u32[]{:S(2)}) %collective-permute-start.5) | collective-permute-done | bytes 524320 | tf_op jit(solution)/shard_map/ppermute | solution.py:203
  97.9 5.3 %shard_map.88 = bf16[4,2,256,256]{3,2,1,0:T(8,128)(2,1)} custom-call(s32[1]{0:T(128)} %bitcast.1.member_ref, bf16[4,256,1024]{2,1,0:T(8,128)(2,1)} %copy-done, bf16[4,256,1024]{2,1,0:T(8,128)(2,1)} %collective-permute-done.3.odd_ref, bf16[4,256,16]{2,1,0:T(8,128)(2,1)} %get-tuple-element.5.even_pair_ref, bf16[4,256,16]{2,1,0:T(8,128)(2,1)} %get-tuple-element.6.odd_pair_ref, ...), custom_call_target="tpu_custom_call" | custom-call | flops 1073741824 | bytes 5242880 | tf_op jit(solution)/shard_map/pallas_call | solution.py:116
  103.2 3.9 %all-to-all-start.1 = ((bf16[8,256,256]{2,1,0:T(8,128)(2,1)}), bf16[8,256,256]{2,1,0:T(8,128)(2,1)S(1)}, u32[]{:S(2)}, u32[]{:S(2)}) async-start(bf16[8,256,256]{2,1,0:T(8,128)(2,1)} %bitcast.33), calls=%async_computation.1 | async-start | bytes 2097152 | tf_op jit(solution)/shard_map/all_to_all | solution.py:221
  109.0 14.3 %collective-permute-done.4.weight_ref = bf16[256,1024]{1,0:T(8,128)(2,1)S(1)} collective-permute-done((bf16[256,1024]{1,0:T(8,128)(2,1)}, bf16[256,1024]{1,0:T(8,128)(2,1)S(1)}, u32[]{:S(2)}, u32[]{:S(2)}) %collective-permute-start.4) | collective-permute-done | bytes 524320 | tf_op jit(solution)/shard_map/ppermute | solution.py:203
  124.2 5.3 %shard_map.87 = bf16[4,2,256,256]{3,2,1,0:T(8,128)(2,1)} custom-call(s32[1]{0:T(128)} %bitcast.1.member_ref, bf16[4,256,1024]{2,1,0:T(8,128)(2,1)} %copy-done, bf16[4,256,1024]{2,1,0:T(8,128)(2,1)} %collective-permute-done.3.odd_ref, bf16[4,256,16]{2,1,0:T(8,128)(2,1)} %get-tuple-element.5.even_pair_ref, bf16[4,256,16]{2,1,0:T(8,128)(2,1)} %get-tuple-element.6.odd_pair_ref, ...), custom_call_target="tpu_custom_call" | custom-call | flops 1073741824 | bytes 5242880 | tf_op jit(solution)/shard_map/pallas_call | solution.py:116
  129.5 3.9 %all-to-all-start = ((bf16[8,256,256]{2,1,0:T(8,128)(2,1)}), bf16[8,256,256]{2,1,0:T(8,128)(2,1)S(1)}, u32[]{:S(2)}, u32[]{:S(2)}) async-start(bf16[8,256,256]{2,1,0:T(8,128)(2,1)} %bitcast.32), calls=%async_computation | async-start | bytes 2097152 | tf_op jit(solution)/shard_map/all_to_all | solution.py:221
  134.4 5.5 %shard_map.85.own_ref = bf16[256,2048]{1,0:T(8,128)(2,1)} custom-call(bf16[256,1024]{1,0:T(8,128)(2,1)} %up_ref.1, bf16[2048,1024]{1,0:T(8,128)(2,1)} %weight_ref.1, bf16[2048,16]{1,0:T(8,128)(2,1)} %copy.22.double_ref, bf16[8,1024]{1,0:T(8,128)(2,1)} %out_adapter_ref.3), custom_call_target="tpu_custom_call" | custom-call | flops 1073741824 | bytes 5767168 | tf_op jit(solution)/shard_map/pallas_call | solution.py:59
  142.2 6.6 %all-to-all-done.refs_0_ = bf16[8,256,256]{2,1,0:T(8,128)(2,1)S(1)} async-done(((bf16[8,256,256]{2,1,0:T(8,128)(2,1)}), bf16[8,256,256]{2,1,0:T(8,128)(2,1)S(1)}, u32[]{:S(2)}, u32[]{:S(2)}) %all-to-all-start) | async-done | bytes 1048608 | tf_op jit(solution)/shard_map/all_to_all | solution.py:221
  149.8 128.4 %shard_map.90 = bf16[256,8192]{1,0:T(8,128)(2,1)} custom-call(s32[1]{0:T(128)} %bitcast.place_ref, bf16[256,2048]{1,0:T(8,128)(2,1)} %shard_map.85.own_ref, bf16[8,256,256]{2,1,0:T(8,128)(2,1)} %copy-done.4, bf16[8,256,256]{2,1,0:T(8,128)(2,1)} %copy-done.3, bf16[8,256,256]{2,1,0:T(8,128)(2,1)} %copy-done.2), custom_call_target="tpu_custom_call" | custom-call | tf_op jit(solution)/shard_map/pallas_call | solution.py:179
  (56 shorter events, 20.0 us)
Async XLA Ops:
  0.6 41.3 %collective-permute-start = (bf16[256,1024]{1,0:T(8,128)(2,1)}, bf16[256,1024]{1,0:T(8,128)(2,1)}, u32[]{:S(2)}, u32[]{:S(2)}) collective-permute-start(bf16[256,1024]{1,0:T(8,128)(2,1)} %up_ref.1), channel_id=1, source_target_pairs={{0,8},{4,12},{8,0},{12,4},{16,24},{20,28},{24,16},{28,20},{1,9},{5... | collective-permute-start | bytes 1572872 | tf_op jit(solution)/shard_map/ppermute | solution.py:207
  3.6 38.3 %collective-permute-start.1 = (bf16[256,1024]{1,0:T(8,128)(2,1)}, bf16[256,1024]{1,0:T(8,128)(2,1)}, u32[]{:S(2)}, u32[]{:S(2)}) collective-permute-start(bf16[256,1024]{1,0:T(8,128)(2,1)} %up_ref.1), channel_id=1, source_target_pairs={{0,16},{4,20},{8,24},{12,28},{16,0},{20,4},{24,8},{28,12},{1,17},{... | collective-permute-start | bytes 1572872 | tf_op jit(solution)/shard_map/ppermute | solution.py:207
  5.2 36.8 %collective-permute-start.2 = (bf16[256,1024]{1,0:T(8,128)(2,1)}, bf16[256,1024]{1,0:T(8,128)(2,1)}, u32[]{:S(2)}, u32[]{:S(2)}) collective-permute-start(bf16[256,1024]{1,0:T(8,128)(2,1)} %up_ref.1), channel_id=1, source_target_pairs={{0,24},{4,28},{8,16},{12,20},{16,8},{20,12},{24,0},{28,4},{1,25},{... | collective-permute-start | bytes 1572872 | tf_op jit(solution)/shard_map/ppermute | solution.py:207
  7.0 9.7 %copy-start.1 = (bf16[256,1024]{1,0:T(8,128)(2,1)S(1)}, bf16[256,1024]{1,0:T(8,128)(2,1)}, u32[]{:S(2)}) copy-start(bf16[256,1024]{1,0:T(8,128)(2,1)} %up_ref.1) | copy-start | bytes 1572868
  7.1 9.7 %copy-start.5 = (bf16[8192,8]{0,1:T(8,128)(2,1)S(1)}, bf16[8192,8]{0,1:T(8,128)(2,1)}, u32[]{:S(2)}) copy-start(bf16[8192,8]{0,1:T(8,128)(2,1)} %param.9) | copy-start | bytes 393220
  7.1 62.0 %collective-permute-start.6 = (bf16[256,1024]{1,0:T(8,128)(2,1)}, bf16[256,1024]{1,0:T(8,128)(2,1)}, u32[]{:S(2)}, u32[]{:S(2)}) collective-permute-start(bf16[256,1024]{1,0:T(8,128)(2,1)} %constant_dynamic-slice_fusion.3), channel_id=1, source_target_pairs={{0,2},{1,3},{2,0},{3,1},{4,6},{5,7},{6,4},{7,5},{8,10},{9,11},{10,... | collective-permute-start | bytes 1572872 | tf_op jit(solution)/shard_map/ppermute | solution.py:203
  23.2 14.3 %all-to-all-start.3 = ((bf16[32,2,1152]{2,1,0:T(2,128)(2,1)}), bf16[32,2,1152]{2,1,0:T(2,128)(2,1)S(1)}, u32[]{:S(2)}, u32[]{:S(2)}) async-start(bf16[32,2,1152]{2,1,0:T(2,128)(2,1)} %reshape.100), calls=%async_computation.3 | async-start | bytes 294912 | tf_op jit(solution)/shard_map/all_to_all | solution.py:241
  38.3 19.4 %all-to-all-start.5 = ((f32[8,1,2304]{2,1,0:T(1,128)}), f32[8,1,2304]{2,1,0:T(1,128)S(1)}, u32[]{:S(2)}, u32[]{:S(2)}) async-start(f32[8,1,2304]{2,1,0:T(1,128)} %broadcast_in_dim.15), calls=%async_computation.5 | async-start | bytes 147456 | tf_op jit(solution)/shard_map/all_to_all | solution.py:245
  43.5 12.9 %copy-start = (bf16[4,256,1024]{2,1,0:T(8,128)(2,1)}, bf16[4,256,1024]{2,1,0:T(8,128)(2,1)S(1)}, u32[]{:S(2)}) copy-start(bf16[4,256,1024]{2,1,0:T(8,128)(2,1)S(1)} %pad_maximum_fusion.even_ref) | copy-start | bytes 6291460
  43.6 20.8 %collective-permute-start.3 = (bf16[4,256,1024]{2,1,0:T(8,128)(2,1)S(1)}, bf16[4,256,1024]{2,1,0:T(8,128)(2,1)}, u32[]{:S(2)}, u32[]{:S(2)}) collective-permute-start(bf16[4,256,1024]{2,1,0:T(8,128)(2,1)S(1)} %pad_maximum_fusion.even_ref), channel_id=1, source_target_pairs={{0,4},{4,0},{8,12},{12,8},{16,20},{20,16},{24,28},{28,24},{1,5},{5... | collective-permute-start | bytes 6291464 | tf_op jit(solution)/shard_map/ppermute | solution.py:209
  57.8 21.3 %all-to-all-start.4 = ((f32[32,1,4096]{2,1,0:T(1,128)}), f32[32,1,4096]{2,1,0:T(1,128)S(1)}, u32[]{:S(2)}, u32[]{:S(2)}) async-start(f32[32,1,4096]{2,1,0:T(1,128)} %copy.20), calls=%async_computation.4 | async-start | bytes 1048576 | tf_op jit(solution)/shard_map/all_to_all | solution.py:252
  79.1 24.1 %all-to-all-start.2 = ((bf16[8,256,256]{2,1,0:T(8,128)(2,1)}), bf16[8,256,256]{2,1,0:T(8,128)(2,1)S(1)}, u32[]{:S(2)}, u32[]{:S(2)}) async-start(bf16[8,256,256]{2,1,0:T(8,128)(2,1)} %bitcast.34), calls=%async_computation.2 | async-start | bytes 2097152 | tf_op jit(solution)/shard_map/all_to_all | solution.py:221
  82.6 14.4 %collective-permute-start.5 = (bf16[256,1024]{1,0:T(8,128)(2,1)}, bf16[256,1024]{1,0:T(8,128)(2,1)S(1)}, u32[]{:S(2)}, u32[]{:S(2)}) collective-permute-start(bf16[256,1024]{1,0:T(8,128)(2,1)} %constant_dynamic-slice_fusion.3), channel_id=1, source_target_pairs={{0,3},{1,0},{2,1},{3,2},{4,7},{5,4},{6,5},{7,6},{8,11},{9,8},{10,9... | collective-permute-start | bytes 1572872 | tf_op jit(solution)/shard_map/ppermute | solution.py:203
  97.1 0.8 copy-start.7
  103.2 26.3 %copy-start.2 = (bf16[8,256,256]{2,1,0:T(8,128)(2,1)}, bf16[8,256,256]{2,1,0:T(8,128)(2,1)S(1)}, u32[]{:S(2)}) copy-start(bf16[8,256,256]{2,1,0:T(8,128)(2,1)S(1)} %all-to-all-done.2.refs_2_) | copy-start | bytes 3145732
  103.2 26.3 %all-to-all-start.1 = ((bf16[8,256,256]{2,1,0:T(8,128)(2,1)}), bf16[8,256,256]{2,1,0:T(8,128)(2,1)S(1)}, u32[]{:S(2)}, u32[]{:S(2)}) async-start(bf16[8,256,256]{2,1,0:T(8,128)(2,1)} %bitcast.33), calls=%async_computation.1 | async-start | bytes 2097152 | tf_op jit(solution)/shard_map/all_to_all | solution.py:221
  107.0 16.3 %collective-permute-start.4 = (bf16[256,1024]{1,0:T(8,128)(2,1)}, bf16[256,1024]{1,0:T(8,128)(2,1)S(1)}, u32[]{:S(2)}, u32[]{:S(2)}) collective-permute-start(bf16[256,1024]{1,0:T(8,128)(2,1)} %constant_dynamic-slice_fusion.3), channel_id=1, source_target_pairs={{0,1},{1,2},{2,3},{3,0},{4,5},{5,6},{6,7},{7,4},{8,9},{9,10},{10,1... | collective-permute-start | bytes 1572872 | tf_op jit(solution)/shard_map/ppermute | solution.py:203
  123.4 0.8 copy-start.6
  129.5 10.4 %copy-start.3 = (bf16[8,256,256]{2,1,0:T(8,128)(2,1)}, bf16[8,256,256]{2,1,0:T(8,128)(2,1)S(1)}, u32[]{:S(2)}) copy-start(bf16[8,256,256]{2,1,0:T(8,128)(2,1)S(1)} %all-to-all-done.1.refs_1_) | copy-start | bytes 3145732
  129.5 19.3 %all-to-all-start = ((bf16[8,256,256]{2,1,0:T(8,128)(2,1)}), bf16[8,256,256]{2,1,0:T(8,128)(2,1)S(1)}, u32[]{:S(2)}, u32[]{:S(2)}) async-start(bf16[8,256,256]{2,1,0:T(8,128)(2,1)} %bitcast.32), calls=%async_computation | async-start | bytes 2097152 | tf_op jit(solution)/shard_map/all_to_all | solution.py:221
  148.8 1.0 copy-start.4

commit v3 on v1

v3 whole, which is shorter than its diff:
```python
import functools

import jax
import jax.numpy as jnp
from jax import lax
from jax.experimental import pallas as pl
from jax.experimental.pallas import tpu as pltpu
from jax.sharding import PartitionSpec as P

PROJ = 4096

lowrank_scale_factor = 2.0

CHEAP = pl.CostEstimate(flops=0, bytes_accessed=0, transcendentals=0)
MEMBER, PLACE, CHIP, START, SHARDS = range(5)
DEAR = pl.CostEstimate(flops=10**11, bytes_accessed=0, transcendentals=0)


def contract_last(left, right):
    return lax.dot_general(
        left, right, (((1,), (1,)), ((), ())), preferred_element_type=jnp.float32
    )


def dot(left, right):
    return jnp.dot(left, right, preferred_element_type=jnp.float32)


def hash_signs(mixed):
    mixed = mixed ^ lax.shift_right_logical(mixed, 15)
    mixed = mixed * 181057748
    mixed = mixed ^ lax.shift_left(mixed, 13)
    return jnp.where(mixed < 0, -1.0, 1.0).astype(jnp.bfloat16)


def split_pair(tokens, adapter_out):
    through = lowrank_scale_factor * contract_last(tokens, adapter_out)
    high = through.astype(jnp.bfloat16)
    low = (through - high.astype(jnp.float32)).astype(jnp.bfloat16)
    return jnp.concatenate([high, low], axis=1)


def twice(part):
    return jnp.concatenate([part, part], axis=0)


def own_kernel(info_ref, up_ref, weight_ref, in_adapter_ref, out_adapter_ref, after_ref, out_ref, pair_ref, turned_ref):
    @pl.when(pl.program_id(0) == 0)
    def _():
        pair_ref[...] = split_pair(up_ref[...], out_adapter_ref[...])
        turned_ref[...] = up_ref[...].T

    total = dot(weight_ref[...], turned_ref[...]).T
    total += dot(pair_ref[...], twice(in_adapter_ref[...]))
    out_ref[...] = total.astype(out_ref.dtype)


def own_columns(info, upstream, weight, adapter_in_t, adapter_out, all_columns, after):
    tokens, depth = upstream.shape
    columns = weight.shape[0]
    block = min(1024, columns)
    steps = columns // block
    rank = adapter_in_t.shape[0]
    return pl.pallas_call(
        own_kernel,
        grid_spec=pltpu.PrefetchScalarGridSpec(
            num_scalar_prefetch=1,
            grid=(steps,),
            in_specs=[
                pl.BlockSpec((tokens, depth), lambda i, s: (0, 0)),
                pl.BlockSpec((block, depth), lambda i, s: (i, 0)),
                pl.BlockSpec((rank, block), lambda i, s: (0, s[PLACE] * steps + i)),
                pl.BlockSpec(adapter_out.shape, lambda i, s: (0, 0)),
                pl.BlockSpec(memory_space=pl.ANY),
            ],
            out_specs=pl.BlockSpec((tokens, block), lambda i, s: (0, s[PLACE] * steps + i)),
            scratch_shapes=[
                pltpu.VMEM((tokens, 2 * rank), jnp.bfloat16),
                pltpu.VMEM((depth, tokens), jnp.bfloat16),
            ],
        ),
        out_shape=jax.ShapeDtypeStruct((tokens, all_columns), jnp.bfloat16),
        cost_estimate=CHEAP,
    )(info, upstream, weight, adapter_in_t, adapter_out, after)


def piece_kernel(chips, count, make_pairs, info_ref, *refs):
    token_refs, refs = refs[:chips], refs[chips:]
    weight_refs, refs = refs[: 2 * count], refs[2 * count :]
    adapter_refs, refs = refs[:count], refs[count:]
    pair_ref, refs = refs[0], refs[3:]
    out_refs = refs[:chips]
    rows = token_refs[0].shape[0]
    width = weight_refs[0].shape[0]
    core = lax.rem(info_ref[MEMBER], 2)
    stacked = jnp.concatenate([ref[...] for ref in token_refs], axis=0)
    if make_pairs:
        pairs = split_pair(stacked, pair_ref[...])
        refs[chips][...] = pairs.reshape(refs[chips].shape)
    else:
        pairs = pair_ref[...].reshape(chips * rows, pair_ref.shape[2])
    for index in range(count):
        for half in range(2):
            at = pl.multiple_of(lax.bitwise_xor(core, half) * width, width)
            total = contract_last(stacked, weight_refs[2 * index + half][...])
            total += dot(pairs, twice(adapter_refs[index][:, pl.ds(at, width)]))
            total = total.astype(out_refs[0].dtype)
            at = pl.multiple_of(at + index * 2 * width, width)
            for chip in range(chips):
                out_refs[chip][:, pl.ds(at, width)] = total[chip * rows : (chip + 1) * rows]


def piece_columns(info, shifts, plane, weights, adapter_in_t, pairs, adapter_out, after):
    chips = len(plane)
    tokens, depth = plane[0].shape
    width = weights[0][0].shape[0]
    count = len(weights)
    rank = adapter_in_t.shape[0]
    make_pairs = pairs is None
    if width % 128:
        if make_pairs:
            pairs = jnp.stack([split_pair(part, adapter_out) for part in plane])
        core = lax.rem(info[MEMBER], 2)
        columns = []
        for (mine, other), shift in zip(weights, shifts):
            at = info[SHARDS + shift] * chips + info[CHIP]
            both = jnp.where(core == 0, jnp.concatenate([mine, other]), jnp.concatenate([other, mine]))
            low = twice(lax.dynamic_slice_in_dim(adapter_in_t, at * 2 * width, 2 * width, 1))
            columns.append([contract_last(t, both) + dot(p, low) for t, p in zip(plane, pairs)])
        return [jnp.concatenate(c, axis=1).astype(jnp.bfloat16) for c in zip(*columns)], pairs
    rows = tokens // 2
    pair_block = pl.BlockSpec((chips, rows, 2 * rank), lambda i, s: (0, i, 0))
    out_block = pl.BlockSpec((rows, count * 2 * width), lambda i, s: (i, 0))
    out_shape = jax.ShapeDtypeStruct((tokens, count * 2 * width), jnp.bfloat16)
    outs = pl.pallas_call(
        functools.partial(piece_kernel, chips, count, make_pairs),
        grid_spec=pltpu.PrefetchScalarGridSpec(
            num_scalar_prefetch=1,
            grid=(tokens // rows,),
            in_specs=[pl.BlockSpec((rows, depth), lambda i, s: (i, 0))] * chips
            + [pl.BlockSpec((width, depth), lambda i, s: (0, 0))] * (2 * count)
            + [
                pl.BlockSpec((rank, 2 * width), lambda i, s, at=SHARDS + shift: (0, s[at] * chips + s[CHIP]))
                for shift in shifts
            ]
            + [pl.BlockSpec(adapter_out.shape, lambda i, s: (0, 0)) if make_pairs else pair_block]
            + [pl.BlockSpec(memory_space=pl.ANY)] * 2,
            out_specs=[out_block] * chips + ([pair_block] if make_pairs else []),
        ),
        out_shape=[out_shape] * chips
        + ([jax.ShapeDtypeStruct((chips, tokens, 2 * rank), jnp.bfloat16)] if make_pairs else []),
        cost_estimate=CHEAP,
    )(
        info,
        *plane,
        *[w for pair in weights for w in pair],
        *[adapter_in_t] * count,
        adapter_out if make_pairs else pairs,
        *after,
    )
    return (outs[:chips], outs[chips]) if make_pairs else (outs, pairs)


def place_kernel(chips, info_ref, *refs):
    piece_refs, out_ref = refs[:chips], refs[chips + 2]
    width = piece_refs[0].shape[1]
    for k in range(chips):
        at = pl.multiple_of(lax.bitwise_xor(info_ref[CHIP], k) * width, width)
        out_ref[:, pl.ds(at, width)] = piece_refs[k][...]


def place_columns(info, shifts, pieces, buffer, after, last):
    chips = len(pieces)
    tokens, width = pieces[0].shape
    width = width // len(shifts)
    if width % 128:
        for index, shift in enumerate(shifts):
            for k, piece in enumerate(pieces):
                part = piece[:, index * width : (index + 1) * width]
                at = (info[SHARDS + shift] * chips + lax.bitwise_xor(info[CHIP], k)) * width
                buffer = lax.dynamic_update_slice_in_dim(buffer, part, at, 1)
        return buffer

    def shard_of(w, s):
        at = s[SHARDS + shifts[0]]
        for index in range(1, len(shifts)):
            at = jnp.where(w == index, s[SHARDS + shifts[index]], at)
        return 0, at

    anywhere = pl.BlockSpec(memory_space=pl.ANY)
    return pl.pallas_call(
        functools.partial(place_kernel, chips),
        grid_spec=pltpu.PrefetchScalarGridSpec(
            num_scalar_prefetch=1,
            grid=(len(shifts),),
            in_specs=[pl.BlockSpec((tokens, width), lambda w, s: (0, w))] * chips + [anywhere, anywhere],
            out_specs=pl.BlockSpec((tokens, chips * width), shard_of),
        ),
        out_shape=jax.ShapeDtypeStruct(buffer.shape, buffer.dtype),
        input_output_aliases={1 + chips: 0},
        cost_estimate=DEAR if last else CHEAP,
    )(info, *pieces, buffer, after)


def flat_kernel(rank, groups, chunk_rows, in_ref, up_ref, in_adapter_ref, out_adapter_ref, out_ref, scaled_ref, narrow_ref, turn_ref, flat_ref, line_ref):
    step = pl.program_id(0)
    tokens, block = in_ref.shape
    model = flat_ref.shape[1] - up_ref.shape[1]

    @pl.when(step == 0)
    def _():
        through = lowrank_scale_factor * contract_last(out_adapter_ref[...], up_ref[...])
        scaled_ref[...] = through.astype(jnp.bfloat16)
        narrow_ref[...] = jnp.zeros_like(narrow_ref)

    at = pl.multiple_of(step * block, block)
    flat_ref[:, pl.ds(at, block)] = dot(scaled_ref[...], in_ref[...])
    narrow_ref[...] += contract_last(in_ref[...], in_adapter_ref[...])

    @pl.when(step == pl.num_programs(0) - 1)
    def _():
        narrow = narrow_ref[...].T.astype(jnp.bfloat16)
        turn_ref[...] = (lowrank_scale_factor * dot(narrow, up_ref[...])).T
        span = up_ref.shape[1] // rank
        lines = [turn_ref[pl.ds(row, span, rank), :].T for row in range(rank)]
        for r in range(rank):
            part = jnp.concatenate([line[r : r + 1] for line in lines], axis=0)
            flat_ref[:, model + r * span : model + (r + 1) * span] = part
        if chunk_rows:
            tiles = flat_ref.shape[1] // 128 // groups
            for place in range(groups):
                for tile in range(tiles):
                    at = (place * tiles + tile) * 128
                    line_ref[pl.ds(place * chunk_rows + tile, rank, groups * chunk_rows), :] = flat_ref[
                        :, at : at + 128
                    ]
            out_ref[...] = line_ref[...].astype(jnp.bfloat16)
        else:
            out_ref[...] = flat_ref[...].astype(jnp.bfloat16)


def pair_gradient(inputs, upstream, adapter_in_t, adapter_out, groups, chunk_rows):
    tokens, model = inputs.shape
    depth = upstream.shape[1]
    rank = adapter_in_t.shape[0]
    steps = 2
    block = model // steps
    out_shape = (rank * groups * chunk_rows, 128) if chunk_rows else (rank, model + depth)
    return pl.pallas_call(
        functools.partial(flat_kernel, rank, groups, chunk_rows),
        grid=(steps,),
        in_specs=[
            pl.BlockSpec((tokens, block), lambda i: (0, i)),
            pl.BlockSpec((tokens, depth), lambda i: (0, 0)),
            pl.BlockSpec((rank, block), lambda i: (0, i)),
            pl.BlockSpec((rank, depth), lambda i: (0, 0)),
        ],
        out_specs=pl.BlockSpec(out_shape, lambda i: (0, 0)),
        out_shape=jax.ShapeDtypeStruct(out_shape, jnp.bfloat16),
        scratch_shapes=[
            pltpu.VMEM((rank, tokens), jnp.bfloat16),
            pltpu.VMEM((tokens, rank), jnp.float32),
            pltpu.VMEM((depth, rank), jnp.float32),
            pltpu.VMEM((rank, model + depth), jnp.float32),
            pltpu.VMEM((max(rank * groups * chunk_rows, 8), 128), jnp.float32),
        ],
        cost_estimate=CHEAP,
    )(inputs, upstream, adapter_in_t, adapter_out)


def project_kernel(stride, chunk, width, chunk_rows, mean_rows, info_ref, part_ref, after_ref, out_ref, wide_ref, line_ref):
    devices, rows = wide_ref.shape
    tiles = out_ref.shape[0] // devices

    @pl.when(pl.program_id(0) == 0)
    def _():
        if chunk_rows:
            line_ref[...] = part_ref[...].astype(jnp.float32)
            for tile in range(mean_rows):
                line = line_ref[pl.ds(tile, devices, chunk_rows), :]
                wide_ref[:, tile * 128 : (tile + 1) * 128] = line.astype(jnp.bfloat16)
                mean = jnp.sum(line, axis=0, keepdims=True) / devices
                out_ref[pl.ds(PROJ // 128 + tile, devices, tiles), :] = jnp.broadcast_to(mean, (devices, 128))
        else:
            wide_ref[...] = part_ref[...]

    columns = pl.program_id(0) * width + lax.broadcasted_iota(jnp.int32, (1, width), 1)
    columns = columns * -2048144789
    total = jnp.zeros((devices, width), jnp.float32)
    for at in range(0, rows, chunk):
        count = min(chunk, rows - at)
        lines = lax.broadcasted_iota(jnp.int32, (count, 1), 0) + at
        lines = lines * stride + info_ref[START]
        total += dot(wide_ref[:, at : at + count], hash_signs(lines + columns))
    for tile in range(width // 128):
        at = pl.program_id(0) * (width // 128) + tile
        out_ref[pl.ds(at, devices, tiles), :] = total[:, tile * 128 : (tile + 1) * 128]


def project(info, part, stride, after, devices, length, chunk_rows):
    width = min(1024, PROJ)
    mean_rows = length // 128 if chunk_rows else 0
    tiles = PROJ // 128 + -(-mean_rows // 8) * 8
    return pl.pallas_call(
        functools.partial(project_kernel, stride, 256, width, chunk_rows, mean_rows),
        grid_spec=pltpu.PrefetchScalarGridSpec(
            num_scalar_prefetch=1,
            grid=(PROJ // width,),
            in_specs=[pl.BlockSpec(part.shape, lambda i, s: (0, 0)), pl.BlockSpec(memory_space=pl.ANY)],
            out_specs=pl.BlockSpec((devices * tiles, 128), lambda i, s: (0, 0)),
            scratch_shapes=[
                pltpu.VMEM((devices, length), jnp.bfloat16),
                pltpu.VMEM((max(devices * chunk_rows, 8), 128), jnp.float32),
            ],
        ),
        out_shape=jax.ShapeDtypeStruct((devices * tiles, 128), jnp.float32),
        cost_estimate=CHEAP,
    )(info, part, after).reshape(devices, tiles, 128)


def wrap32(value):
    return (value + 2**31) % 2**32 - 2**31


def per_device(inputs, upstream, value_weight, adapter_in, adapter_out, sign_seed):
    groups, members = lax.axis_size("fsdp"), lax.axis_size("grp")
    place, member = lax.axis_index("fsdp"), lax.axis_index("grp")
    devices = groups * members
    adapter_in_t = adapter_in.T
    rank, model = adapter_in_t.shape
    tokens = inputs.shape[0]
    columns = value_weight.shape[0]
    width = columns // members

    def along(array, shift):
        return lax.ppermute(array, "fsdp", [(i, (i + shift) % groups) for i in range(groups)])

    def across(array, mask):
        return lax.ppermute(array, "grp", [(i, i ^ mask) for i in range(members)])

    slice_own = lax.dynamic_slice_in_dim(value_weight, member * width, width, 0)
    shifts = sorted(range(1, groups), key=lambda s: (min(s, groups - s), s))
    weights = {}
    for s in shifts:
        if s in (1, groups - 1):
            weights[s] = along(slice_own, s)
        elif s <= groups // 2:
            weights[s] = along(weights[s - 1], 1)
        else:
            weights[s] = along(weights[s + 1], -1)
    chips = members // 2
    chip = member // 2
    plane = [across(upstream, 2 * k) if k else upstream for k in range(chips)]

    share = (model + upstream.shape[1]) // groups
    length = rank * share // members
    assert members % rank == 0
    split = members // rank
    row = member // split
    column = place * share + (member % split) * length
    start = (column * rank + row) * -1640531535 + sign_seed[0] * 668265263
    info = jnp.stack([member, place, chip, start] + [lax.rem(place + groups - s, groups) for s in range(groups)])

    chunk_rows = 0 if length % 128 or split > 1 else -(-length // 1024) * 8
    flat = pair_gradient(inputs, upstream, adapter_in_t, adapter_out, groups, chunk_rows)
    both = ("grp", "fsdp")
    if chunk_rows:
        chunks = flat.reshape(devices, chunk_rows, 128)
    else:
        chunks = flat.reshape(rank, groups, split, length).swapaxes(1, 2).reshape(devices, length)
    received = lax.all_to_all(chunks, both, split_axis=0, concat_axis=0, tiled=True)
    if chunk_rows:
        received = received.reshape(devices * chunk_rows, 128)

    result = own_columns(info, upstream, value_weight, adapter_in_t, adapter_out, groups * columns, flat)

    near = [s for s in shifts if s in (1, groups - 1)]
    batches = [near] + [[s] for s in shifts if s not in near]
    pairs, after, sent, feats = None, (result, received), [], None
    for batch in batches:
        pieces, pairs = piece_columns(
            info,
            batch,
            plane,
            [(weights[s], across(weights[s], 1)) for s in batch],
            adapter_in_t,
            pairs,
            adapter_out,
            after,
        )
        sent.append((batch, [across(p, 2 * k) if k else p for k, p in enumerate(pieces)]))
        after = (pieces[0], pieces[0])
        if feats is None:
            feats = project(
                info, received, wrap32(-1640531535 * rank), pieces[0], devices, length, chunk_rows
            )
            after = (feats, feats)
    parts = lax.all_to_all(feats, both, split_axis=0, concat_axis=0, tiled=True)
    raw = jnp.sum(parts[:, : PROJ // 128], axis=0)
    features = (raw * lax.rsqrt(jnp.mean(raw * raw) + 1e-06)).reshape(1, PROJ)
    mean_rows = length // 128
    if chunk_rows:
        totals = parts.reshape(members, groups, -1, 128)[:, :, PROJ // 128 : PROJ // 128 + mean_rows]
        totals = lax.dynamic_index_in_dim(totals, place, 1, keepdims=False)
    else:
        local_total = jnp.sum(received.astype(jnp.float32), axis=0) / devices
        totals = lax.all_to_all(
            jnp.broadcast_to(local_total, (members, length)), "grp", split_axis=0, concat_axis=0, tiled=True
        )
    mean_grad = totals.reshape(rank, share).T.reshape(-1)

    for index, (batch, pieces) in enumerate(sent):
        result = place_columns(info, batch, pieces, result, after[0], index == len(sent) - 1)
    return (result, features, mean_grad)


def solution(mesh):
    return jax.shard_map(
        per_device,
        mesh=mesh,
        in_specs=(
            P(("grp", "fsdp"), None),
            P(("grp", "fsdp"), None),
            P("fsdp", None),
            P(),
            P(),
            P(),
        ),
        out_specs=(P(("grp", "fsdp"), None), P(("grp", "fsdp"), None), P("fsdp")),
        check_vma=False,
    )
```

time: 189 us -> 118 us (0.62)
  waiting for transfers between devices: 105 us -> 32.9 us
  Pallas kernels: 0 us -> 44.6 us
  matrix products: 33 us -> 0 us
  between operations: 15.6 us -> 2.18 us
  starting transfers between devices: 19.5 us -> 27.7 us
  local copies, waits for them, and re-layouts: 12 us -> 7.66 us
    all_to_all x4 -> x2, waiting for transfers between devices: 105 us -> 7.7 us  [the longest x1 5.44 us: per_device(): parts = lax.all_to_all(feats, both, split_axis=0, concat_axis=0, tiled=True)]
    pallas_call x0 -> x7, Pallas kernels: none -> 44.6 us  [the longest x1 15.7 us: project(): pl.pallas_call(functools.partial(project_kernel, stride, 256, width, chun...]
    dot_general x6 -> x0, matrix products: 33 us -> none  [the longest x1 12.6 us: per_device(): partial_feats = jnp.dot(received, signs, preferred_element_type=jnp.float32)]
    ppermute x0 -> x15, waiting for transfers between devices: none -> 25.2 us  [the longest x3 16.9 us: along(): lax.ppermute(array, 'fsdp', [(i, (i + shift) % groups) for i in range(gro...]
    ppermute x0 -> x15, starting transfers between devices: none -> 18.9 us  [the longest x12 13.8 us: across(): return lax.ppermute(array, 'grp', [(i, i ^ mask) for i in range(members)])]
    all_to_all x4 -> x2, starting transfers between devices: 19.5 us -> 8.78 us  [the longest x1 5.3 us: per_device(): lax.all_to_all(chunks, both, split_axis=0, concat_axis=0, tiled=True)]
    all_to_all x2 -> x0, local copies, waits for them, and re-layouts: 6.13 us -> none  [the longest x1 4.79 us: per_device(): lax.all_to_all(columns, 'fsdp', split_axis=0, concat_axis=1, tiled=True)]
    unnamed x12 -> x29, local copies, waits for them, and re-layouts: 1.48 us -> 4.41 us
  transfers between devices with their start and end apart: 5 -> 17, of which waited for: 3 -> 5; matrix products, arithmetic and copies ran while one was open for 23% -> 1% of each run, Pallas kernels for 0% -> 38%
where the time goes in v3:
time: 118 us; the launch traced here: 116 us
  Pallas kernels  44.6 us (38%)
  waiting for transfers between devices  32.9 us (28%)
  starting transfers between devices  27.7 us (23%)
  local copies, waits for them, and re-layouts  7.66 us (6%)
  between operations  2.18 us (2%)
  other arithmetic  1.26 us (1%)
    ppermute x3, waiting for transfers between devices, along(): lax.ppermute(array, 'fsdp', [(i, (i + shift) % groups) for i in range(gro...  16.9 us
    pallas_call x1, Pallas kernels, project(): pl.pallas_call(functools.partial(project_kernel, stride, 256, width, chun...  15.7 us
    ppermute x12, starting transfers between devices, across(): return lax.ppermute(array, 'grp', [(i, i ^ mask) for i in range(members)])  13.8 us
    pallas_call x2, Pallas kernels, piece_columns(): pl.pallas_call(functools.partial(piece_kernel, chips, count, make_pairs),...  12 us
    ppermute x12, waiting for transfers between devices, across(): return lax.ppermute(array, 'grp', [(i, i ^ mask) for i in range(members)])  8.33 us
    pallas_call x2, Pallas kernels, place_columns(): pl.pallas_call(functools.partial(place_kernel, chips), grid_spec=pltpu.Pr...  6.15 us
    all_to_all x1, waiting for transfers between devices, per_device(): parts = lax.all_to_all(feats, both, split_axis=0, concat_axis=0, tiled=True)  5.44 us
    pallas_call x1, Pallas kernels, own_columns(): pl.pallas_call(own_kernel, grid_spec=pltpu.PrefetchScalarGridSpec(num_sca...  5.42 us
  transfers between devices with their start and end apart: 17, of which 5 were waited for; matrix products, arithmetic and copies ran while one was open for 1% of the time, Pallas kernels for 38%

profile of v3, /device:TPU:0, one launch (start us, length us, event | category | flops | bytes accessed | tf_op | source)
XLA Modules:
  0.0 116.3 jit_solution(8319767006304394010)
XLA Ops:
  0.6 1.1 constant_dynamic-slice_fusion.1
  1.7 3.1 %collective-permute-start.3 = (bf16[256,1024]{1,0:T(8,128)(2,1)S(1)}, bf16[256,1024]{1,0:T(8,128)(2,1)S(1)}, u32[]{:S(2)}, u32[]{:S(2)}) collective-permute-start(bf16[256,1024]{1,0:T(8,128)(2,1)S(1)} %constant_dynamic-slice_fusion.1), channel_id=1, source_target_pairs={{0,1},{1,2},{2,3},{3,0},{4,5},{5,6},{6,7},{7,4},{8,9},{9,10},{10,1... | collective-permute-start | bytes 1572872 | tf_op jit(solution)/shard_map/ppermute | solution.py:336
  4.8 2.1 %collective-permute-start.7 = (bf16[256,1024]{1,0:T(8,128)(2,1)S(1)}, bf16[256,1024]{1,0:T(8,128)(2,1)S(1)}, u32[]{:S(2)}, u32[]{:S(2)}) collective-permute-start(bf16[256,1024]{1,0:T(8,128)(2,1)S(1)} %constant_dynamic-slice_fusion.1), channel_id=1, source_target_pairs={{0,3},{1,0},{2,1},{3,2},{4,7},{5,4},{6,5},{7,6},{8,11},{9,8},{10,9... | collective-permute-start | bytes 1572872 | tf_op jit(solution)/shard_map/ppermute | solution.py:336
  6.9 2.6 %collective-permute-start.2 = (bf16[256,1024]{1,0:T(8,128)(2,1)}, bf16[256,1024]{1,0:T(8,128)(2,1)S(1)}, u32[]{:S(2)}, u32[]{:S(2)}) collective-permute-start(bf16[256,1024]{1,0:T(8,128)(2,1)} %refs_0_.3), channel_id=1, source_target_pairs={{0,24},{4,28},{8,16},{12,20},{16,8},{20,12},{24,0},{28,4},{1,25},{... | collective-permute-start | bytes 1572872 | tf_op jit(solution)/shard_map/ppermute | solution.py:339
  9.5 10.1 %collective-permute-done.3.refs_4_ = bf16[256,1024]{1,0:T(8,128)(2,1)S(1)} collective-permute-done((bf16[256,1024]{1,0:T(8,128)(2,1)S(1)}, bf16[256,1024]{1,0:T(8,128)(2,1)S(1)}, u32[]{:S(2)}, u32[]{:S(2)}) %collective-permute-start.3) | collective-permute-done | bytes 524320 | tf_op jit(solution)/shard_map/ppermute | solution.py:336
  19.6 1.8 %collective-permute-start.1 = (bf16[256,1024]{1,0:T(8,128)(2,1)}, bf16[256,1024]{1,0:T(8,128)(2,1)S(1)}, u32[]{:S(2)}, u32[]{:S(2)}) collective-permute-start(bf16[256,1024]{1,0:T(8,128)(2,1)} %refs_0_.3), channel_id=1, source_target_pairs={{0,16},{4,20},{8,24},{12,28},{16,0},{20,4},{24,8},{28,12},{1,17},{... | collective-permute-start | bytes 1572872 | tf_op jit(solution)/shard_map/ppermute | solution.py:339
  21.4 1.5 %collective-permute-start = (bf16[256,1024]{1,0:T(8,128)(2,1)}, bf16[256,1024]{1,0:T(8,128)(2,1)S(1)}, u32[]{:S(2)}, u32[]{:S(2)}) collective-permute-start(bf16[256,1024]{1,0:T(8,128)(2,1)} %refs_0_.3), channel_id=1, source_target_pairs={{0,8},{4,12},{8,0},{12,4},{16,24},{20,28},{24,16},{28,20},{1,9},{5... | collective-permute-start | bytes 1572872 | tf_op jit(solution)/shard_map/ppermute | solution.py:339
  22.9 6.8 %collective-permute-done.7.refs_6_ = bf16[256,1024]{1,0:T(8,128)(2,1)S(1)} collective-permute-done((bf16[256,1024]{1,0:T(8,128)(2,1)S(1)}, bf16[256,1024]{1,0:T(8,128)(2,1)S(1)}, u32[]{:S(2)}, u32[]{:S(2)}) %collective-permute-start.7) | collective-permute-done | bytes 524320 | tf_op jit(solution)/shard_map/ppermute | solution.py:336
  30.2 5.3 %shard_map.85.after_ref = bf16[768,128]{1,0:T(8,128)(2,1)} custom-call(bf16[256,8192]{1,0:T(8,128)(2,1)} %in_ref.1, bf16[256,1024]{1,0:T(8,128)(2,1)} %refs_0_.3, bf16[8,8192]{1,0:T(8,128)(2,1)} %bitcast.21, bf16[8,1024]{1,0:T(8,128)(2,1)} %refs_10_.1), custom_call_target="tpu_custom_call" | custom-call | tf_op jit(solution)/shard_map/pallas_call | solution.py:249
  35.5 5.3 %all-to-all-start = ((bf16[32,24,128]{2,1,0:T(8,128)(2,1)}), bf16[32,24,128]{2,1,0:T(8,128)(2,1)S(1)}, u32[]{:S(2)}, u32[]{:S(2)}) async-start(bf16[32,24,128]{2,1,0:T(8,128)(2,1)} %bitcast.26), calls=%async_computation | async-start | bytes 393216 | tf_op jit(solution)/shard_map/all_to_all | solution.py:371
  42.1 5.4 %shard_map.86.refs_11_.refs_4_ = bf16[256,8192]{1,0:T(8,128)(2,1)} custom-call(s32[8]{0:T(128)} %stack.35.info_ref, bf16[256,1024]{1,0:T(8,128)(2,1)} %refs_0_.3, bf16[2048,1024]{1,0:T(8,128)(2,1)} %weight_ref.1, bf16[8,8192]{1,0:T(8,128)(2,1)} %bitcast.22, bf16[8,1024]{1,0:T(8,128)(2,1)} %refs_10_.1, bf16[768,128]{1,0:T(8,128)(2,1)} %shard_map.85.after_ref), custom_call_target="tpu_custom_call" | custom-call | tf_op jit(solution)/shard_map/pallas_call | solution.py:64
  47.8 2.3 %all-to-all-done = bf16[32,24,128]{2,1,0:T(8,128)(2,1)S(1)} async-done(((bf16[32,24,128]{2,1,0:T(8,128)(2,1)}), bf16[32,24,128]{2,1,0:T(8,128)(2,1)S(1)}, u32[]{:S(2)}, u32[]{:S(2)}) %all-to-all-start) | async-done | bytes 196640 | tf_op jit(solution)/shard_map/all_to_all | solution.py:371
  51.4 7.3 %shard_map.87 = (bf16[256,1024]{1,0:T(8,128)(2,1)}, bf16[256,1024]{1,0:T(8,128)(2,1)}, bf16[256,1024]{1,0:T(8,128)(2,1)}, bf16[256,1024]{1,0:T(8,128)(2,1)}, bf16[4,256,16]{2,1,0:T(8,128)(2,1)}) custom-call(s32[8]{0:T(128)} %stack.35.info_ref, bf16[256,1024]{1,0:T(8,128)(2,1)} %refs_0_.3, bf16[256,1024]{1,0:T(8,128)(2,1)} %copy-done.2, ...), custom_call_target="tpu_custom_call" | custom-call | tf_op jit(solution)/shard_map/pallas_call | solution.py:135
  58.7 1.0 collective-permute-start.12
  60.2 2.1 %collective-permute-start.14 = (bf16[256,1024]{1,0:T(8,128)(2,1)}, bf16[256,1024]{1,0:T(8,128)(2,1)S(1)}, u32[]{:S(2)}, u32[]{:S(2)}) collective-permute-start(bf16[256,1024]{1,0:T(8,128)(2,1)} %get-tuple-element.20), channel_id=1, source_target_pairs={{0,24},{4,28},{8,16},{12,20},{16,8},{20,12},{24,0},{28,4},{1,25},{... | collective-permute-start | bytes 1572872 | tf_op jit(solution)/shard_map/ppermute | solution.py:339
  62.2 15.7 %shard_map.88 = f32[1792,128]{1,0:T(8,128)} custom-call(s32[8]{0:T(128)} %stack.35.info_ref, bf16[768,128]{1,0:T(8,128)(2,1)} %bitcast.28, bf16[256,1024]{1,0:T(8,128)(2,1)} %get-tuple-element.13.after_ref.refs_0_), custom_call_target="tpu_custom_call" | custom-call | tf_op jit(solution)/shard_map/pallas_call | solution.py:304
  78.7 4.7 %shard_map.89 = (bf16[256,512]{1,0:T(8,128)(2,1)}, bf16[256,512]{1,0:T(8,128)(2,1)}, bf16[256,512]{1,0:T(8,128)(2,1)}, bf16[256,512]{1,0:T(8,128)(2,1)}) custom-call(s32[8]{0:T(128)} %stack.35.info_ref, bf16[256,1024]{1,0:T(8,128)(2,1)} %refs_0_.3, bf16[256,1024]{1,0:T(8,128)(2,1)} %copy-done.2, bf16[256,1024]{1,0:T(8,128)(2,1)} %copy-done.1, ...), custom_call_target="tpu_custom_call" | custom-call | tf_op jit(solution)/shard_map/pallas_call | solution.py:135
  84.9 2.1 %collective-permute-start.11 = (bf16[256,512]{1,0:T(8,128)(2,1)}, bf16[256,512]{1,0:T(8,128)(2,1)S(1)}, u32[]{:S(2)}, u32[]{:S(2)}) collective-permute-start(bf16[256,512]{1,0:T(8,128)(2,1)} %get-tuple-element.17), channel_id=1, source_target_pairs={{0,24},{4,28},{8,16},{12,20},{16,8},{20,12},{24,0},{28,4},{1,25},{... | collective-permute-start | bytes 786440 | tf_op jit(solution)/shard_map/ppermute | solution.py:339
  86.9 3.5 %all-to-all-start.1 = ((f32[32,56,128]{2,1,0:T(8,128)}), f32[32,56,128]{2,1,0:T(8,128)S(1)}, u32[]{:S(2)}, u32[]{:S(2)}) async-start(f32[32,56,128]{2,1,0:T(8,128)} %bitcast.12.refs_8_.refs_9_), calls=%async_computation.1 | async-start | bytes 1835008 | tf_op jit(solution)/shard_map/all_to_all | solution.py:398
  91.4 3.3 %shard_map.90.refs_4_ = bf16[256,8192]{1,0:T(8,128)(2,1)} custom-call(s32[8]{0:T(128)} %stack.35.info_ref, bf16[256,1024]{1,0:T(8,128)(2,1)} %get-tuple-element.13.after_ref.refs_0_, bf16[256,1024]{1,0:T(8,128)(2,1)} %copy-done.8, bf16[256,1024]{1,0:T(8,128)(2,1)} %copy-done.9, bf16[256,1024]{1,0:T(8,128)(2,1)} %copy-done.10, ...), custom_call_target="tpu_custom_call", output_to_operand_aliasing={{}: (5, {})} | custom-call | tf_op jit(solution)/shard_map/pallas_call | solution.py:191
  94.7 8.3 %collective-permute-done.10.refs_2_ = bf16[256,512]{1,0:T(8,128)(2,1)S(1)} collective-permute-done((bf16[256,512]{1,0:T(8,128)(2,1)}, bf16[256,512]{1,0:T(8,128)(2,1)S(1)}, u32[]{:S(2)}, u32[]{:S(2)}) %collective-permute-start.10) | collective-permute-done | bytes 262176 | tf_op jit(solution)/shard_map/ppermute | solution.py:339
  104.4 2.9 %shard_map.91 = bf16[256,8192]{1,0:T(8,128)(2,1)} custom-call(s32[8]{0:T(128)} %stack.35.info_ref, bf16[256,512]{1,0:T(8,128)(2,1)} %get-tuple-element.14.refs_5_.refs_0_, bf16[256,512]{1,0:T(8,128)(2,1)} %copy-done.11, bf16[256,512]{1,0:T(8,128)(2,1)} %copy-done.12, bf16[256,512]{1,0:T(8,128)(2,1)} %copy-done.13, ...), custom_call_target="tpu_custom_call", output_to_operand_aliasing={{}: (5, {})} | custom-call | flops 99999997952 | tf_op jit(solution)/shard_map/pallas_call | solution.py:191
  107.3 5.4 %all-to-all-done.1 = f32[32,56,128]{2,1,0:T(8,128)S(1)} async-done(((f32[32,56,128]{2,1,0:T(8,128)}), f32[32,56,128]{2,1,0:T(8,128)S(1)}, u32[]{:S(2)}, u32[]{:S(2)}) %all-to-all-start.1) | async-done | bytes 917536 | tf_op jit(solution)/shard_map/all_to_all | solution.py:398
  115.1 1.1 reshape.45
  (55 shorter events, 9.5 us)
Async XLA Ops:
  1.7 17.9 %collective-permute-start.3 = (bf16[256,1024]{1,0:T(8,128)(2,1)S(1)}, bf16[256,1024]{1,0:T(8,128)(2,1)S(1)}, u32[]{:S(2)}, u32[]{:S(2)}) collective-permute-start(bf16[256,1024]{1,0:T(8,128)(2,1)S(1)} %constant_dynamic-slice_fusion.1), channel_id=1, source_target_pairs={{0,1},{1,2},{2,3},{3,0},{4,5},{5,6},{6,7},{7,4},{8,9},{9,10},{10,1... | collective-permute-start | bytes 1572872 | tf_op jit(solution)/shard_map/ppermute | solution.py:336
  4.8 24.8 %collective-permute-start.7 = (bf16[256,1024]{1,0:T(8,128)(2,1)S(1)}, bf16[256,1024]{1,0:T(8,128)(2,1)S(1)}, u32[]{:S(2)}, u32[]{:S(2)}) collective-permute-start(bf16[256,1024]{1,0:T(8,128)(2,1)S(1)} %constant_dynamic-slice_fusion.1), channel_id=1, source_target_pairs={{0,3},{1,0},{2,1},{3,2},{4,7},{5,4},{6,5},{7,6},{8,11},{9,8},{10,9... | collective-permute-start | bytes 1572872 | tf_op jit(solution)/shard_map/ppermute | solution.py:336
  6.9 22.8 %collective-permute-start.2 = (bf16[256,1024]{1,0:T(8,128)(2,1)}, bf16[256,1024]{1,0:T(8,128)(2,1)S(1)}, u32[]{:S(2)}, u32[]{:S(2)}) collective-permute-start(bf16[256,1024]{1,0:T(8,128)(2,1)} %refs_0_.3), channel_id=1, source_target_pairs={{0,24},{4,28},{8,16},{12,20},{16,8},{20,12},{24,0},{28,4},{1,25},{... | collective-permute-start | bytes 1572872 | tf_op jit(solution)/shard_map/ppermute | solution.py:339
  19.6 27.9 %copy-start.4 = (bf16[256,1024]{1,0:T(8,128)(2,1)}, bf16[256,1024]{1,0:T(8,128)(2,1)S(1)}, u32[]{:S(2)}) copy-start(bf16[256,1024]{1,0:T(8,128)(2,1)S(1)} %collective-permute-done.3.refs_4_) | copy-start | bytes 1572868
  19.6 27.9 %collective-permute-start.4 = (bf16[256,1024]{1,0:T(8,128)(2,1)S(1)}, bf16[256,1024]{1,0:T(8,128)(2,1)}, u32[]{:S(2)}, u32[]{:S(2)}) collective-permute-start(bf16[256,1024]{1,0:T(8,128)(2,1)S(1)} %collective-permute-done.3.refs_4_), channel_id=1, source_target_pairs={{0,1},{1,2},{2,3},{3,0},{4,5},{5,6},{6,7},{7,4},{8,9},{9,10},{10,1... | collective-permute-start | bytes 1572872 | tf_op jit(solution)/shard_map/ppermute | solution.py:336
  19.6 30.5 %collective-permute-start.1 = (bf16[256,1024]{1,0:T(8,128)(2,1)}, bf16[256,1024]{1,0:T(8,128)(2,1)S(1)}, u32[]{:S(2)}, u32[]{:S(2)}) collective-permute-start(bf16[256,1024]{1,0:T(8,128)(2,1)} %refs_0_.3), channel_id=1, source_target_pairs={{0,16},{4,20},{8,24},{12,28},{16,0},{20,4},{24,8},{28,12},{1,17},{... | collective-permute-start | bytes 1572872 | tf_op jit(solution)/shard_map/ppermute | solution.py:339
  21.4 28.7 %collective-permute-start = (bf16[256,1024]{1,0:T(8,128)(2,1)}, bf16[256,1024]{1,0:T(8,128)(2,1)S(1)}, u32[]{:S(2)}, u32[]{:S(2)}) collective-permute-start(bf16[256,1024]{1,0:T(8,128)(2,1)} %refs_0_.3), channel_id=1, source_target_pairs={{0,8},{4,12},{8,0},{12,4},{16,24},{20,28},{24,16},{28,20},{1,9},{5... | collective-permute-start | bytes 1572872 | tf_op jit(solution)/shard_map/ppermute | solution.py:339
  29.6 17.9 %copy-start.5 = (bf16[256,1024]{1,0:T(8,128)(2,1)}, bf16[256,1024]{1,0:T(8,128)(2,1)S(1)}, u32[]{:S(2)}) copy-start(bf16[256,1024]{1,0:T(8,128)(2,1)S(1)} %collective-permute-done.7.refs_6_) | copy-start | bytes 1572868
  29.6 20.5 %collective-permute-start.8 = (bf16[256,1024]{1,0:T(8,128)(2,1)S(1)}, bf16[256,1024]{1,0:T(8,128)(2,1)S(1)}, u32[]{:S(2)}, u32[]{:S(2)}) collective-permute-start(bf16[256,1024]{1,0:T(8,128)(2,1)S(1)} %collective-permute-done.7.refs_6_), channel_id=1, source_target_pairs={{0,4},{4,0},{8,12},{12,8},{16,20},{20,16},{24,28},{28,24},{1,5},{5... | collective-permute-start | bytes 1572872 | tf_op jit(solution)/shard_map/ppermute | solution.py:339
  29.6 17.9 %copy-start = (bf16[256,1024]{1,0:T(8,128)(2,1)}, bf16[256,1024]{1,0:T(8,128)(2,1)S(1)}, u32[]{:S(2)}) copy-start(bf16[256,1024]{1,0:T(8,128)(2,1)S(1)} %collective-permute-done.2.refs_3_) | copy-start | bytes 1572868
  29.7 20.5 %collective-permute-start.6 = (bf16[256,1024]{1,0:T(8,128)(2,1)S(1)}, bf16[256,1024]{1,0:T(8,128)(2,1)}, u32[]{:S(2)}, u32[]{:S(2)}) collective-permute-start(bf16[256,1024]{1,0:T(8,128)(2,1)S(1)} %collective-permute-done.3.refs_4_), channel_id=1, source_target_pairs={{0,4},{4,0},{8,12},{12,8},{16,20},{20,16},{24,28},{28,24},{1,5},{5... | collective-permute-start | bytes 1572872 | tf_op jit(solution)/shard_map/ppermute | solution.py:339
  35.5 14.6 %all-to-all-start = ((bf16[32,24,128]{2,1,0:T(8,128)(2,1)}), bf16[32,24,128]{2,1,0:T(8,128)(2,1)S(1)}, u32[]{:S(2)}, u32[]{:S(2)}) async-start(bf16[32,24,128]{2,1,0:T(8,128)(2,1)} %bitcast.26), calls=%async_computation | async-start | bytes 393216 | tf_op jit(solution)/shard_map/all_to_all | solution.py:371
  47.5 30.4 %collective-permute-start.5 = (bf16[256,1024]{1,0:T(8,128)(2,1)}, bf16[256,1024]{1,0:T(8,128)(2,1)S(1)}, u32[]{:S(2)}, u32[]{:S(2)}) collective-permute-start(bf16[256,1024]{1,0:T(8,128)(2,1)} %collective-permute-done.4.refs_4_), channel_id=1, source_target_pairs={{0,4},{4,0},{8,12},{12,8},{16,20},{20,16},{24,28},{28,24},{1,5},{5... | collective-permute-start | bytes 1572872 | tf_op jit(solution)/shard_map/ppermute | solution.py:339
  50.1 1.1 copy-start.2
  50.1 1.2 %copy-start.6 = (bf16[256,1024]{1,0:T(8,128)(2,1)}, bf16[256,1024]{1,0:T(8,128)(2,1)S(1)}, u32[]{:S(2)}) copy-start(bf16[256,1024]{1,0:T(8,128)(2,1)S(1)} %collective-permute-done.8.refs_7_) | copy-start | bytes 1572868
  58.7 26.2 %collective-permute-start.12 = (bf16[256,1024]{1,0:T(8,128)(2,1)}, bf16[256,1024]{1,0:T(8,128)(2,1)S(1)}, u32[]{:S(2)}, u32[]{:S(2)}) collective-permute-start(bf16[256,1024]{1,0:T(8,128)(2,1)} %get-tuple-element.18), channel_id=1, source_target_pairs={{0,8},{4,12},{8,0},{12,4},{16,24},{20,28},{24,16},{28,20},{1,9},{5... | collective-permute-start | bytes 1572872 | tf_op jit(solution)/shard_map/ppermute | solution.py:339
  59.6 30.8 %collective-permute-start.13 = (bf16[256,1024]{1,0:T(8,128)(2,1)}, bf16[256,1024]{1,0:T(8,128)(2,1)S(1)}, u32[]{:S(2)}, u32[]{:S(2)}) collective-permute-start(bf16[256,1024]{1,0:T(8,128)(2,1)} %get-tuple-element.19), channel_id=1, source_target_pairs={{0,16},{4,20},{8,24},{12,28},{16,0},{20,4},{24,8},{28,12},{1,17},{... | collective-permute-start | bytes 1572872 | tf_op jit(solution)/shard_map/ppermute | solution.py:339
  60.2 30.3 %collective-permute-start.14 = (bf16[256,1024]{1,0:T(8,128)(2,1)}, bf16[256,1024]{1,0:T(8,128)(2,1)S(1)}, u32[]{:S(2)}, u32[]{:S(2)}) collective-permute-start(bf16[256,1024]{1,0:T(8,128)(2,1)} %get-tuple-element.20), channel_id=1, source_target_pairs={{0,24},{4,28},{8,16},{12,20},{16,8},{20,12},{24,0},{28,4},{1,25},{... | collective-permute-start | bytes 1572872 | tf_op jit(solution)/shard_map/ppermute | solution.py:339
  83.4 11.3 %collective-permute-start.9 = (bf16[256,512]{1,0:T(8,128)(2,1)}, bf16[256,512]{1,0:T(8,128)(2,1)S(1)}, u32[]{:S(2)}, u32[]{:S(2)}) collective-permute-start(bf16[256,512]{1,0:T(8,128)(2,1)} %get-tuple-element.15), channel_id=1, source_target_pairs={{0,8},{4,12},{8,0},{12,4},{16,24},{20,28},{24,16},{28,20},{1,9},{5... | collective-permute-start | bytes 786440 | tf_op jit(solution)/shard_map/ppermute | solution.py:339
  84.3 18.7 %collective-permute-start.10 = (bf16[256,512]{1,0:T(8,128)(2,1)}, bf16[256,512]{1,0:T(8,128)(2,1)S(1)}, u32[]{:S(2)}, u32[]{:S(2)}) collective-permute-start(bf16[256,512]{1,0:T(8,128)(2,1)} %get-tuple-element.16), channel_id=1, source_target_pairs={{0,16},{4,20},{8,24},{12,28},{16,0},{20,4},{24,8},{28,12},{1,17},{... | collective-permute-start | bytes 786440 | tf_op jit(solution)/shard_map/ppermute | solution.py:339
  84.8 5.6 %copy-start.8 = (bf16[256,1024]{1,0:T(8,128)(2,1)}, bf16[256,1024]{1,0:T(8,128)(2,1)S(1)}, u32[]{:S(2)}) copy-start(bf16[256,1024]{1,0:T(8,128)(2,1)S(1)} %collective-permute-done.12.refs_1_) | copy-start | bytes 1572868
  84.9 18.1 %collective-permute-start.11 = (bf16[256,512]{1,0:T(8,128)(2,1)}, bf16[256,512]{1,0:T(8,128)(2,1)S(1)}, u32[]{:S(2)}, u32[]{:S(2)}) collective-permute-start(bf16[256,512]{1,0:T(8,128)(2,1)} %get-tuple-element.17), channel_id=1, source_target_pairs={{0,24},{4,28},{8,16},{12,20},{16,8},{20,12},{24,0},{28,4},{1,25},{... | collective-permute-start | bytes 786440 | tf_op jit(solution)/shard_map/ppermute | solution.py:339
  86.9 25.8 %all-to-all-start.1 = ((f32[32,56,128]{2,1,0:T(8,128)}), f32[32,56,128]{2,1,0:T(8,128)S(1)}, u32[]{:S(2)}, u32[]{:S(2)}) async-start(f32[32,56,128]{2,1,0:T(8,128)} %bitcast.12.refs_8_.refs_9_), calls=%async_computation.1 | async-start | bytes 1835008 | tf_op jit(solution)/shard_map/all_to_all | solution.py:398
  94.7 8.3 %copy-start.11 = (bf16[256,512]{1,0:T(8,128)(2,1)}, bf16[256,512]{1,0:T(8,128)(2,1)S(1)}, u32[]{:S(2)}) copy-start(bf16[256,512]{1,0:T(8,128)(2,1)S(1)} %collective-permute-done.9.refs_1_) | copy-start | bytes 786436
  (7 other events, 5.6 us)

commit v4 on v3

--- a/solution.py
+++ b/solution.py
@@ -84,21 +84,38 @@
     )(info, upstream, weight, adapter_in_t, adapter_out, after)
 
 
-def piece_kernel(chips, count, make_pairs, info_ref, *refs):
+def pair_kernel(chips, *refs):
+    out_adapter_ref, after_ref, out_ref = refs[chips:]
+    for chip in range(chips):
+        out_ref[chip] = split_pair(refs[chip][...], out_adapter_ref[...])
+
+
+def plane_pairs(plane, adapter_out, after):
+    chips = len(plane)
+    tokens, depth = plane[0].shape
+    rank2 = 2 * adapter_out.shape[0]
+    return pl.pallas_call(
+        functools.partial(pair_kernel, chips),
+        grid=(1,),
+        in_specs=[pl.BlockSpec((tokens, depth), lambda i: (0, 0))] * chips
+        + [pl.BlockSpec(adapter_out.shape, lambda i: (0, 0)), pl.BlockSpec(memory_space=pl.ANY)],
+        out_specs=pl.BlockSpec((chips, tokens, rank2), lambda i: (0, 0, 0)),
+        out_shape=jax.ShapeDtypeStruct((chips, tokens, rank2), jnp.bfloat16),
+        cost_estimate=DEAR,
+    )(*plane, adapter_out, after)
+
+
+def piece_kernel(chips, count, extra, info_ref, *refs):
     token_refs, refs = refs[:chips], refs[chips:]
     weight_refs, refs = refs[: 2 * count], refs[2 * count :]
     adapter_refs, refs = refs[:count], refs[count:]
-    pair_ref, refs = refs[0], refs[3:]
+    pair_ref, refs = refs[0], refs[1 + extra :]
     out_refs = refs[:chips]
     rows = token_refs[0].shape[0]
     width = weight_refs[0].shape[0]
     core = lax.rem(info_ref[MEMBER], 2)
     stacked = jnp.concatenate([ref[...] for ref in token_refs], axis=0)
-    if make_pairs:
-        pairs = split_pair(stacked, pair_ref[...])
-        refs[chips][...] = pairs.reshape(refs[chips].shape)
-    else:
-        pairs = pair_ref[...].reshape(chips * rows, pair_ref.shape[2])
+    pairs = pair_ref[...].reshape(chips * rows, pair_ref.shape[2])
     for index in range(count):
         for half in range(2):
             at = pl.multiple_of(lax.bitwise_xor(core, half) * width, width)
@@ -110,16 +127,13 @@
                 out_refs[chip][:, pl.ds(at, width)] = total[chip * rows : (chip + 1) * rows]
 
 
-def piece_columns(info, shifts, plane, weights, adapter_in_t, pairs, adapter_out, after):
+def piece_columns(info, shifts, plane, weights, adapter_in_t, pairs, after):
     chips = len(plane)
     tokens, depth = plane[0].shape
     width = weights[0][0].shape[0]
     count = len(weights)
     rank = adapter_in_t.shape[0]
-    make_pairs = pairs is None
     if width % 128:
-        if make_pairs:
-            pairs = jnp.stack([split_pair(part, adapter_out) for part in plane])
         core = lax.rem(info[MEMBER], 2)
         columns = []
         for (mine, other), shift in zip(weights, shifts):
@@ -127,13 +141,13 @@
             both = jnp.where(core == 0, jnp.concatenate([mine, other]), jnp.concatenate([other, mine]))
             low = twice(lax.dynamic_slice_in_dim(adapter_in_t, at * 2 * width, 2 * width, 1))
             columns.append([contract_last(t, both) + dot(p, low) for t, p in zip(plane, pairs)])
-        return [jnp.concatenate(c, axis=1).astype(jnp.bfloat16) for c in zip(*columns)], pairs
+        return [jnp.concatenate(c, axis=1).astype(jnp.bfloat16) for c in zip(*columns)]
     rows = tokens // 2
     pair_block = pl.BlockSpec((chips, rows, 2 * rank), lambda i, s: (0, i, 0))
     out_block = pl.BlockSpec((rows, count * 2 * width), lambda i, s: (i, 0))
     out_shape = jax.ShapeDtypeStruct((tokens, count * 2 * width), jnp.bfloat16)
     outs = pl.pallas_call(
-        functools.partial(piece_kernel, chips, count, make_pairs),
+        functools.partial(piece_kernel, chips, count, len(after)),
         grid_spec=pltpu.PrefetchScalarGridSpec(
             num_scalar_prefetch=1,
             grid=(tokens // rows,),
@@ -143,22 +157,21 @@
                 pl.BlockSpec((rank, 2 * width), lambda i, s, at=SHARDS + shift: (0, s[at] * chips + s[CHIP]))
                 for shift in shifts
             ]
-            + [pl.BlockSpec(adapter_out.shape, lambda i, s: (0, 0)) if make_pairs else pair_block]
-            + [pl.BlockSpec(memory_space=pl.ANY)] * 2,
-            out_specs=[out_block] * chips + ([pair_block] if make_pairs else []),
+            + [pair_block]
+            + [pl.BlockSpec(memory_space=pl.ANY)] * len(after),
+            out_specs=[out_block] * chips,
         ),
-        out_shape=[out_shape] * chips
-        + ([jax.ShapeDtypeStruct((chips, tokens, 2 * rank), jnp.bfloat16)] if make_pairs else []),
-        cost_estimate=CHEAP,
+        out_shape=[out_shape] * chips,
+        cost_estimate=CHEAP if len(after) == 1 else DEAR,
     )(
         info,
         *plane,
         *[w for pair in weights for w in pair],
         *[adapter_in_t] * count,
-        adapter_out if make_pairs else pairs,
+        pairs,
         *after,
     )
-    return (outs[:chips], outs[chips]) if make_pairs else (outs, pairs)
+    return outs
 
 
 def place_kernel(chips, info_ref, *refs):
@@ -268,9 +281,9 @@
     )(inputs, upstream, adapter_in_t, adapter_out)
 
 
-def project_kernel(stride, chunk, width, chunk_rows, mean_rows, info_ref, part_ref, after_ref, out_ref, wide_ref, line_ref):
+def project_kernel(stride, chunk, width, chunk_rows, mean_rows, info_ref, part_ref, after_ref, out_ref, wide_ref, line_ref, sum_ref):
     devices, rows = wide_ref.shape
-    tiles = out_ref.shape[0] // devices
+    tiles = sum_ref.shape[0] // devices
 
     @pl.when(pl.program_id(0) == 0)
     def _():
@@ -280,7 +293,7 @@
                 line = line_ref[pl.ds(tile, devices, chunk_rows), :]
                 wide_ref[:, tile * 128 : (tile + 1) * 128] = line.astype(jnp.bfloat16)
                 mean = jnp.sum(line, axis=0, keepdims=True) / devices
-                out_ref[pl.ds(PROJ // 128 + tile, devices, tiles), :] = jnp.broadcast_to(mean, (devices, 128))
+                sum_ref[pl.ds(PROJ // 128 + tile, devices, tiles), :] = jnp.broadcast_to(mean, (devices, 128))
         else:
             wide_ref[...] = part_ref[...]
 
@@ -294,11 +307,15 @@
         total += dot(wide_ref[:, at : at + count], hash_signs(lines + columns))
     for tile in range(width // 128):
         at = pl.program_id(0) * (width // 128) + tile
-        out_ref[pl.ds(at, devices, tiles), :] = total[:, tile * 128 : (tile + 1) * 128]
+        sum_ref[pl.ds(at, devices, tiles), :] = total[:, tile * 128 : (tile + 1) * 128]
+
+    @pl.when(pl.program_id(0) == pl.num_programs(0) - 1)
+    def _():
+        out_ref[...] = sum_ref[...].astype(out_ref.dtype)
 
 
 def project(info, part, stride, after, devices, length, chunk_rows):
-    width = min(1024, PROJ)
+    width = min(2048, PROJ)
     mean_rows = length // 128 if chunk_rows else 0
     tiles = PROJ // 128 + -(-mean_rows // 8) * 8
     return pl.pallas_call(
@@ -311,10 +328,11 @@
             scratch_shapes=[
                 pltpu.VMEM((devices, length), jnp.bfloat16),
                 pltpu.VMEM((max(devices * chunk_rows, 8), 128), jnp.float32),
+                pltpu.VMEM((devices * tiles, 128), jnp.float32),
             ],
         ),
-        out_shape=jax.ShapeDtypeStruct((devices * tiles, 128), jnp.float32),
-        cost_estimate=CHEAP,
+        out_shape=jax.ShapeDtypeStruct((devices * tiles, 128), jnp.bfloat16),
+        cost_estimate=DEAR,
     )(info, part, after).reshape(devices, tiles, 128)
 
 
@@ -376,32 +394,32 @@
 
     near = [s for s in shifts if s in (1, groups - 1)]
     batches = [near] + [[s] for s in shifts if s not in near]
-    pairs, after, sent, feats = None, (result, received), [], None
+    pairs = plane_pairs(plane, adapter_out, result)
+    after, sent, feats = [pairs], [], None
     for batch in batches:
-        pieces, pairs = piece_columns(
+        pieces = piece_columns(
             info,
             batch,
             plane,
             [(weights[s], across(weights[s], 1)) for s in batch],
             adapter_in_t,
             pairs,
-            adapter_out,
             after,
         )
         sent.append((batch, [across(p, 2 * k) if k else p for k, p in enumerate(pieces)]))
-        after = (pieces[0], pieces[0])
+        after = [p for k, p in enumerate(sent[-1][1]) if k]
         if feats is None:
             feats = project(
                 info, received, wrap32(-1640531535 * rank), pieces[0], devices, length, chunk_rows
             )
-            after = (feats, feats)
+            after.append(feats)
     parts = lax.all_to_all(feats, both, split_axis=0, concat_axis=0, tiled=True)
-    raw = jnp.sum(parts[:, : PROJ // 128], axis=0)
+    raw = jnp.sum(parts[:, : PROJ // 128].astype(jnp.float32), axis=0)
     features = (raw * lax.rsqrt(jnp.mean(raw * raw) + 1e-06)).reshape(1, PROJ)
     mean_rows = length // 128
     if chunk_rows:
         totals = parts.reshape(members, groups, -1, 128)[:, :, PROJ // 128 : PROJ // 128 + mean_rows]
-        totals = lax.dynamic_index_in_dim(totals, place, 1, keepdims=False)
+        totals = lax.dynamic_index_in_dim(totals, place, 1, keepdims=False).astype(jnp.float32)
     else:
         local_total = jnp.sum(received.astype(jnp.float32), axis=0) / devices
         totals = lax.all_to_all(
@@ -410,7 +428,7 @@
     mean_grad = totals.reshape(rank, share).T.reshape(-1)
 
     for index, (batch, pieces) in enumerate(sent):
-        result = place_columns(info, batch, pieces, result, after[0], index == len(sent) - 1)
+        result = place_columns(info, batch, pieces, result, features, index == len(sent) - 1)
     return (result, features, mean_grad)
 
 

time: 118 us -> 96.5 us (0.82); the launches traced: 116 us -> 96 us
  waiting for transfers between devices: 32.9 us -> 13 us
  starting transfers between devices: 27.7 us -> 24.8 us
  Pallas kernels: 44.6 us -> 46.4 us
    ppermute x3, waiting for transfers between devices: 16.9 us -> 3.31 us  [along(): lax.ppermute(array, 'fsdp', [(i, (i + shift) % groups) for i in range(gro...]
    all_to_all x1, waiting for transfers between devices: 5.44 us -> 0.01 us  [per_device(): parts = lax.all_to_all(feats, both, split_axis=0, concat_axis=0, tiled=True)]
    ppermute x12, starting transfers between devices: 13.8 us -> 10.9 us  [across(): return lax.ppermute(array, 'grp', [(i, i ^ mask) for i in range(members)])]
    all_to_all x1, waiting for transfers between devices: 2.27 us -> 0.01 us  [per_device(): lax.all_to_all(chunks, both, split_axis=0, concat_axis=0, tiled=True)]
    pallas_call x2 -> x3, Pallas kernels: 12 us -> 14.2 us  [the longest x2 11.2 us: piece_columns(): pl.pallas_call(functools.partial(piece_kernel, chips, count, len(after)),...]
    ppermute x12, waiting for transfers between devices: 8.33 us -> 9.69 us  [across(): return lax.ppermute(array, 'grp', [(i, i ^ mask) for i in range(members)])]
    unnamed x29 -> x28, local copies, waits for them, and re-layouts: 4.41 us -> 4.38 us
  transfers between devices with their start and end apart: 17 -> 17, of which waited for: 5 -> 5; matrix products, arithmetic and copies ran while one was open for 1% -> 4% of each run, Pallas kernels for 38% -> 45%
where the time goes in v4:
time: 96.5 us; the launch traced here: 96 us
  Pallas kernels  46.4 us (48%)
  starting transfers between devices  24.8 us (26%)
  waiting for transfers between devices  13 us (13%)
  local copies, waits for them, and re-layouts  8.47 us (9%)
  between operations  2.16 us (2%)
  other arithmetic  1.27 us (1%)
    pallas_call x1, Pallas kernels, project(): pl.pallas_call(functools.partial(project_kernel, stride, 256, width, chun...  15.3 us
    pallas_call x2, Pallas kernels, piece_columns(): pl.pallas_call(functools.partial(piece_kernel, chips, count, len(after)),...  11.2 us
    ppermute x12, starting transfers between devices, across(): return lax.ppermute(array, 'grp', [(i, i ^ mask) for i in range(members)])  10.9 us
    ppermute x12, waiting for transfers between devices, across(): return lax.ppermute(array, 'grp', [(i, i ^ mask) for i in range(members)])  9.69 us
    pallas_call x2, Pallas kernels, place_columns(): pl.pallas_call(functools.partial(place_kernel, chips), grid_spec=pltpu.Pr...  6.15 us
    ppermute x3, starting transfers between devices, along(): lax.ppermute(array, 'fsdp', [(i, (i + shift) % groups) for i in range(gro...  6.09 us
    pallas_call x1, Pallas kernels, own_columns(): pl.pallas_call(own_kernel, grid_spec=pltpu.PrefetchScalarGridSpec(num_sca...  5.42 us
    pallas_call x1, Pallas kernels, pair_gradient(): pl.pallas_call(functools.partial(flat_kernel, rank, groups, chunk_rows),...  5.32 us
  transfers between devices with their start and end apart: 17, of which 5 were waited for; matrix products, arithmetic and copies ran while one was open for 4% of the time, Pallas kernels for 45%

profile of v4, /device:TPU:0, one launch (start us, length us, event | category | flops | bytes accessed | tf_op | source)
XLA Modules:
  0.0 96.0 jit_solution(15156660473205312398)
XLA Ops:
  0.6 1.9 %constant_dynamic-slice_fusion.1 = bf16[256,1024]{1,0:T(8,128)(2,1)} fusion(bf16[2048,1024]{1,0:T(8,128)(2,1)} %weight_ref.1, s32[]{:T(128)S(6)} %select_n.18), kind=kLoop, calls=%fused_computation.6 | loop fusion | bytes 1048580 | tf_op jit(solution)/shard_map/dynamic_slice | solution.py:359
  2.5 3.0 %collective-permute-start.3 = (bf16[256,1024]{1,0:T(8,128)(2,1)}, bf16[256,1024]{1,0:T(8,128)(2,1)S(1)}, u32[]{:S(2)}, u32[]{:S(2)}) collective-permute-start(bf16[256,1024]{1,0:T(8,128)(2,1)} %constant_dynamic-slice_fusion.1), channel_id=1, source_target_pairs={{0,1},{1,2},{2,3},{3,0},{4,5},{5,6},{6,7},{7,4},{8,9},{9,10},{10,1... | collective-permute-start | bytes 1572872 | tf_op jit(solution)/shard_map/ppermute | solution.py:354
  5.5 2.0 %collective-permute-start.7 = (bf16[256,1024]{1,0:T(8,128)(2,1)}, bf16[256,1024]{1,0:T(8,128)(2,1)S(1)}, u32[]{:S(2)}, u32[]{:S(2)}) collective-permute-start(bf16[256,1024]{1,0:T(8,128)(2,1)} %constant_dynamic-slice_fusion.1), channel_id=1, source_target_pairs={{0,3},{1,0},{2,1},{3,2},{4,7},{5,4},{6,5},{7,6},{8,11},{9,8},{10,9... | collective-permute-start | bytes 1572872 | tf_op jit(solution)/shard_map/ppermute | solution.py:354
  7.6 2.7 %collective-permute-start.2 = (bf16[256,1024]{1,0:T(8,128)(2,1)}, bf16[256,1024]{1,0:T(8,128)(2,1)S(1)}, u32[]{:S(2)}, u32[]{:S(2)}) collective-permute-start(bf16[256,1024]{1,0:T(8,128)(2,1)} %refs_0_.5), channel_id=1, source_target_pairs={{0,24},{4,28},{8,16},{12,20},{16,8},{20,12},{24,0},{28,4},{1,25},{... | collective-permute-start | bytes 1572872 | tf_op jit(solution)/shard_map/ppermute | solution.py:357
  11.1 5.3 %shard_map.85.after_ref = bf16[768,128]{1,0:T(8,128)(2,1)} custom-call(bf16[256,8192]{1,0:T(8,128)(2,1)} %in_ref.1, bf16[256,1024]{1,0:T(8,128)(2,1)} %refs_0_.5, bf16[8,8192]{1,0:T(8,128)(2,1)} %bitcast.22, bf16[8,1024]{1,0:T(8,128)(2,1)} %refs_4_.1), custom_call_target="tpu_custom_call" | custom-call | tf_op jit(solution)/shard_map/pallas_call | solution.py:262
  16.4 4.3 %all-to-all-start = ((bf16[32,24,128]{2,1,0:T(8,128)(2,1)}), bf16[32,24,128]{2,1,0:T(8,128)(2,1)S(1)}, u32[]{:S(2)}, u32[]{:S(2)}) async-start(bf16[32,24,128]{2,1,0:T(8,128)(2,1)} %bitcast.28), calls=%async_computation | async-start | bytes 393216 | tf_op jit(solution)/shard_map/all_to_all | solution.py:389
  22.0 5.4 %shard_map.86.refs_5_.refs_4_ = bf16[256,8192]{1,0:T(8,128)(2,1)} custom-call(s32[8]{0:T(128)} %stack.35.info_ref, bf16[256,1024]{1,0:T(8,128)(2,1)} %refs_0_.5, bf16[2048,1024]{1,0:T(8,128)(2,1)} %weight_ref.1, bf16[8,8192]{1,0:T(8,128)(2,1)} %bitcast.23, bf16[8,1024]{1,0:T(8,128)(2,1)} %refs_4_.1, bf16[768,128]{1,0:T(8,128)(2,1)} %shard_map.85.after_ref), custom_call_target="tpu_custom_call" | custom-call | tf_op jit(solution)/shard_map/pallas_call | solution.py:64
  27.7 3.3 %collective-permute-done.7.refs_6_ = bf16[256,1024]{1,0:T(8,128)(2,1)S(1)} collective-permute-done((bf16[256,1024]{1,0:T(8,128)(2,1)}, bf16[256,1024]{1,0:T(8,128)(2,1)S(1)}, u32[]{:S(2)}, u32[]{:S(2)}) %collective-permute-start.7) | collective-permute-done | bytes 524320 | tf_op jit(solution)/shard_map/ppermute | solution.py:354
  31.0 1.0 %collective-permute-start.4 = (bf16[256,1024]{1,0:T(8,128)(2,1)S(1)}, bf16[256,1024]{1,0:T(8,128)(2,1)S(1)}, u32[]{:S(2)}, u32[]{:S(2)}) collective-permute-start(bf16[256,1024]{1,0:T(8,128)(2,1)S(1)} %collective-permute-done.3.refs_4_), channel_id=1, source_target_pairs={{0,1},{1,2},{2,3},{3,0},{4,5},{5,6},{6,7},{7,4},{8,9},{9,10},{10,1... | collective-permute-start | bytes 1572872 | tf_op jit(solution)/shard_map/ppermute | solution.py:354
  32.1 2.6 %collective-permute-done.1.refs_2_ = bf16[256,1024]{1,0:T(8,128)(2,1)S(1)} collective-permute-done((bf16[256,1024]{1,0:T(8,128)(2,1)}, bf16[256,1024]{1,0:T(8,128)(2,1)S(1)}, u32[]{:S(2)}, u32[]{:S(2)}) %collective-permute-start.1) | collective-permute-done | bytes 524320 | tf_op jit(solution)/shard_map/ppermute | solution.py:357
  36.3 3.0 %shard_map.87.refs_10_.refs_11_.refs_7_ = bf16[4,256,16]{2,1,0:T(8,128)(2,1)} custom-call(bf16[256,1024]{1,0:T(8,128)(2,1)} %refs_0_.5, bf16[256,1024]{1,0:T(8,128)(2,1)} %copy-done.2, bf16[256,1024]{1,0:T(8,128)(2,1)} %copy-done.1, bf16[256,1024]{1,0:T(8,128)(2,1)} %copy-done, bf16[8,1024]{1,0:T(8,128)(2,1)} %refs_4_.1, ...), custom_call_target="tpu_custom_call" | custom-call | flops 99999997952 | tf_op jit(solution)/shard_map/pallas_call | solution.py:97
  39.3 6.6 %shard_map.88 = (bf16[256,1024]{1,0:T(8,128)(2,1)}, bf16[256,1024]{1,0:T(8,128)(2,1)}, bf16[256,1024]{1,0:T(8,128)(2,1)}, bf16[256,1024]{1,0:T(8,128)(2,1)}) custom-call(s32[8]{0:T(128)} %stack.35.info_ref, bf16[256,1024]{1,0:T(8,128)(2,1)} %refs_0_.5, bf16[256,1024]{1,0:T(8,128)(2,1)} %copy-done.2, bf16[256,1024]{1,0:T(8,128)(2,1)} %copy-done.1, ...), custom_call_target="tpu_custom_call" | custom-call | tf_op jit(solution)/shard_map/pallas_call | solution.py:149
  45.9 1.6 %collective-permute-start.9 = (bf16[256,1024]{1,0:T(8,128)(2,1)}, bf16[256,1024]{1,0:T(8,128)(2,1)S(1)}, u32[]{:S(2)}, u32[]{:S(2)}) collective-permute-start(bf16[256,1024]{1,0:T(8,128)(2,1)} %get-tuple-element.11), channel_id=1, source_target_pairs={{0,8},{4,12},{8,0},{12,4},{16,24},{20,28},{24,16},{28,20},{1,9},{5... | collective-permute-start | bytes 1572872 | tf_op jit(solution)/shard_map/ppermute | solution.py:357
  47.5 1.0 %collective-permute-start.10 = (bf16[256,1024]{1,0:T(8,128)(2,1)}, bf16[256,1024]{1,0:T(8,128)(2,1)S(1)}, u32[]{:S(2)}, u32[]{:S(2)}) collective-permute-start(bf16[256,1024]{1,0:T(8,128)(2,1)} %get-tuple-element.12), channel_id=1, source_target_pairs={{0,16},{4,20},{8,24},{12,28},{16,0},{20,4},{24,8},{28,12},{1,17},{... | collective-permute-start | bytes 1572872 | tf_op jit(solution)/shard_map/ppermute | solution.py:357
  48.4 1.0 %collective-permute-start.11 = (bf16[256,1024]{1,0:T(8,128)(2,1)}, bf16[256,1024]{1,0:T(8,128)(2,1)S(1)}, u32[]{:S(2)}, u32[]{:S(2)}) collective-permute-start(bf16[256,1024]{1,0:T(8,128)(2,1)} %get-tuple-element.13), channel_id=1, source_target_pairs={{0,24},{4,28},{8,16},{12,20},{16,8},{20,12},{24,0},{28,4},{1,25},{... | collective-permute-start | bytes 1572872 | tf_op jit(solution)/shard_map/ppermute | solution.py:357
  50.2 15.3 %shard_map.89 = bf16[1792,128]{1,0:T(8,128)(2,1)} custom-call(s32[8]{0:T(128)} %stack.35.info_ref, bf16[768,128]{1,0:T(8,128)(2,1)} %bitcast.31, bf16[256,1024]{1,0:T(8,128)(2,1)} %get-tuple-element.14.after_ref.refs_0_), custom_call_target="tpu_custom_call" | custom-call | flops 99999997952 | tf_op jit(solution)/shard_map/pallas_call | solution.py:321
  65.4 3.5 %all-to-all-start.1 = ((bf16[32,56,128]{2,1,0:T(8,128)(2,1)}), bf16[32,56,128]{2,1,0:T(8,128)(2,1)S(1)}, u32[]{:S(2)}, u32[]{:S(2)}) async-start(bf16[32,56,128]{2,1,0:T(8,128)(2,1)} %bitcast.29), calls=%async_computation.1 | async-start | bytes 917504 | tf_op jit(solution)/shard_map/all_to_all | solution.py:416
  69.0 3.4 %collective-permute-done.10.refs_9_.refs_2_ = bf16[256,1024]{1,0:T(8,128)(2,1)S(1)} collective-permute-done((bf16[256,1024]{1,0:T(8,128)(2,1)}, bf16[256,1024]{1,0:T(8,128)(2,1)S(1)}, u32[]{:S(2)}, u32[]{:S(2)}) %collective-permute-start.10) | collective-permute-done | bytes 524320 | tf_op jit(solution)/shard_map/ppermute | solution.py:357
  74.0 4.7 %shard_map.90 = (bf16[256,512]{1,0:T(8,128)(2,1)}, bf16[256,512]{1,0:T(8,128)(2,1)}, bf16[256,512]{1,0:T(8,128)(2,1)}, bf16[256,512]{1,0:T(8,128)(2,1)}) custom-call(s32[8]{0:T(128)} %stack.35.info_ref, bf16[256,1024]{1,0:T(8,128)(2,1)} %refs_0_.5, bf16[256,1024]{1,0:T(8,128)(2,1)} %copy-done.2, bf16[256,1024]{1,0:T(8,128)(2,1)} %copy-done.1, ...), custom_call_target="tpu_custom_call" | custom-call | flops 99999997952 | tf_op jit(solution)/shard_map/pallas_call | solution.py:149
  79.1 2.6 %collective-permute-start.13 = (bf16[256,512]{1,0:T(8,128)(2,1)}, bf16[256,512]{1,0:T(8,128)(2,1)S(1)}, u32[]{:S(2)}, u32[]{:S(2)}) collective-permute-start(bf16[256,512]{1,0:T(8,128)(2,1)} %get-tuple-element.17), channel_id=1, source_target_pairs={{0,16},{4,20},{8,24},{12,28},{16,0},{20,4},{24,8},{28,12},{1,17},{... | collective-permute-start | bytes 786440 | tf_op jit(solution)/shard_map/ppermute | solution.py:357
  84.0 1.1 %reshape.50 = f32[18432]{0:T(1024)} reshape(f32[2304,8]{1,0:T(8,128)S(1)} %copy.12) | data formatting | bytes 147456 | tf_op jit(solution)/shard_map/reshape | solution.py:428
  85.7 3.3 %shard_map.91.refs_4_ = bf16[256,8192]{1,0:T(8,128)(2,1)} custom-call(s32[8]{0:T(128)} %stack.35.info_ref, bf16[256,1024]{1,0:T(8,128)(2,1)} %get-tuple-element.14.after_ref.refs_0_, bf16[256,1024]{1,0:T(8,128)(2,1)} %copy-done.5, bf16[256,1024]{1,0:T(8,128)(2,1)} %copy-done.6, bf16[256,1024]{1,0:T(8,128)(2,1)} %copy-done.7, ...), custom_call_target="tpu_custom_call", output_to_operand_aliasing={{}: (5, {})} | custom-call | tf_op jit(solution)/shard_map/pallas_call | solution.py:204
  89.0 3.4 %collective-permute-done.13.refs_2_ = bf16[256,512]{1,0:T(8,128)(2,1)S(1)} collective-permute-done((bf16[256,512]{1,0:T(8,128)(2,1)}, bf16[256,512]{1,0:T(8,128)(2,1)S(1)}, u32[]{:S(2)}, u32[]{:S(2)}) %collective-permute-start.13) | collective-permute-done | bytes 262176 | tf_op jit(solution)/shard_map/ppermute | solution.py:357
  93.1 2.9 %shard_map.92 = bf16[256,8192]{1,0:T(8,128)(2,1)} custom-call(s32[8]{0:T(128)} %stack.35.info_ref, bf16[256,512]{1,0:T(8,128)(2,1)} %get-tuple-element.15.refs_0_, bf16[256,512]{1,0:T(8,128)(2,1)} %copy-done.11, bf16[256,512]{1,0:T(8,128)(2,1)} %copy-done.12, bf16[256,512]{1,0:T(8,128)(2,1)} %copy-done.13, ...), custom_call_target="tpu_custom_call", output_to_operand_aliasing={{}: (5, {})} | custom-call | flops 99999997952 | tf_op jit(solution)/shard_map/pallas_call | solution.py:204
  (56 shorter events, 9.1 us)
Async XLA Ops:
  2.5 24.9 %collective-permute-start.3 = (bf16[256,1024]{1,0:T(8,128)(2,1)}, bf16[256,1024]{1,0:T(8,128)(2,1)S(1)}, u32[]{:S(2)}, u32[]{:S(2)}) collective-permute-start(bf16[256,1024]{1,0:T(8,128)(2,1)} %constant_dynamic-slice_fusion.1), channel_id=1, source_target_pairs={{0,1},{1,2},{2,3},{3,0},{4,5},{5,6},{6,7},{7,4},{8,9},{9,10},{10,1... | collective-permute-start | bytes 1572872 | tf_op jit(solution)/shard_map/ppermute | solution.py:354
  5.5 25.5 %collective-permute-start.7 = (bf16[256,1024]{1,0:T(8,128)(2,1)}, bf16[256,1024]{1,0:T(8,128)(2,1)S(1)}, u32[]{:S(2)}, u32[]{:S(2)}) collective-permute-start(bf16[256,1024]{1,0:T(8,128)(2,1)} %constant_dynamic-slice_fusion.1), channel_id=1, source_target_pairs={{0,3},{1,0},{2,1},{3,2},{4,7},{5,4},{6,5},{7,6},{8,11},{9,8},{10,9... | collective-permute-start | bytes 1572872 | tf_op jit(solution)/shard_map/ppermute | solution.py:354
  7.6 24.5 %collective-permute-start.2 = (bf16[256,1024]{1,0:T(8,128)(2,1)}, bf16[256,1024]{1,0:T(8,128)(2,1)S(1)}, u32[]{:S(2)}, u32[]{:S(2)}) collective-permute-start(bf16[256,1024]{1,0:T(8,128)(2,1)} %refs_0_.5), channel_id=1, source_target_pairs={{0,24},{4,28},{8,16},{12,20},{16,8},{20,12},{24,0},{28,4},{1,25},{... | collective-permute-start | bytes 1572872 | tf_op jit(solution)/shard_map/ppermute | solution.py:357
  10.2 24.5 %collective-permute-start.1 = (bf16[256,1024]{1,0:T(8,128)(2,1)}, bf16[256,1024]{1,0:T(8,128)(2,1)S(1)}, u32[]{:S(2)}, u32[]{:S(2)}) collective-permute-start(bf16[256,1024]{1,0:T(8,128)(2,1)} %refs_0_.5), channel_id=1, source_target_pairs={{0,16},{4,20},{8,24},{12,28},{16,0},{20,4},{24,8},{28,12},{1,17},{... | collective-permute-start | bytes 1572872 | tf_op jit(solution)/shard_map/ppermute | solution.py:357
  10.8 24.3 %collective-permute-start = (bf16[256,1024]{1,0:T(8,128)(2,1)}, bf16[256,1024]{1,0:T(8,128)(2,1)S(1)}, u32[]{:S(2)}, u32[]{:S(2)}) collective-permute-start(bf16[256,1024]{1,0:T(8,128)(2,1)} %refs_0_.5), channel_id=1, source_target_pairs={{0,8},{4,12},{8,0},{12,4},{16,24},{20,28},{24,16},{28,20},{1,9},{5... | collective-permute-start | bytes 1572872 | tf_op jit(solution)/shard_map/ppermute | solution.py:357
  16.4 33.1 %all-to-all-start = ((bf16[32,24,128]{2,1,0:T(8,128)(2,1)}), bf16[32,24,128]{2,1,0:T(8,128)(2,1)S(1)}, u32[]{:S(2)}, u32[]{:S(2)}) async-start(bf16[32,24,128]{2,1,0:T(8,128)(2,1)} %bitcast.28), calls=%async_computation | async-start | bytes 393216 | tf_op jit(solution)/shard_map/all_to_all | solution.py:389
  27.4 11.9 %copy-start.3 = (bf16[256,1024]{1,0:T(8,128)(2,1)}, bf16[256,1024]{1,0:T(8,128)(2,1)S(1)}, u32[]{:S(2)}) copy-start(bf16[256,1024]{1,0:T(8,128)(2,1)S(1)} %collective-permute-done.3.refs_4_) | copy-start | bytes 1572868
  27.4 11.9 %collective-permute-start.6 = (bf16[256,1024]{1,0:T(8,128)(2,1)S(1)}, bf16[256,1024]{1,0:T(8,128)(2,1)}, u32[]{:S(2)}, u32[]{:S(2)}) collective-permute-start(bf16[256,1024]{1,0:T(8,128)(2,1)S(1)} %collective-permute-done.3.refs_4_), channel_id=1, source_target_pairs={{0,4},{4,0},{8,12},{12,8},{16,20},{20,16},{24,28},{28,24},{1,5},{5... | collective-permute-start | bytes 1572872 | tf_op jit(solution)/shard_map/ppermute | solution.py:357
  31.0 8.3 %copy-start.4 = (bf16[256,1024]{1,0:T(8,128)(2,1)}, bf16[256,1024]{1,0:T(8,128)(2,1)S(1)}, u32[]{:S(2)}) copy-start(bf16[256,1024]{1,0:T(8,128)(2,1)S(1)} %collective-permute-done.7.refs_6_) | copy-start | bytes 1572868
  31.0 18.4 %collective-permute-start.4 = (bf16[256,1024]{1,0:T(8,128)(2,1)S(1)}, bf16[256,1024]{1,0:T(8,128)(2,1)S(1)}, u32[]{:S(2)}, u32[]{:S(2)}) collective-permute-start(bf16[256,1024]{1,0:T(8,128)(2,1)S(1)} %collective-permute-done.3.refs_4_), channel_id=1, source_target_pairs={{0,1},{1,2},{2,3},{3,0},{4,5},{5,6},{6,7},{7,4},{8,9},{9,10},{10,1... | collective-permute-start | bytes 1572872 | tf_op jit(solution)/shard_map/ppermute | solution.py:354
  32.1 3.0 %copy-start = (bf16[256,1024]{1,0:T(8,128)(2,1)}, bf16[256,1024]{1,0:T(8,128)(2,1)S(1)}, u32[]{:S(2)}) copy-start(bf16[256,1024]{1,0:T(8,128)(2,1)S(1)} %collective-permute-done.2.refs_3_) | copy-start | bytes 1572868
  32.1 7.2 %collective-permute-start.8 = (bf16[256,1024]{1,0:T(8,128)(2,1)S(1)}, bf16[256,1024]{1,0:T(8,128)(2,1)}, u32[]{:S(2)}, u32[]{:S(2)}) collective-permute-start(bf16[256,1024]{1,0:T(8,128)(2,1)S(1)} %collective-permute-done.7.refs_6_), channel_id=1, source_target_pairs={{0,4},{4,0},{8,12},{12,8},{16,20},{20,16},{24,28},{28,24},{1,5},{5... | collective-permute-start | bytes 1572872 | tf_op jit(solution)/shard_map/ppermute | solution.py:357
  45.9 23.1 %collective-permute-start.9 = (bf16[256,1024]{1,0:T(8,128)(2,1)}, bf16[256,1024]{1,0:T(8,128)(2,1)S(1)}, u32[]{:S(2)}, u32[]{:S(2)}) collective-permute-start(bf16[256,1024]{1,0:T(8,128)(2,1)} %get-tuple-element.11), channel_id=1, source_target_pairs={{0,8},{4,12},{8,0},{12,4},{16,24},{20,28},{24,16},{28,20},{1,9},{5... | collective-permute-start | bytes 1572872 | tf_op jit(solution)/shard_map/ppermute | solution.py:357
  47.5 24.9 %collective-permute-start.10 = (bf16[256,1024]{1,0:T(8,128)(2,1)}, bf16[256,1024]{1,0:T(8,128)(2,1)S(1)}, u32[]{:S(2)}, u32[]{:S(2)}) collective-permute-start(bf16[256,1024]{1,0:T(8,128)(2,1)} %get-tuple-element.12), channel_id=1, source_target_pairs={{0,16},{4,20},{8,24},{12,28},{16,0},{20,4},{24,8},{28,12},{1,17},{... | collective-permute-start | bytes 1572872 | tf_op jit(solution)/shard_map/ppermute | solution.py:357
  48.4 23.9 %collective-permute-start.11 = (bf16[256,1024]{1,0:T(8,128)(2,1)}, bf16[256,1024]{1,0:T(8,128)(2,1)S(1)}, u32[]{:S(2)}, u32[]{:S(2)}) collective-permute-start(bf16[256,1024]{1,0:T(8,128)(2,1)} %get-tuple-element.13), channel_id=1, source_target_pairs={{0,24},{4,28},{8,16},{12,20},{16,8},{20,12},{24,0},{28,4},{1,25},{... | collective-permute-start | bytes 1572872 | tf_op jit(solution)/shard_map/ppermute | solution.py:357
  49.4 16.0 %copy-start.9 = (bf16[256,1024]{1,0:T(8,128)(2,1)}, bf16[256,1024]{1,0:T(8,128)(2,1)S(1)}, u32[]{:S(2)}) copy-start(bf16[256,1024]{1,0:T(8,128)(2,1)S(1)} %collective-permute-done.4.refs_4_) | copy-start | bytes 1572868
  49.4 19.5 %collective-permute-start.5 = (bf16[256,1024]{1,0:T(8,128)(2,1)S(1)}, bf16[256,1024]{1,0:T(8,128)(2,1)S(1)}, u32[]{:S(2)}, u32[]{:S(2)}) collective-permute-start(bf16[256,1024]{1,0:T(8,128)(2,1)S(1)} %collective-permute-done.4.refs_4_), channel_id=1, source_target_pairs={{0,4},{4,0},{8,12},{12,8},{16,20},{20,16},{24,28},{28,24},{1,5},{5... | collective-permute-start | bytes 1572872 | tf_op jit(solution)/shard_map/ppermute | solution.py:357
  65.4 16.7 %all-to-all-start.1 = ((bf16[32,56,128]{2,1,0:T(8,128)(2,1)}), bf16[32,56,128]{2,1,0:T(8,128)(2,1)S(1)}, u32[]{:S(2)}, u32[]{:S(2)}) async-start(bf16[32,56,128]{2,1,0:T(8,128)(2,1)} %bitcast.29), calls=%async_computation.1 | async-start | bytes 917504 | tf_op jit(solution)/shard_map/all_to_all | solution.py:416
  69.0 3.4 %copy-start.10 = (bf16[256,1024]{1,0:T(8,128)(2,1)}, bf16[256,1024]{1,0:T(8,128)(2,1)S(1)}, u32[]{:S(2)}) copy-start(bf16[256,1024]{1,0:T(8,128)(2,1)S(1)} %collective-permute-done.5.refs_5_) | copy-start | bytes 1572868
  69.0 3.4 %copy-start.5 = (bf16[256,1024]{1,0:T(8,128)(2,1)}, bf16[256,1024]{1,0:T(8,128)(2,1)S(1)}, u32[]{:S(2)}) copy-start(bf16[256,1024]{1,0:T(8,128)(2,1)S(1)} %collective-permute-done.9.refs_8_.refs_1_) | copy-start | bytes 1572868
  78.7 10.3 %collective-permute-start.12 = (bf16[256,512]{1,0:T(8,128)(2,1)}, bf16[256,512]{1,0:T(8,128)(2,1)S(1)}, u32[]{:S(2)}, u32[]{:S(2)}) collective-permute-start(bf16[256,512]{1,0:T(8,128)(2,1)} %get-tuple-element.16), channel_id=1, source_target_pairs={{0,8},{4,12},{8,0},{12,4},{16,24},{20,28},{24,16},{28,20},{1,9},{5... | collective-permute-start | bytes 786440 | tf_op jit(solution)/shard_map/ppermute | solution.py:357
  79.1 13.2 %collective-permute-start.13 = (bf16[256,512]{1,0:T(8,128)(2,1)}, bf16[256,512]{1,0:T(8,128)(2,1)S(1)}, u32[]{:S(2)}, u32[]{:S(2)}) collective-permute-start(bf16[256,512]{1,0:T(8,128)(2,1)} %get-tuple-element.17), channel_id=1, source_target_pairs={{0,16},{4,20},{8,24},{12,28},{16,0},{20,4},{24,8},{28,12},{1,17},{... | collective-permute-start | bytes 786440 | tf_op jit(solution)/shard_map/ppermute | solution.py:357
  81.8 10.6 %collective-permute-start.14 = (bf16[256,512]{1,0:T(8,128)(2,1)}, bf16[256,512]{1,0:T(8,128)(2,1)S(1)}, u32[]{:S(2)}, u32[]{:S(2)}) collective-permute-start(bf16[256,512]{1,0:T(8,128)(2,1)} %get-tuple-element.18), channel_id=1, source_target_pairs={{0,24},{4,28},{8,16},{12,20},{16,8},{20,12},{24,0},{28,4},{1,25},{... | collective-permute-start | bytes 786440 | tf_op jit(solution)/shard_map/ppermute | solution.py:357
  89.0 3.4 %copy-start.11 = (bf16[256,512]{1,0:T(8,128)(2,1)}, bf16[256,512]{1,0:T(8,128)(2,1)S(1)}, u32[]{:S(2)}) copy-start(bf16[256,512]{1,0:T(8,128)(2,1)S(1)} %collective-permute-done.12.refs_1_) | copy-start | bytes 786436
  (7 other events, 5.4 us)

commit v5 on v4

--- a/solution.py
+++ b/solution.py
@@ -12,6 +12,7 @@
 lowrank_scale_factor = 2.0
 
 CHEAP = pl.CostEstimate(flops=0, bytes_accessed=0, transcendentals=0)
+VMEM_BYTES = 24 * 2**20
 MEMBER, PLACE, CHIP, START, SHARDS = range(5)
 DEAR = pl.CostEstimate(flops=10**11, bytes_accessed=0, transcendentals=0)
 
@@ -30,7 +31,7 @@
     mixed = mixed ^ lax.shift_right_logical(mixed, 15)
     mixed = mixed * 181057748
     mixed = mixed ^ lax.shift_left(mixed, 13)
-    return jnp.where(mixed < 0, -1.0, 1.0).astype(jnp.bfloat16)
+    return jnp.where(mixed < 0, jnp.bfloat16(-1.0), jnp.bfloat16(1.0))
 
 
 def split_pair(tokens, adapter_out):
@@ -40,15 +41,23 @@
     return jnp.concatenate([high, low], axis=1)
 
 
+ANYWHERE = pl.BlockSpec(memory_space=pl.ANY)
+IN_VMEM = pl.BlockSpec(memory_space=pltpu.VMEM)
+IN_SMEM = pl.BlockSpec(memory_space=pltpu.SMEM)
+TOKEN = jax.ShapeDtypeStruct((8, 128), jnp.float32)
+TOKEN_BLOCK = pl.BlockSpec((8, 128), lambda *_: (0, 0))
+
+
 def twice(part):
     return jnp.concatenate([part, part], axis=0)
 
 
-def own_kernel(info_ref, up_ref, weight_ref, in_adapter_ref, out_adapter_ref, after_ref, out_ref, pair_ref, turned_ref):
+def own_kernel(info_ref, up_ref, weight_ref, in_adapter_ref, out_adapter_ref, after_ref, out_ref, token_ref, pair_ref, turned_ref):
     @pl.when(pl.program_id(0) == 0)
     def _():
         pair_ref[...] = split_pair(up_ref[...], out_adapter_ref[...])
         turned_ref[...] = up_ref[...].T
+        token_ref[...] = jnp.zeros_like(token_ref)
 
     total = dot(weight_ref[...], turned_ref[...]).T
     total += dot(pair_ref[...], twice(in_adapter_ref[...]))
@@ -73,14 +82,15 @@
                 pl.BlockSpec(adapter_out.shape, lambda i, s: (0, 0)),
                 pl.BlockSpec(memory_space=pl.ANY),
             ],
-            out_specs=pl.BlockSpec((tokens, block), lambda i, s: (0, s[PLACE] * steps + i)),
+            out_specs=[pl.BlockSpec((tokens, block), lambda i, s: (0, s[PLACE] * steps + i)), TOKEN_BLOCK],
             scratch_shapes=[
                 pltpu.VMEM((tokens, 2 * rank), jnp.bfloat16),
                 pltpu.VMEM((depth, tokens), jnp.bfloat16),
             ],
         ),
-        out_shape=jax.ShapeDtypeStruct((tokens, all_columns), jnp.bfloat16),
+        out_shape=[jax.ShapeDtypeStruct((tokens, all_columns), jnp.bfloat16), TOKEN],
         cost_estimate=CHEAP,
+        compiler_params=pltpu.CompilerParams(vmem_limit_bytes=VMEM_BYTES),
     )(info, upstream, weight, adapter_in_t, adapter_out, after)
 
 
@@ -92,127 +102,147 @@
 
 def plane_pairs(plane, adapter_out, after):
     chips = len(plane)
-    tokens, depth = plane[0].shape
-    rank2 = 2 * adapter_out.shape[0]
+    tokens = plane[0].shape[0]
     return pl.pallas_call(
         functools.partial(pair_kernel, chips),
-        grid=(1,),
-        in_specs=[pl.BlockSpec((tokens, depth), lambda i: (0, 0))] * chips
-        + [pl.BlockSpec(adapter_out.shape, lambda i: (0, 0)), pl.BlockSpec(memory_space=pl.ANY)],
-        out_specs=pl.BlockSpec((chips, tokens, rank2), lambda i: (0, 0, 0)),
-        out_shape=jax.ShapeDtypeStruct((chips, tokens, rank2), jnp.bfloat16),
+        in_specs=[IN_VMEM] * (chips + 1) + [ANYWHERE],
+        out_specs=IN_VMEM,
+        out_shape=jax.ShapeDtypeStruct((chips, tokens, 2 * adapter_out.shape[0]), jnp.bfloat16),
         cost_estimate=DEAR,
+        compiler_params=pltpu.CompilerParams(vmem_limit_bytes=VMEM_BYTES),
     )(*plane, adapter_out, after)
 
 
-def piece_kernel(chips, count, extra, info_ref, *refs):
-    token_refs, refs = refs[:chips], refs[chips:]
-    weight_refs, refs = refs[: 2 * count], refs[2 * count :]
-    adapter_refs, refs = refs[:count], refs[count:]
-    pair_ref, refs = refs[0], refs[1 + extra :]
-    out_refs = refs[:chips]
+def slice_columns(info_ref, shift, half, width, chips, tokens, weight, adapter_ref, pairs):
+    at = pl.multiple_of(lax.bitwise_xor(lax.rem(info_ref[MEMBER], 2), half) * width, width)
+    here = (info_ref[SHARDS + shift] * chips + info_ref[CHIP]) * 2 * width + at
+    total = contract_last(tokens, weight)
+    total += dot(pairs, twice(adapter_ref[:, pl.ds(pl.multiple_of(here, width), width)]))
+    return at, total.astype(jnp.bfloat16)
+
+
+def piece_kernel(shifts, chips, info_ref, *refs):
+    others = chips - 1
+    token_refs, refs = refs[:others], refs[others:]
+    weight_refs, refs = refs[: 2 * len(shifts)], refs[2 * len(shifts) :]
+    adapter_ref, pair_ref, _ = refs[:3]
+    out_refs, token_ref = refs[3 : 3 + others], refs[3 + others]
+    token_ref[...] = jnp.zeros_like(token_ref)
     rows = token_refs[0].shape[0]
     width = weight_refs[0].shape[0]
-    core = lax.rem(info_ref[MEMBER], 2)
     stacked = jnp.concatenate([ref[...] for ref in token_refs], axis=0)
-    pairs = pair_ref[...].reshape(chips * rows, pair_ref.shape[2])
-    for index in range(count):
+    pairs = pair_ref[1:].reshape(others * rows, pair_ref.shape[2])
+    for index, shift in enumerate(shifts):
         for half in range(2):
-            at = pl.multiple_of(lax.bitwise_xor(core, half) * width, width)
-            total = contract_last(stacked, weight_refs[2 * index + half][...])
-            total += dot(pairs, twice(adapter_refs[index][:, pl.ds(at, width)]))
-            total = total.astype(out_refs[0].dtype)
+            weight = weight_refs[2 * index + half][...]
+            at, total = slice_columns(info_ref, shift, half, width, chips, stacked, weight, adapter_ref, pairs)
             at = pl.multiple_of(at + index * 2 * width, width)
-            for chip in range(chips):
-                out_refs[chip][:, pl.ds(at, width)] = total[chip * rows : (chip + 1) * rows]
-
-
-def piece_columns(info, shifts, plane, weights, adapter_in_t, pairs, after):
+            for k in range(others):
+                out_refs[k][:, pl.ds(at, width)] = total[k * rows : (k + 1) * rows]
+
+
+def plain_columns(info, shift, tokens, weights, adapter_in_t, pairs, chips):
+    mine, other = weights
+    width = mine.shape[0]
+    ordered = [jnp.concatenate([mine, other]), jnp.concatenate([other, mine])]
+    both = jnp.where(lax.rem(info[MEMBER], 2) == 0, *ordered)
+    at = (info[SHARDS + shift] * chips + info[CHIP]) * 2 * width
+    low = twice(lax.dynamic_slice_in_dim(adapter_in_t, at, 2 * width, 1))
+    return (contract_last(tokens, both) + dot(pairs, low)).astype(jnp.bfloat16)
+
+
+def piece_columns(info, shifts, plane, weights, adapter_in_t, pairs, after, cost):
     chips = len(plane)
-    tokens, depth = plane[0].shape
+    tokens = plane[0].shape[0]
     width = weights[0][0].shape[0]
+    if width % 128:
+        columns = [
+            [plain_columns(info, s, plane[k], w, adapter_in_t, pairs[k], chips) for s, w in zip(shifts, weights)]
+            for k in range(1, chips)
+        ]
+        return [jnp.concatenate(c, axis=1) for c in columns], after
     count = len(weights)
-    rank = adapter_in_t.shape[0]
-    if width % 128:
-        core = lax.rem(info[MEMBER], 2)
-        columns = []
-        for (mine, other), shift in zip(weights, shifts):
-            at = info[SHARDS + shift] * chips + info[CHIP]
-            both = jnp.where(core == 0, jnp.concatenate([mine, other]), jnp.concatenate([other, mine]))
-            low = twice(lax.dynamic_slice_in_dim(adapter_in_t, at * 2 * width, 2 * width, 1))
-            columns.append([contract_last(t, both) + dot(p, low) for t, p in zip(plane, pairs)])
-        return [jnp.concatenate(c, axis=1).astype(jnp.bfloat16) for c in zip(*columns)]
-    rows = tokens // 2
-    pair_block = pl.BlockSpec((chips, rows, 2 * rank), lambda i, s: (0, i, 0))
-    out_block = pl.BlockSpec((rows, count * 2 * width), lambda i, s: (i, 0))
     out_shape = jax.ShapeDtypeStruct((tokens, count * 2 * width), jnp.bfloat16)
     outs = pl.pallas_call(
-        functools.partial(piece_kernel, chips, count, len(after)),
-        grid_spec=pltpu.PrefetchScalarGridSpec(
-            num_scalar_prefetch=1,
-            grid=(tokens // rows,),
-            in_specs=[pl.BlockSpec((rows, depth), lambda i, s: (i, 0))] * chips
-            + [pl.BlockSpec((width, depth), lambda i, s: (0, 0))] * (2 * count)
-            + [
-                pl.BlockSpec((rank, 2 * width), lambda i, s, at=SHARDS + shift: (0, s[at] * chips + s[CHIP]))
-                for shift in shifts
-            ]
-            + [pair_block]
-            + [pl.BlockSpec(memory_space=pl.ANY)] * len(after),
-            out_specs=[out_block] * chips,
-        ),
-        out_shape=[out_shape] * chips,
-        cost_estimate=CHEAP if len(after) == 1 else DEAR,
-    )(
-        info,
-        *plane,
-        *[w for pair in weights for w in pair],
-        *[adapter_in_t] * count,
-        pairs,
-        *after,
-    )
-    return outs
-
-
-def place_kernel(chips, info_ref, *refs):
-    piece_refs, out_ref = refs[:chips], refs[chips + 2]
-    width = piece_refs[0].shape[1]
-    for k in range(chips):
-        at = pl.multiple_of(lax.bitwise_xor(info_ref[CHIP], k) * width, width)
-        out_ref[:, pl.ds(at, width)] = piece_refs[k][...]
-
-
-def place_columns(info, shifts, pieces, buffer, after, last):
-    chips = len(pieces)
-    tokens, width = pieces[0].shape
-    width = width // len(shifts)
-    if width % 128:
+        functools.partial(piece_kernel, shifts, chips),
+        in_specs=[IN_SMEM] + [IN_VMEM] * (chips - 1 + 2 * count + 2) + [ANYWHERE],
+        out_specs=[IN_VMEM] * chips,
+        out_shape=[out_shape] * (chips - 1) + [TOKEN],
+        cost_estimate=cost,
+        compiler_params=pltpu.CompilerParams(vmem_limit_bytes=VMEM_BYTES),
+    )(info, *plane[1:], *[w for pair in weights for w in pair], adapter_in_t, pairs, after)
+    return outs[:-1], outs[-1]
+
+
+def place_kernel(shifts, chips, mine, info_ref, *refs):
+    piece_refs, refs = refs[: chips - 1], refs[chips - 1 :]
+    if mine:
+        up_ref, refs = refs[0], refs[1:]
+        weight_refs, refs = refs[: 2 * len(mine)], refs[2 * len(mine) :]
+        adapter_ref, pair_ref, refs = refs[0], refs[1], refs[2:]
+        mine_ref, refs = refs[-1], refs[:-1]
+    out_ref, sems = refs[2:]
+    width = piece_refs[0].shape[1] // len(shifts)
+    copies = []
+
+    def send(source, at):
+        at = pl.multiple_of(at * width, width)
+        copies.append(pltpu.make_async_copy(source, out_ref.at[:, pl.ds(at, width)], sems.at[len(copies)]))
+        copies[-1].start()
+
+    for index, shift in enumerate(shifts):
+        for k in range(1, chips):
+            at = info_ref[SHARDS + shift] * chips + lax.bitwise_xor(info_ref[CHIP], k)
+            send(piece_refs[k - 1].at[:, pl.ds(index * width, width)], at)
+    for index, shift in enumerate(mine):
+        for half in range(2):
+            at, total = slice_columns(
+                info_ref,
+                shift,
+                half,
+                width // 2,
+                chips,
+                up_ref[...],
+                weight_refs[2 * index + half][...],
+                adapter_ref,
+                pair_ref[0],
+            )
+            mine_ref[:, pl.ds(pl.multiple_of(at + index * width, width // 2), width // 2)] = total
+        send(mine_ref.at[:, pl.ds(index * width, width)], info_ref[SHARDS + shift] * chips + info_ref[CHIP])
+    for copy in copies:
+        copy.wait()
+
+
+def place_columns(info, shifts, pieces, buffer, after, cost, mine, upstream, weights, adapter_in_t, pairs):
+    chips = len(pieces) + 1
+    tokens = pieces[0].shape[0]
+    width = pieces[0].shape[1] // len(shifts)
+    if width % 128 or width % 256 and mine:
         for index, shift in enumerate(shifts):
-            for k, piece in enumerate(pieces):
+            for k, piece in enumerate(pieces, 1):
                 part = piece[:, index * width : (index + 1) * width]
                 at = (info[SHARDS + shift] * chips + lax.bitwise_xor(info[CHIP], k)) * width
                 buffer = lax.dynamic_update_slice_in_dim(buffer, part, at, 1)
+        for shift in mine:
+            part = plain_columns(info, shift, upstream, weights[shift], adapter_in_t, pairs[0], chips)
+            at = (info[SHARDS + shift] * chips + info[CHIP]) * width
+            buffer = lax.dynamic_update_slice_in_dim(buffer, part, at, 1)
         return buffer
-
-    def shard_of(w, s):
-        at = s[SHARDS + shifts[0]]
-        for index in range(1, len(shifts)):
-            at = jnp.where(w == index, s[SHARDS + shifts[index]], at)
-        return 0, at
-
-    anywhere = pl.BlockSpec(memory_space=pl.ANY)
+    extra = []
+    if mine:
+        extra = [upstream] + [w for shift in mine for w in weights[shift]] + [adapter_in_t, pairs]
+    operands = [info, *pieces, *extra, buffer, after]
     return pl.pallas_call(
-        functools.partial(place_kernel, chips),
-        grid_spec=pltpu.PrefetchScalarGridSpec(
-            num_scalar_prefetch=1,
-            grid=(len(shifts),),
-            in_specs=[pl.BlockSpec((tokens, width), lambda w, s: (0, w))] * chips + [anywhere, anywhere],
-            out_specs=pl.BlockSpec((tokens, chips * width), shard_of),
-        ),
+        functools.partial(place_kernel, shifts, chips, mine),
+        in_specs=[IN_SMEM] + [IN_VMEM] * (len(operands) - 3) + [ANYWHERE] * 2,
+        out_specs=ANYWHERE,
         out_shape=jax.ShapeDtypeStruct(buffer.shape, buffer.dtype),
-        input_output_aliases={1 + chips: 0},
-        cost_estimate=DEAR if last else CHEAP,
-    )(info, *pieces, buffer, after)
+        scratch_shapes=[pltpu.SemaphoreType.DMA(((chips - 1) * len(shifts) + len(mine),))]
+        + ([pltpu.VMEM((tokens, len(mine) * width), jnp.bfloat16)] if mine else []),
+        input_output_aliases={len(operands) - 2: 0},
+        cost_estimate=cost,
+        compiler_params=pltpu.CompilerParams(vmem_limit_bytes=VMEM_BYTES),
+    )(*operands)
 
 
 def flat_kernel(rank, groups, chunk_rows, in_ref, up_ref, in_adapter_ref, out_adapter_ref, out_ref, scaled_ref, narrow_ref, turn_ref, flat_ref, line_ref):
@@ -281,12 +311,13 @@
     )(inputs, upstream, adapter_in_t, adapter_out)
 
 
-def project_kernel(stride, chunk, width, chunk_rows, mean_rows, info_ref, part_ref, after_ref, out_ref, wide_ref, line_ref, sum_ref):
+def project_kernel(stride, chunk, width, chunk_rows, mean_rows, info_ref, part_ref, after_ref, out_ref, token_ref, wide_ref, line_ref, sum_ref):
     devices, rows = wide_ref.shape
     tiles = sum_ref.shape[0] // devices
 
     @pl.when(pl.program_id(0) == 0)
     def _():
+        token_ref[...] = jnp.zeros_like(token_ref)
         if chunk_rows:
             line_ref[...] = part_ref[...].astype(jnp.float32)
             for tile in range(mean_rows):
@@ -315,25 +346,27 @@
 
 
 def project(info, part, stride, after, devices, length, chunk_rows):
-    width = min(2048, PROJ)
+    width = PROJ
     mean_rows = length // 128 if chunk_rows else 0
     tiles = PROJ // 128 + -(-mean_rows // 8) * 8
-    return pl.pallas_call(
+    feats, token = pl.pallas_call(
         functools.partial(project_kernel, stride, 256, width, chunk_rows, mean_rows),
         grid_spec=pltpu.PrefetchScalarGridSpec(
             num_scalar_prefetch=1,
             grid=(PROJ // width,),
             in_specs=[pl.BlockSpec(part.shape, lambda i, s: (0, 0)), pl.BlockSpec(memory_space=pl.ANY)],
-            out_specs=pl.BlockSpec((devices * tiles, 128), lambda i, s: (0, 0)),
+            out_specs=[pl.BlockSpec((devices * tiles, 128), lambda i, s: (0, 0)), TOKEN_BLOCK],
             scratch_shapes=[
                 pltpu.VMEM((devices, length), jnp.bfloat16),
                 pltpu.VMEM((max(devices * chunk_rows, 8), 128), jnp.float32),
                 pltpu.VMEM((devices * tiles, 128), jnp.float32),
             ],
         ),
-        out_shape=jax.ShapeDtypeStruct((devices * tiles, 128), jnp.bfloat16),
+        out_shape=[jax.ShapeDtypeStruct((devices * tiles, 128), jnp.bfloat16), TOKEN],
         cost_estimate=DEAR,
-    )(info, part, after).reshape(devices, tiles, 128)
+        compiler_params=pltpu.CompilerParams(vmem_limit_bytes=VMEM_BYTES),
+    )(info, part, after)
+    return feats.reshape(devices, tiles, 128), token
 
 
 def wrap32(value):
@@ -390,29 +423,30 @@
     if chunk_rows:
         received = received.reshape(devices * chunk_rows, 128)
 
-    result = own_columns(info, upstream, value_weight, adapter_in_t, adapter_out, groups * columns, flat)
+    result, token = own_columns(info, upstream, value_weight, adapter_in_t, adapter_out, groups * columns, flat)
 
     near = [s for s in shifts if s in (1, groups - 1)]
     batches = [near] + [[s] for s in shifts if s not in near]
-    pairs = plane_pairs(plane, adapter_out, result)
-    after, sent, feats = [pairs], [], None
+    pairs = plane_pairs(plane, adapter_out, token)
+    after, sent, feats = pairs, [], None
+    slices = {s: (weights[s], across(weights[s], 1)) for s in shifts}
     for batch in batches:
-        pieces = piece_columns(
+        pieces, token = piece_columns(
             info,
             batch,
             plane,
-            [(weights[s], across(weights[s], 1)) for s in batch],
+            [slices[s] for s in batch],
             adapter_in_t,
             pairs,
             after,
+            CHEAP,
         )
-        sent.append((batch, [across(p, 2 * k) if k else p for k, p in enumerate(pieces)]))
-        after = [p for k, p in enumerate(sent[-1][1]) if k]
+        sent.append((batch, [across(p, 2 * k) for k, p in enumerate(pieces, 1)]))
         if feats is None:
-            feats = project(
-                info, received, wrap32(-1640531535 * rank), pieces[0], devices, length, chunk_rows
+            feats, token = project(
+                info, received, wrap32(-1640531535 * rank), token, devices, length, chunk_rows
             )
-            after.append(feats)
+            after = token
     parts = lax.all_to_all(feats, both, split_axis=0, concat_axis=0, tiled=True)
     raw = jnp.sum(parts[:, : PROJ // 128].astype(jnp.float32), axis=0)
     features = (raw * lax.rsqrt(jnp.mean(raw * raw) + 1e-06)).reshape(1, PROJ)
@@ -428,7 +462,20 @@
     mean_grad = totals.reshape(rank, share).T.reshape(-1)
 
     for index, (batch, pieces) in enumerate(sent):
-        result = place_columns(info, batch, pieces, result, features, index == len(sent) - 1)
+        first, last = index == 0, index == len(sent) - 1
+        result = place_columns(
+            info,
+            batch,
+            pieces,
+            result,
+            features if last else token,
+            CHEAP if last else DEAR,
+            shifts if first else [],
+            upstream,
+            slices,
+            adapter_in_t,
+            pairs,
+        )
     return (result, features, mean_grad)
 
 

time: 96.5 us -> 86.6 us (0.90)
  Pallas kernels: 46.4 us -> 34.2 us
  local copies, waits for them, and re-layouts: 8.47 us -> 10.5 us
    pallas_call x5, Pallas kernels: 20.4 us -> 13.5 us  [the longest x2 6.94 us: piece_columns(): pl.pallas_call(functools.partial(piece_kernel, shifts, chips), in_specs=[...]
    ppermute x12, waiting for transfers between devices: 9.69 us -> 5.81 us  [across(): return lax.ppermute(array, 'grp', [(i, i ^ mask) for i in range(members)])]
    pallas_call x1, Pallas kernels: 15.3 us -> 11.8 us  [project(): pl.pallas_call(functools.partial(project_kernel, stride, 256, width, chun...]
    pallas_call x1, Pallas kernels: 5.42 us -> 3.59 us  [own_columns(): pl.pallas_call(own_kernel, grid_spec=pltpu.PrefetchScalarGridSpec(num_sca...]
    unnamed x28 -> x29, local copies, waits for them, and re-layouts: 4.38 us -> 6.04 us
    ppermute x3, waiting for transfers between devices: 3.31 us -> 4.95 us  [along(): lax.ppermute(array, 'fsdp', [(i, (i + shift) % groups) for i in range(gro...]
    all_to_all x1, waiting for transfers between devices: 0.01 us -> 1.48 us  [per_device(): lax.all_to_all(chunks, both, split_axis=0, concat_axis=0, tiled=True)]
  transfers between devices with their start and end apart: 17 -> 17, of which waited for: 5 -> 8; matrix products, arithmetic and copies ran while one was open for 4% -> 5% of each run, Pallas kernels for 45% -> 37%
where the time goes in v5:
time: 86.6 us; the launch traced here: 86 us
  Pallas kernels  34.2 us (39%)
  starting transfers between devices  24.5 us (28%)
  waiting for transfers between devices  12.8 us (15%)
  local copies, waits for them, and re-layouts  10.5 us (12%)
  between operations  2.39 us (3%)
  other arithmetic  1.63 us (2%)
    pallas_call x1, Pallas kernels, project(): pl.pallas_call(functools.partial(project_kernel, stride, 256, width, chun...  11.8 us
    ppermute x12, starting transfers between devices, across(): return lax.ppermute(array, 'grp', [(i, i ^ mask) for i in range(members)])  10.7 us
    pallas_call x2, Pallas kernels, piece_columns(): pl.pallas_call(functools.partial(piece_kernel, shifts, chips), in_specs=[...  6.94 us
    ppermute x3, starting transfers between devices, along(): lax.ppermute(array, 'fsdp', [(i, (i + shift) % groups) for i in range(gro...  6.09 us
    unnamed x29, local copies, waits for them, and re-layouts  6.04 us
    ppermute x12, waiting for transfers between devices, across(): return lax.ppermute(array, 'grp', [(i, i ^ mask) for i in range(members)])  5.81 us
    pallas_call x2, Pallas kernels, place_columns(): pl.pallas_call(functools.partial(place_kernel, shifts, chips, mine), in_s...  5.8 us
    pallas_call x1, Pallas kernels, pair_gradient(): pl.pallas_call(functools.partial(flat_kernel, rank, groups, chunk_rows),...  5.31 us
  transfers between devices with their start and end apart: 17, of which 8 were waited for; matrix products, arithmetic and copies ran while one was open for 5% of the time, Pallas kernels for 37%

profile of v5, /device:TPU:0, one launch (start us, length us, event | category | flops | bytes accessed | tf_op | source)
XLA Modules:
  0.0 86.0 jit_solution(1206629508303411221)
XLA Ops:
  0.7 1.9 %constant_dynamic-slice_fusion = bf16[256,1024]{1,0:T(8,128)(2,1)} fusion(bf16[2048,1024]{1,0:T(8,128)(2,1)} %weight_ref.1, s32[]{:T(128)S(6)} %select_n.18), kind=kLoop, calls=%fused_computation.5 | loop fusion | bytes 1048580 | tf_op jit(solution)/shard_map/dynamic_slice | solution.py:392
  2.6 3.0 %collective-permute-start.3 = (bf16[256,1024]{1,0:T(8,128)(2,1)}, bf16[256,1024]{1,0:T(8,128)(2,1)S(1)}, u32[]{:S(2)}, u32[]{:S(2)}) collective-permute-start(bf16[256,1024]{1,0:T(8,128)(2,1)} %constant_dynamic-slice_fusion), channel_id=1, source_target_pairs={{0,1},{1,2},{2,3},{3,0},{4,5},{5,6},{6,7},{7,4},{8,9},{9,10},{10,1... | collective-permute-start | bytes 1572872 | tf_op jit(solution)/shard_map/ppermute | solution.py:387
  5.6 2.0 %collective-permute-start.7 = (bf16[256,1024]{1,0:T(8,128)(2,1)}, bf16[256,1024]{1,0:T(8,128)(2,1)S(1)}, u32[]{:S(2)}, u32[]{:S(2)}) collective-permute-start(bf16[256,1024]{1,0:T(8,128)(2,1)} %constant_dynamic-slice_fusion), channel_id=1, source_target_pairs={{0,3},{1,0},{2,1},{3,2},{4,7},{5,4},{6,5},{7,6},{8,11},{9,8},{10,9... | collective-permute-start | bytes 1572872 | tf_op jit(solution)/shard_map/ppermute | solution.py:387
  7.7 2.7 %collective-permute-start.2 = (bf16[256,1024]{1,0:T(8,128)(2,1)}, bf16[256,1024]{1,0:T(8,128)(2,1)S(1)}, u32[]{:S(2)}, u32[]{:S(2)}) collective-permute-start(bf16[256,1024]{1,0:T(8,128)(2,1)} %refs_3_.1), channel_id=1, source_target_pairs={{0,24},{4,28},{8,16},{12,20},{16,8},{20,12},{24,0},{28,4},{1,25},{... | collective-permute-start | bytes 1572872 | tf_op jit(solution)/shard_map/ppermute | solution.py:390
  11.2 5.3 %shard_map.85.after_ref = bf16[768,128]{1,0:T(8,128)(2,1)} custom-call(bf16[256,8192]{1,0:T(8,128)(2,1)} %in_ref.1, bf16[256,1024]{1,0:T(8,128)(2,1)} %refs_3_.1, bf16[8,8192]{1,0:T(8,128)(2,1)} %bitcast.24, bf16[8,1024]{1,0:T(8,128)(2,1)} %refs_4_.1), custom_call_target="tpu_custom_call" | custom-call | tf_op jit(solution)/shard_map/pallas_call | solution.py:292
  16.5 4.4 %all-to-all-start = ((bf16[32,24,128]{2,1,0:T(8,128)(2,1)}), bf16[32,24,128]{2,1,0:T(8,128)(2,1)}, u32[]{:S(2)}, u32[]{:S(2)}) async-start(bf16[32,24,128]{2,1,0:T(8,128)(2,1)} %bitcast.29), calls=%async_computation | async-start | bytes 393216 | tf_op jit(solution)/shard_map/all_to_all | solution.py:422
  21.7 2.2 %copy-done = bf16[2048,1024]{1,0:T(8,128)(2,1)S(1)} copy-done((bf16[2048,1024]{1,0:T(8,128)(2,1)S(1)}, bf16[2048,1024]{1,0:T(8,128)(2,1)}, u32[]{:S(2)}) %copy-start) | copy-done | bytes 4194328
  24.8 3.6 %shard_map.86 = (bf16[256,8192]{1,0:T(8,128)(2,1)}, f32[8,128]{1,0:T(8,128)S(1)}) custom-call(s32[8]{0:T(128)S(1)} %stack.35.info_ref, bf16[256,1024]{1,0:T(8,128)(2,1)S(1)} %copy-done.1, bf16[2048,1024]{1,0:T(8,128)(2,1)S(1)} %copy-done, bf16[8,8192]{1,0:T(8,128)(2,1)S(1)} %bitcast.25, bf16[8,1024]{1,0:T(8,128)(2,1)S(1)} %copy-done.9, ...), custom_call_target="tpu_custom_call" | custom-call | tf_op jit(solution)/shard_map/pallas_call | solution.py:73
  28.6 2.6 %collective-permute-done.7.refs_5_.refs_6_ = bf16[256,1024]{1,0:T(8,128)(2,1)S(1)} collective-permute-done((bf16[256,1024]{1,0:T(8,128)(2,1)}, bf16[256,1024]{1,0:T(8,128)(2,1)S(1)}, u32[]{:S(2)}, u32[]{:S(2)}) %collective-permute-start.7) | collective-permute-done | bytes 524320 | tf_op jit(solution)/shard_map/ppermute | solution.py:387
  32.2 2.6 %collective-permute-done.1.refs_2_.refs_1_ = bf16[256,1024]{1,0:T(8,128)(2,1)S(1)} collective-permute-done((bf16[256,1024]{1,0:T(8,128)(2,1)}, bf16[256,1024]{1,0:T(8,128)(2,1)S(1)}, u32[]{:S(2)}, u32[]{:S(2)}) %collective-permute-start.1) | collective-permute-done | bytes 524320 | tf_op jit(solution)/shard_map/ppermute | solution.py:390
  36.0 3.8 %shard_map.88 = (bf16[256,1024]{1,0:T(8,128)(2,1)}, bf16[256,1024]{1,0:T(8,128)(2,1)}, bf16[256,1024]{1,0:T(8,128)(2,1)}, f32[8,128]{1,0:T(8,128)S(1)}) custom-call(s32[8]{0:T(128)S(1)} %copy-done.12, bf16[256,1024]{1,0:T(8,128)(2,1)S(1)} %collective-permute-done.refs_1_.refs_0_, bf16[256,1024]{1,0:T(8,128)(2,1)S(1)} %collective-permute-done.1.refs_2_.refs_1_, ...), custom_call_target="tpu_custom_call" | custom-call | tf_op jit(solution)/shard_map/pallas_call | solution.py:166
  39.8 1.5 %collective-permute-start.12 = (bf16[256,1024]{1,0:T(8,128)(2,1)}, bf16[256,1024]{1,0:T(8,128)(2,1)}, u32[]{:S(2)}, u32[]{:S(2)}) collective-permute-start(bf16[256,1024]{1,0:T(8,128)(2,1)} %get-tuple-element.21), channel_id=1, source_target_pairs={{0,8},{4,12},{8,0},{12,4},{16,24},{20,28},{24,16},{28,20},{1,9},{5... | collective-permute-start | bytes 1572872 | tf_op jit(solution)/shard_map/ppermute | solution.py:390
  41.9 1.3 %collective-permute-start.14 = (bf16[256,1024]{1,0:T(8,128)(2,1)}, bf16[256,1024]{1,0:T(8,128)(2,1)}, u32[]{:S(2)}, u32[]{:S(2)}) collective-permute-start(bf16[256,1024]{1,0:T(8,128)(2,1)} %get-tuple-element.23), channel_id=1, source_target_pairs={{0,24},{4,28},{8,16},{12,20},{16,8},{20,12},{24,0},{28,4},{1,25},{... | collective-permute-start | bytes 1572872 | tf_op jit(solution)/shard_map/ppermute | solution.py:390
  43.2 2.4 %collective-permute-done.4.refs_3_.refs_8_ = bf16[256,1024]{1,0:T(8,128)(2,1)} collective-permute-done((bf16[256,1024]{1,0:T(8,128)(2,1)S(1)}, bf16[256,1024]{1,0:T(8,128)(2,1)}, u32[]{:S(2)}, u32[]{:S(2)}) %collective-permute-start.4) | collective-permute-done | bytes 524320 | tf_op jit(solution)/shard_map/ppermute | solution.py:387
  45.6 1.5 %all-to-all-done = bf16[32,24,128]{2,1,0:T(8,128)(2,1)} async-done(((bf16[32,24,128]{2,1,0:T(8,128)(2,1)}), bf16[32,24,128]{2,1,0:T(8,128)(2,1)}, u32[]{:S(2)}, u32[]{:S(2)}) %all-to-all-start) | async-done | bytes 196640 | tf_op jit(solution)/shard_map/all_to_all | solution.py:422
  47.1 11.8 %shard_map.89 = (bf16[1792,128]{1,0:T(8,128)(2,1)S(1)}, f32[8,128]{1,0:T(8,128)S(1)}) custom-call(s32[8]{0:T(128)S(1)} %copy-done.13, bf16[768,128]{1,0:T(8,128)(2,1)} %bitcast.11.part_ref, f32[8,128]{1,0:T(8,128)S(1)} %get-tuple-element.16.after_ref), custom_call_target="tpu_custom_call" | custom-call | flops 99999997952 | tf_op jit(solution)/shard_map/pallas_call | solution.py:352
  59.7 3.3 %all-to-all-start.1 = ((bf16[32,56,128]{2,1,0:T(8,128)(2,1)}), bf16[32,56,128]{2,1,0:T(8,128)(2,1)}, u32[]{:S(2)}, u32[]{:S(2)}) async-start(bf16[32,56,128]{2,1,0:T(8,128)(2,1)} %bitcast.30), calls=%async_computation.1 | async-start | bytes 917504 | tf_op jit(solution)/shard_map/all_to_all | solution.py:450
  63.0 3.1 %shard_map.90 = (bf16[256,512]{1,0:T(8,128)(2,1)}, bf16[256,512]{1,0:T(8,128)(2,1)}, bf16[256,512]{1,0:T(8,128)(2,1)}, f32[8,128]{1,0:T(8,128)S(1)}) custom-call(s32[8]{0:T(128)S(1)} %copy-done.13, bf16[256,1024]{1,0:T(8,128)(2,1)S(1)} %collective-permute-done.refs_1_.refs_0_, bf16[256,1024]{1,0:T(8,128)(2,1)S(1)} %collective-permute-done.1.refs_2_.refs_1_, ...), custom_call_target="tpu_custom_call" | custom-call | tf_op jit(solution)/shard_map/pallas_call | solution.py:166
  66.2 1.6 %collective-permute-start.9 = (bf16[256,512]{1,0:T(8,128)(2,1)}, bf16[256,512]{1,0:T(8,128)(2,1)}, u32[]{:S(2)}, u32[]{:S(2)}) collective-permute-start(bf16[256,512]{1,0:T(8,128)(2,1)} %get-tuple-element.18), channel_id=1, source_target_pairs={{0,8},{4,12},{8,0},{12,4},{16,24},{20,28},{24,16},{28,20},{1,9},{5... | collective-permute-start | bytes 786440 | tf_op jit(solution)/shard_map/ppermute | solution.py:390
  67.8 1.5 %collective-permute-start.10 = (bf16[256,512]{1,0:T(8,128)(2,1)}, bf16[256,512]{1,0:T(8,128)(2,1)}, u32[]{:S(2)}, u32[]{:S(2)}) collective-permute-start(bf16[256,512]{1,0:T(8,128)(2,1)} %get-tuple-element.19), channel_id=1, source_target_pairs={{0,16},{4,20},{8,24},{12,28},{16,0},{20,4},{24,8},{28,12},{1,17},{... | collective-permute-start | bytes 786440 | tf_op jit(solution)/shard_map/ppermute | solution.py:390
  71.8 3.8 %shard_map.91.refs_3_ = bf16[256,8192]{1,0:T(8,128)(2,1)} custom-call(s32[8]{0:T(128)S(1)} %copy-done.13, bf16[256,1024]{1,0:T(8,128)(2,1)} %collective-permute-done.12.refs_0_, bf16[256,1024]{1,0:T(8,128)(2,1)} %collective-permute-done.13.refs_1_, bf16[256,1024]{1,0:T(8,128)(2,1)} %collective-permute-done.14.refs_2_, ...), custom_call_target="tpu_custom_call", output_to_operand_aliasing={{}: (13, {})} | custom-call | flops 99999997952 | tf_op jit(solution)/shard_map/pallas_call | solution.py:235
  81.0 1.4 %collective-permute-done.10.refs_1_ = bf16[256,512]{1,0:T(8,128)(2,1)} collective-permute-done((bf16[256,512]{1,0:T(8,128)(2,1)}, bf16[256,512]{1,0:T(8,128)(2,1)}, u32[]{:S(2)}, u32[]{:S(2)}) %collective-permute-start.10) | collective-permute-done | bytes 262176 | tf_op jit(solution)/shard_map/ppermute | solution.py:390
  82.3 1.5 %collective-permute-done.11.refs_2_ = bf16[256,512]{1,0:T(8,128)(2,1)} collective-permute-done((bf16[256,512]{1,0:T(8,128)(2,1)}, bf16[256,512]{1,0:T(8,128)(2,1)}, u32[]{:S(2)}, u32[]{:S(2)}) %collective-permute-start.11) | collective-permute-done | bytes 262176 | tf_op jit(solution)/shard_map/ppermute | solution.py:390
  83.8 2.0 %shard_map.92 = bf16[256,8192]{1,0:T(8,128)(2,1)} custom-call(s32[8]{0:T(128)S(1)} %copy-done.13, bf16[256,512]{1,0:T(8,128)(2,1)} %collective-permute-done.9.refs_0_, bf16[256,512]{1,0:T(8,128)(2,1)} %collective-permute-done.10.refs_1_, bf16[256,512]{1,0:T(8,128)(2,1)} %collective-permute-done.11.refs_2_, ...), custom_call_target="tpu_custom_call", output_to_operand_aliasing={{}: (4, {})} | custom-call | tf_op jit(solution)/shard_map/pallas_call | solution.py:235
  (56 shorter events, 12.8 us)
Async XLA Ops:
  0.6 21.0 %copy-start.1 = (bf16[256,1024]{1,0:T(8,128)(2,1)S(1)}, bf16[256,1024]{1,0:T(8,128)(2,1)}, u32[]{:S(2)}) copy-start(bf16[256,1024]{1,0:T(8,128)(2,1)} %refs_3_.1) | copy-start | bytes 1572868
  0.6 21.0 %copy-start.9 = (bf16[8,1024]{1,0:T(8,128)(2,1)S(1)}, bf16[8,1024]{1,0:T(8,128)(2,1)}, u32[]{:S(2)}) copy-start(bf16[8,1024]{1,0:T(8,128)(2,1)} %refs_4_.1) | copy-start | bytes 49156
  0.7 21.0 %copy-start.2 = (bf16[8192,8]{0,1:T(8,128)(2,1)S(1)}, bf16[8192,8]{0,1:T(8,128)(2,1)}, u32[]{:S(2)}) copy-start(bf16[8192,8]{0,1:T(8,128)(2,1)} %param.9) | copy-start | bytes 393220
  2.6 25.7 %collective-permute-start.3 = (bf16[256,1024]{1,0:T(8,128)(2,1)}, bf16[256,1024]{1,0:T(8,128)(2,1)S(1)}, u32[]{:S(2)}, u32[]{:S(2)}) collective-permute-start(bf16[256,1024]{1,0:T(8,128)(2,1)} %constant_dynamic-slice_fusion), channel_id=1, source_target_pairs={{0,1},{1,2},{2,3},{3,0},{4,5},{5,6},{6,7},{7,4},{8,9},{9,10},{10,1... | collective-permute-start | bytes 1572872 | tf_op jit(solution)/shard_map/ppermute | solution.py:387
  5.6 25.5 %collective-permute-start.7 = (bf16[256,1024]{1,0:T(8,128)(2,1)}, bf16[256,1024]{1,0:T(8,128)(2,1)S(1)}, u32[]{:S(2)}, u32[]{:S(2)}) collective-permute-start(bf16[256,1024]{1,0:T(8,128)(2,1)} %constant_dynamic-slice_fusion), channel_id=1, source_target_pairs={{0,3},{1,0},{2,1},{3,2},{4,7},{5,4},{6,5},{7,6},{8,11},{9,8},{10,9... | collective-permute-start | bytes 1572872 | tf_op jit(solution)/shard_map/ppermute | solution.py:387
  7.7 24.5 %collective-permute-start.2 = (bf16[256,1024]{1,0:T(8,128)(2,1)}, bf16[256,1024]{1,0:T(8,128)(2,1)S(1)}, u32[]{:S(2)}, u32[]{:S(2)}) collective-permute-start(bf16[256,1024]{1,0:T(8,128)(2,1)} %refs_3_.1), channel_id=1, source_target_pairs={{0,24},{4,28},{8,16},{12,20},{16,8},{20,12},{24,0},{28,4},{1,25},{... | collective-permute-start | bytes 1572872 | tf_op jit(solution)/shard_map/ppermute | solution.py:390
  10.3 24.5 %collective-permute-start.1 = (bf16[256,1024]{1,0:T(8,128)(2,1)}, bf16[256,1024]{1,0:T(8,128)(2,1)S(1)}, u32[]{:S(2)}, u32[]{:S(2)}) collective-permute-start(bf16[256,1024]{1,0:T(8,128)(2,1)} %refs_3_.1), channel_id=1, source_target_pairs={{0,16},{4,20},{8,24},{12,28},{16,0},{20,4},{24,8},{28,12},{1,17},{... | collective-permute-start | bytes 1572872 | tf_op jit(solution)/shard_map/ppermute | solution.py:390
  10.8 24.3 %collective-permute-start = (bf16[256,1024]{1,0:T(8,128)(2,1)}, bf16[256,1024]{1,0:T(8,128)(2,1)S(1)}, u32[]{:S(2)}, u32[]{:S(2)}) collective-permute-start(bf16[256,1024]{1,0:T(8,128)(2,1)} %refs_3_.1), channel_id=1, source_target_pairs={{0,8},{4,12},{8,0},{12,4},{16,24},{20,28},{24,16},{28,20},{1,9},{5... | collective-permute-start | bytes 1572872 | tf_op jit(solution)/shard_map/ppermute | solution.py:390
  16.5 30.6 %all-to-all-start = ((bf16[32,24,128]{2,1,0:T(8,128)(2,1)}), bf16[32,24,128]{2,1,0:T(8,128)(2,1)}, u32[]{:S(2)}, u32[]{:S(2)}) async-start(bf16[32,24,128]{2,1,0:T(8,128)(2,1)} %bitcast.29), calls=%async_computation | async-start | bytes 393216 | tf_op jit(solution)/shard_map/all_to_all | solution.py:422
  24.8 10.4 %copy-start.11 = (s32[8]{0:T(128)}, s32[8]{0:T(128)S(1)}, u32[]{:S(2)}) copy-start(s32[8]{0:T(128)S(1)} %stack.35.info_ref) | copy-start | bytes 100
  28.4 7.6 %collective-permute-start.6 = (bf16[256,1024]{1,0:T(8,128)(2,1)S(1)}, bf16[256,1024]{1,0:T(8,128)(2,1)S(1)}, u32[]{:S(2)}, u32[]{:S(2)}) collective-permute-start(bf16[256,1024]{1,0:T(8,128)(2,1)S(1)} %collective-permute-done.3.refs_3_.refs_4_), channel_id=1, source_target_pairs={{0,4},{4,0},{8,12},{12,8},{16,20},{20,16},{24,28},{28,24},{1,5},{5... | collective-permute-start | bytes 1572872 | tf_op jit(solution)/shard_map/ppermute | solution.py:390
  31.1 14.5 %collective-permute-start.4 = (bf16[256,1024]{1,0:T(8,128)(2,1)S(1)}, bf16[256,1024]{1,0:T(8,128)(2,1)}, u32[]{:S(2)}, u32[]{:S(2)}) collective-permute-start(bf16[256,1024]{1,0:T(8,128)(2,1)S(1)} %collective-permute-done.3.refs_3_.refs_4_), channel_id=1, source_target_pairs={{0,1},{1,2},{2,3},{3,0},{4,5},{5,6},{6,7},{7,4},{8,9},{9,10},{10,1... | collective-permute-start | bytes 1572872 | tf_op jit(solution)/shard_map/ppermute | solution.py:387
  32.2 3.7 %collective-permute-start.8 = (bf16[256,1024]{1,0:T(8,128)(2,1)S(1)}, bf16[256,1024]{1,0:T(8,128)(2,1)S(1)}, u32[]{:S(2)}, u32[]{:S(2)}) collective-permute-start(bf16[256,1024]{1,0:T(8,128)(2,1)S(1)} %collective-permute-done.7.refs_5_.refs_6_), channel_id=1, source_target_pairs={{0,4},{4,0},{8,12},{12,8},{16,20},{20,16},{24,28},{28,24},{1,5},{5... | collective-permute-start | bytes 1572872 | tf_op jit(solution)/shard_map/ppermute | solution.py:390
  35.9 11.2 %copy-start.13 = (s32[8]{0:T(128)S(1)}, s32[8]{0:T(128)}, u32[]{:S(2)}) copy-start(s32[8]{0:T(128)} %copy-done.11) | copy-start | bytes 100
  35.9 9.7 %copy-start.6 = (bf16[256,1024]{1,0:T(8,128)(2,1)}, bf16[256,1024]{1,0:T(8,128)(2,1)S(1)}, u32[]{:S(2)}) copy-start(bf16[256,1024]{1,0:T(8,128)(2,1)S(1)} %collective-permute-done.8.refs_6_.refs_7_) | copy-start | bytes 1572868
  35.9 9.7 %copy-start.4 = (bf16[256,1024]{1,0:T(8,128)(2,1)}, bf16[256,1024]{1,0:T(8,128)(2,1)S(1)}, u32[]{:S(2)}) copy-start(bf16[256,1024]{1,0:T(8,128)(2,1)S(1)} %collective-permute-done.6.refs_4_.refs_5_) | copy-start | bytes 1572868
  39.8 29.5 %collective-permute-start.12 = (bf16[256,1024]{1,0:T(8,128)(2,1)}, bf16[256,1024]{1,0:T(8,128)(2,1)}, u32[]{:S(2)}, u32[]{:S(2)}) collective-permute-start(bf16[256,1024]{1,0:T(8,128)(2,1)} %get-tuple-element.21), channel_id=1, source_target_pairs={{0,8},{4,12},{8,0},{12,4},{16,24},{20,28},{24,16},{28,20},{1,9},{5... | collective-permute-start | bytes 1572872 | tf_op jit(solution)/shard_map/ppermute | solution.py:390
  41.3 28.4 %collective-permute-start.13 = (bf16[256,1024]{1,0:T(8,128)(2,1)}, bf16[256,1024]{1,0:T(8,128)(2,1)}, u32[]{:S(2)}, u32[]{:S(2)}) collective-permute-start(bf16[256,1024]{1,0:T(8,128)(2,1)} %get-tuple-element.22), channel_id=1, source_target_pairs={{0,16},{4,20},{8,24},{12,28},{16,0},{20,4},{24,8},{28,12},{1,17},{... | collective-permute-start | bytes 1572872 | tf_op jit(solution)/shard_map/ppermute | solution.py:390
  41.9 27.7 %collective-permute-start.14 = (bf16[256,1024]{1,0:T(8,128)(2,1)}, bf16[256,1024]{1,0:T(8,128)(2,1)}, u32[]{:S(2)}, u32[]{:S(2)}) collective-permute-start(bf16[256,1024]{1,0:T(8,128)(2,1)} %get-tuple-element.23), channel_id=1, source_target_pairs={{0,24},{4,28},{8,16},{12,20},{16,8},{20,12},{24,0},{28,4},{1,25},{... | collective-permute-start | bytes 1572872 | tf_op jit(solution)/shard_map/ppermute | solution.py:390
  45.6 17.4 %collective-permute-start.5 = (bf16[256,1024]{1,0:T(8,128)(2,1)}, bf16[256,1024]{1,0:T(8,128)(2,1)}, u32[]{:S(2)}, u32[]{:S(2)}) collective-permute-start(bf16[256,1024]{1,0:T(8,128)(2,1)} %collective-permute-done.4.refs_3_.refs_8_), channel_id=1, source_target_pairs={{0,4},{4,0},{8,12},{12,8},{16,20},{20,16},{24,28},{28,24},{1,5},{5... | collective-permute-start | bytes 1572872 | tf_op jit(solution)/shard_map/ppermute | solution.py:390
  59.7 16.4 %all-to-all-start.1 = ((bf16[32,56,128]{2,1,0:T(8,128)(2,1)}), bf16[32,56,128]{2,1,0:T(8,128)(2,1)}, u32[]{:S(2)}, u32[]{:S(2)}) async-start(bf16[32,56,128]{2,1,0:T(8,128)(2,1)} %bitcast.30), calls=%async_computation.1 | async-start | bytes 917504 | tf_op jit(solution)/shard_map/all_to_all | solution.py:450
  66.2 14.8 %collective-permute-start.9 = (bf16[256,512]{1,0:T(8,128)(2,1)}, bf16[256,512]{1,0:T(8,128)(2,1)}, u32[]{:S(2)}, u32[]{:S(2)}) collective-permute-start(bf16[256,512]{1,0:T(8,128)(2,1)} %get-tuple-element.18), channel_id=1, source_target_pairs={{0,8},{4,12},{8,0},{12,4},{16,24},{20,28},{24,16},{28,20},{1,9},{5... | collective-permute-start | bytes 786440 | tf_op jit(solution)/shard_map/ppermute | solution.py:390
  67.8 14.6 %collective-permute-start.10 = (bf16[256,512]{1,0:T(8,128)(2,1)}, bf16[256,512]{1,0:T(8,128)(2,1)}, u32[]{:S(2)}, u32[]{:S(2)}) collective-permute-start(bf16[256,512]{1,0:T(8,128)(2,1)} %get-tuple-element.19), channel_id=1, source_target_pairs={{0,16},{4,20},{8,24},{12,28},{16,0},{20,4},{24,8},{28,12},{1,17},{... | collective-permute-start | bytes 786440 | tf_op jit(solution)/shard_map/ppermute | solution.py:390
  69.3 14.6 %collective-permute-start.11 = (bf16[256,512]{1,0:T(8,128)(2,1)}, bf16[256,512]{1,0:T(8,128)(2,1)}, u32[]{:S(2)}, u32[]{:S(2)}) collective-permute-start(bf16[256,512]{1,0:T(8,128)(2,1)} %get-tuple-element.20), channel_id=1, source_target_pairs={{0,24},{4,28},{8,16},{12,20},{16,8},{20,12},{24,0},{28,4},{1,25},{... | collective-permute-start | bytes 786440 | tf_op jit(solution)/shard_map/ppermute | solution.py:390
  (7 other events, 11.7 us)

commit v6 on v5

--- a/solution.py
+++ b/solution.py
@@ -13,7 +13,7 @@
 
 CHEAP = pl.CostEstimate(flops=0, bytes_accessed=0, transcendentals=0)
 VMEM_BYTES = 24 * 2**20
-MEMBER, PLACE, CHIP, START, SHARDS = range(5)
+MEMBER, PLACE, CHIP, SHARDS = range(4)
 DEAR = pl.CostEstimate(flops=10**11, bytes_accessed=0, transcendentals=0)
 
 
@@ -50,6 +50,29 @@
 
 def twice(part):
     return jnp.concatenate([part, part], axis=0)
+
+
+def here(groups):
+    member, place = lax.axis_index("grp"), lax.axis_index("fsdp")
+    return [member, place, lax.div(member, 2)] + [lax.rem(place + groups - s, groups) for s in range(groups)]
+
+
+def slice_kernel(width, weight_ref, out_ref, sem):
+    at = pl.multiple_of(lax.axis_index("grp") * width, width)
+    copy = pltpu.make_async_copy(weight_ref.at[pl.ds(at, width)], out_ref, sem)
+    copy.start()
+    copy.wait()
+
+
+def member_slice(weight, width):
+    return pl.pallas_call(
+        functools.partial(slice_kernel, width),
+        in_specs=[ANYWHERE],
+        out_specs=IN_VMEM,
+        out_shape=jax.ShapeDtypeStruct((width, weight.shape[1]), weight.dtype),
+        scratch_shapes=[pltpu.SemaphoreType.DMA],
+        cost_estimate=CHEAP,
+    )(weight)
 
 
 def own_kernel(info_ref, up_ref, weight_ref, in_adapter_ref, out_adapter_ref, after_ref, out_ref, token_ref, pair_ref, turned_ref):
@@ -78,11 +101,11 @@
             in_specs=[
                 pl.BlockSpec((tokens, depth), lambda i, s: (0, 0)),
                 pl.BlockSpec((block, depth), lambda i, s: (i, 0)),
-                pl.BlockSpec((rank, block), lambda i, s: (0, s[PLACE] * steps + i)),
+                pl.BlockSpec((rank, block), lambda i, s: (0, s[0] * steps + i)),
                 pl.BlockSpec(adapter_out.shape, lambda i, s: (0, 0)),
                 pl.BlockSpec(memory_space=pl.ANY),
             ],
-            out_specs=[pl.BlockSpec((tokens, block), lambda i, s: (0, s[PLACE] * steps + i)), TOKEN_BLOCK],
+            out_specs=[pl.BlockSpec((tokens, block), lambda i, s: (0, s[0] * steps + i)), TOKEN_BLOCK],
             scratch_shapes=[
                 pltpu.VMEM((tokens, 2 * rank), jnp.bfloat16),
                 pltpu.VMEM((depth, tokens), jnp.bfloat16),
@@ -91,7 +114,7 @@
         out_shape=[jax.ShapeDtypeStruct((tokens, all_columns), jnp.bfloat16), TOKEN],
         cost_estimate=CHEAP,
         compiler_params=pltpu.CompilerParams(vmem_limit_bytes=VMEM_BYTES),
-    )(info, upstream, weight, adapter_in_t, adapter_out, after)
+    )(info[PLACE].reshape(1), upstream, weight, adapter_in_t, adapter_out, after)
 
 
 def pair_kernel(chips, *refs):
@@ -121,7 +144,8 @@
     return at, total.astype(jnp.bfloat16)
 
 
-def piece_kernel(shifts, chips, info_ref, *refs):
+def piece_kernel(shifts, chips, groups, *refs):
+    info_ref = here(groups)
     others = chips - 1
     token_refs, refs = refs[:others], refs[others:]
     weight_refs, refs = refs[: 2 * len(shifts)], refs[2 * len(shifts) :]
@@ -164,17 +188,18 @@
     count = len(weights)
     out_shape = jax.ShapeDtypeStruct((tokens, count * 2 * width), jnp.bfloat16)
     outs = pl.pallas_call(
-        functools.partial(piece_kernel, shifts, chips),
-        in_specs=[IN_SMEM] + [IN_VMEM] * (chips - 1 + 2 * count + 2) + [ANYWHERE],
+        functools.partial(piece_kernel, shifts, chips, lax.axis_size("fsdp")),
+        in_specs=[IN_VMEM] * (chips - 1 + 2 * count + 2) + [ANYWHERE],
         out_specs=[IN_VMEM] * chips,
         out_shape=[out_shape] * (chips - 1) + [TOKEN],
         cost_estimate=cost,
         compiler_params=pltpu.CompilerParams(vmem_limit_bytes=VMEM_BYTES),
-    )(info, *plane[1:], *[w for pair in weights for w in pair], adapter_in_t, pairs, after)
+    )(*plane[1:], *[w for pair in weights for w in pair], adapter_in_t, pairs, after)
     return outs[:-1], outs[-1]
 
 
-def place_kernel(shifts, chips, mine, info_ref, *refs):
+def place_kernel(shifts, chips, mine, groups, *refs):
+    info_ref = here(groups)
     piece_refs, refs = refs[: chips - 1], refs[chips - 1 :]
     if mine:
         up_ref, refs = refs[0], refs[1:]
@@ -231,10 +256,10 @@
     extra = []
     if mine:
         extra = [upstream] + [w for shift in mine for w in weights[shift]] + [adapter_in_t, pairs]
-    operands = [info, *pieces, *extra, buffer, after]
+    operands = [*pieces, *extra, buffer, after]
     return pl.pallas_call(
-        functools.partial(place_kernel, shifts, chips, mine),
-        in_specs=[IN_SMEM] + [IN_VMEM] * (len(operands) - 3) + [ANYWHERE] * 2,
+        functools.partial(place_kernel, shifts, chips, mine, lax.axis_size("fsdp")),
+        in_specs=[IN_VMEM] * (len(operands) - 2) + [ANYWHERE] * 2,
         out_specs=ANYWHERE,
         out_shape=jax.ShapeDtypeStruct(buffer.shape, buffer.dtype),
         scratch_shapes=[pltpu.SemaphoreType.DMA(((chips - 1) * len(shifts) + len(mine),))]
@@ -311,7 +336,7 @@
     )(inputs, upstream, adapter_in_t, adapter_out)
 
 
-def project_kernel(stride, chunk, width, chunk_rows, mean_rows, info_ref, part_ref, after_ref, out_ref, token_ref, wide_ref, line_ref, sum_ref):
+def project_kernel(stride, chunk, width, chunk_rows, mean_rows, first, seed_ref, part_ref, after_ref, out_ref, token_ref, wide_ref, line_ref, sum_ref):
     devices, rows = wide_ref.shape
     tiles = sum_ref.shape[0] // devices
 
@@ -328,13 +353,14 @@
         else:
             wide_ref[...] = part_ref[...]
 
+    start = first() * -1640531535 + seed_ref[0] * 668265263
     columns = pl.program_id(0) * width + lax.broadcasted_iota(jnp.int32, (1, width), 1)
     columns = columns * -2048144789
     total = jnp.zeros((devices, width), jnp.float32)
     for at in range(0, rows, chunk):
         count = min(chunk, rows - at)
         lines = lax.broadcasted_iota(jnp.int32, (count, 1), 0) + at
-        lines = lines * stride + info_ref[START]
+        lines = lines * stride + start
         total += dot(wide_ref[:, at : at + count], hash_signs(lines + columns))
     for tile in range(width // 128):
         at = pl.program_id(0) * (width // 128) + tile
@@ -345,12 +371,12 @@
         out_ref[...] = sum_ref[...].astype(out_ref.dtype)
 
 
-def project(info, part, stride, after, devices, length, chunk_rows):
+def project(seed, first, part, stride, after, devices, length, chunk_rows):
     width = PROJ
     mean_rows = length // 128 if chunk_rows else 0
     tiles = PROJ // 128 + -(-mean_rows // 8) * 8
     feats, token = pl.pallas_call(
-        functools.partial(project_kernel, stride, 256, width, chunk_rows, mean_rows),
+        functools.partial(project_kernel, stride, 256, width, chunk_rows, mean_rows, first),
         grid_spec=pltpu.PrefetchScalarGridSpec(
             num_scalar_prefetch=1,
             grid=(PROJ // width,),
@@ -365,7 +391,7 @@
         out_shape=[jax.ShapeDtypeStruct((devices * tiles, 128), jnp.bfloat16), TOKEN],
         cost_estimate=DEAR,
         compiler_params=pltpu.CompilerParams(vmem_limit_bytes=VMEM_BYTES),
-    )(info, part, after)
+    )(seed, part, after)
     return feats.reshape(devices, tiles, 128), token
 
 
@@ -389,7 +415,7 @@
     def across(array, mask):
         return lax.ppermute(array, "grp", [(i, i ^ mask) for i in range(members)])
 
-    slice_own = lax.dynamic_slice_in_dim(value_weight, member * width, width, 0)
+    slice_own = member_slice(value_weight, width)
     shifts = sorted(range(1, groups), key=lambda s: (min(s, groups - s), s))
     weights = {}
     for s in shifts:
@@ -407,10 +433,13 @@
     length = rank * share // members
     assert members % rank == 0
     split = members // rank
-    row = member // split
-    column = place * share + (member % split) * length
-    start = (column * rank + row) * -1640531535 + sign_seed[0] * 668265263
-    info = jnp.stack([member, place, chip, start] + [lax.rem(place + groups - s, groups) for s in range(groups)])
+    info = here(groups)
+
+    def first_parameter():
+        member, place = here(groups)[:2]
+        row = lax.div(member, split)
+        column = place * share + lax.rem(member, split) * length
+        return column * rank + row
 
     chunk_rows = 0 if length % 128 or split > 1 else -(-length // 1024) * 8
     flat = pair_gradient(inputs, upstream, adapter_in_t, adapter_out, groups, chunk_rows)
@@ -444,7 +473,14 @@
         sent.append((batch, [across(p, 2 * k) for k, p in enumerate(pieces, 1)]))
         if feats is None:
             feats, token = project(
-                info, received, wrap32(-1640531535 * rank), token, devices, length, chunk_rows
+                sign_seed,
+                first_parameter,
+                received,
+                wrap32(-1640531535 * rank),
+                token,
+                devices,
+                length,
+                chunk_rows,
             )
             after = token
     parts = lax.all_to_all(feats, both, split_axis=0, concat_axis=0, tiled=True)

time: 86.6 us -> 85.7 us (0.990)
  local copies, waits for them, and re-layouts: 10.5 us -> 7.71 us
  Pallas kernels: 34.2 us -> 35.8 us
    pallas_call x4 -> x5, Pallas kernels: 12.7 us -> 15.6 us  [the longest x2 7.82 us: piece_columns(): pl.pallas_call(functools.partial(piece_kernel, shifts, chips, lax.axis_si...]
    dynamic_slice x1 -> x0, local copies, waits for them, and re-layouts: 1.95 us -> none  [per_device(): slice_own = lax.dynamic_slice_in_dim(value_weight, member * width, width, 0)]
    ppermute x12, waiting for transfers between devices: 5.81 us -> 6.69 us  [across(): return lax.ppermute(array, 'grp', [(i, i ^ mask) for i in range(members)])]
    unnamed x29 -> x23, local copies, waits for them, and re-layouts: 6.04 us -> 5.24 us
  transfers between devices with their start and end apart: 17 -> 17, of which waited for: 8 -> 8; matrix products, arithmetic and copies ran while one was open for 5% -> 5% of each run, Pallas kernels for 37% -> 38%
where the time goes in v6:
time: 85.7 us; the launch traced here: 85.1 us
  Pallas kernels  35.8 us (42%)
  starting transfers between devices  24.4 us (28%)
  waiting for transfers between devices  13.2 us (15%)
  local copies, waits for them, and re-layouts  7.71 us (9%)
  between operations  2.37 us (3%)
  other arithmetic  1.63 us (2%)
    pallas_call x1, Pallas kernels, project(): pl.pallas_call(functools.partial(project_kernel, stride, 256, width, chun...  11.1 us
    ppermute x12, starting transfers between devices, across(): return lax.ppermute(array, 'grp', [(i, i ^ mask) for i in range(members)])  10.7 us
    pallas_call x2, Pallas kernels, piece_columns(): pl.pallas_call(functools.partial(piece_kernel, shifts, chips, lax.axis_si...  7.82 us
    ppermute x12, waiting for transfers between devices, across(): return lax.ppermute(array, 'grp', [(i, i ^ mask) for i in range(members)])  6.69 us
    ppermute x3, starting transfers between devices, along(): lax.ppermute(array, 'fsdp', [(i, (i + shift) % groups) for i in range(gro...  6.21 us
    pallas_call x2, Pallas kernels, place_columns(): pl.pallas_call(functools.partial(place_kernel, shifts, chips, mine, lax.a...  5.78 us
    pallas_call x1, Pallas kernels, pair_gradient(): pl.pallas_call(functools.partial(flat_kernel, rank, groups, chunk_rows),...  5.31 us
    unnamed x23, local copies, waits for them, and re-layouts  5.24 us
  transfers between devices with their start and end apart: 17, of which 8 were waited for; matrix products, arithmetic and copies ran while one was open for 5% of the time, Pallas kernels for 38%

profile of v6, /device:TPU:0, one launch (start us, length us, event | category | flops | bytes accessed | tf_op | source)
XLA Modules:
  0.0 85.1 jit_solution(6994717439429052961)
XLA Ops:
  0.7 2.0 %shard_map.85 = bf16[256,1024]{1,0:T(8,128)(2,1)} custom-call(bf16[2048,1024]{1,0:T(8,128)(2,1)} %weight_ref.3), custom_call_target="tpu_custom_call" | custom-call | tf_op jit(solution)/shard_map/pallas_call | solution.py:68
  2.6 3.1 %collective-permute-start.3 = (bf16[256,1024]{1,0:T(8,128)(2,1)}, bf16[256,1024]{1,0:T(8,128)(2,1)S(1)}, u32[]{:S(2)}, u32[]{:S(2)}) collective-permute-start(bf16[256,1024]{1,0:T(8,128)(2,1)} %shard_map.85), channel_id=1, source_target_pairs={{0,1},{1,2},{2,3},{3,0},{4,5},{5,6},{6,7},{7,4},{8,9},{9,10},{10,1... | collective-permute-start | bytes 1572872 | tf_op jit(solution)/shard_map/ppermute | solution.py:413
  5.7 2.1 %collective-permute-start.7 = (bf16[256,1024]{1,0:T(8,128)(2,1)}, bf16[256,1024]{1,0:T(8,128)(2,1)}, u32[]{:S(2)}, u32[]{:S(2)}) collective-permute-start(bf16[256,1024]{1,0:T(8,128)(2,1)} %shard_map.85), channel_id=1, source_target_pairs={{0,3},{1,0},{2,1},{3,2},{4,7},{5,4},{6,5},{7,6},{8,11},{9,8},{10,9... | collective-permute-start | bytes 1572872 | tf_op jit(solution)/shard_map/ppermute | solution.py:413
  7.8 2.6 %collective-permute-start.2 = (bf16[256,1024]{1,0:T(8,128)(2,1)S(1)}, bf16[256,1024]{1,0:T(8,128)(2,1)S(1)}, u32[]{:S(2)}, u32[]{:S(2)}) collective-permute-start(bf16[256,1024]{1,0:T(8,128)(2,1)S(1)} %copy-done.1), channel_id=1, source_target_pairs={{0,24},{4,28},{8,16},{12,20},{16,8},{20,12},{24,0},{28,4},{1,25},{... | collective-permute-start | bytes 1572872 | tf_op jit(solution)/shard_map/ppermute | solution.py:416
  11.3 5.3 %shard_map.86.after_ref = bf16[768,128]{1,0:T(8,128)(2,1)} custom-call(bf16[256,8192]{1,0:T(8,128)(2,1)} %in_ref.1, bf16[256,1024]{1,0:T(8,128)(2,1)} %refs_3_.1, bf16[8,8192]{1,0:T(8,128)(2,1)} %bitcast.16, bf16[8,1024]{1,0:T(8,128)(2,1)} %refs_4_.1), custom_call_target="tpu_custom_call" | custom-call | tf_op jit(solution)/shard_map/pallas_call | solution.py:317
  16.6 4.2 %all-to-all-start = ((bf16[32,24,128]{2,1,0:T(8,128)(2,1)}), bf16[32,24,128]{2,1,0:T(8,128)(2,1)S(1)}, u32[]{:S(2)}, u32[]{:S(2)}) async-start(bf16[32,24,128]{2,1,0:T(8,128)(2,1)} %bitcast.21), calls=%async_computation | async-start | bytes 393216 | tf_op jit(solution)/shard_map/all_to_all | solution.py:451
  21.5 2.2 %copy-done = bf16[2048,1024]{1,0:T(8,128)(2,1)S(1)} copy-done((bf16[2048,1024]{1,0:T(8,128)(2,1)S(1)}, bf16[2048,1024]{1,0:T(8,128)(2,1)}, u32[]{:S(2)}) %copy-start) | copy-done | bytes 4194328
  24.6 3.0 %shard_map.87 = (bf16[256,8192]{1,0:T(8,128)(2,1)}, f32[8,128]{1,0:T(8,128)S(1)}) custom-call(s32[1]{0:T(128)} %bitcast.1.info_ref, bf16[256,1024]{1,0:T(8,128)(2,1)S(1)} %copy-done.2, bf16[2048,1024]{1,0:T(8,128)(2,1)S(1)} %copy-done, bf16[8,8192]{1,0:T(8,128)(2,1)S(1)} %bitcast.17, bf16[8,1024]{1,0:T(8,128)(2,1)S(1)} %copy-done.9, ...), custom_call_target="tpu_custom_call" | custom-call | tf_op jit(solution)/shard_map/pallas_call | solution.py:96
  27.9 3.4 %collective-permute-done.7.refs_5_.refs_6_ = bf16[256,1024]{1,0:T(8,128)(2,1)} collective-permute-done((bf16[256,1024]{1,0:T(8,128)(2,1)}, bf16[256,1024]{1,0:T(8,128)(2,1)}, u32[]{:S(2)}, u32[]{:S(2)}) %collective-permute-start.7) | collective-permute-done | bytes 524320 | tf_op jit(solution)/shard_map/ppermute | solution.py:413
  32.4 2.4 %collective-permute-done.1.refs_2_.refs_1_ = bf16[256,1024]{1,0:T(8,128)(2,1)S(1)} collective-permute-done((bf16[256,1024]{1,0:T(8,128)(2,1)S(1)}, bf16[256,1024]{1,0:T(8,128)(2,1)S(1)}, u32[]{:S(2)}, u32[]{:S(2)}) %collective-permute-start.1) | collective-permute-done | bytes 524320 | tf_op jit(solution)/shard_map/ppermute | solution.py:416
  35.8 4.7 %shard_map.89 = (bf16[256,1024]{1,0:T(8,128)(2,1)}, bf16[256,1024]{1,0:T(8,128)(2,1)}, bf16[256,1024]{1,0:T(8,128)(2,1)}, f32[8,128]{1,0:T(8,128)S(1)}) custom-call(bf16[256,1024]{1,0:T(8,128)(2,1)S(1)} %collective-permute-done.refs_1_.refs_0_, bf16[256,1024]{1,0:T(8,128)(2,1)S(1)} %collective-permute-done.1.refs_2_.refs_1_, ...), custom_call_target="tpu_custom_call" | custom-call | tf_op jit(solution)/shard_map/pallas_call | solution.py:190
  40.5 1.6 %collective-permute-start.12 = (bf16[256,1024]{1,0:T(8,128)(2,1)}, bf16[256,1024]{1,0:T(8,128)(2,1)}, u32[]{:S(2)}, u32[]{:S(2)}) collective-permute-start(bf16[256,1024]{1,0:T(8,128)(2,1)} %get-tuple-element.21), channel_id=1, source_target_pairs={{0,8},{4,12},{8,0},{12,4},{16,24},{20,28},{24,16},{28,20},{1,9},{5... | collective-permute-start | bytes 1572872 | tf_op jit(solution)/shard_map/ppermute | solution.py:416
  42.7 1.2 %collective-permute-start.14 = (bf16[256,1024]{1,0:T(8,128)(2,1)}, bf16[256,1024]{1,0:T(8,128)(2,1)}, u32[]{:S(2)}, u32[]{:S(2)}) collective-permute-start(bf16[256,1024]{1,0:T(8,128)(2,1)} %get-tuple-element.23), channel_id=1, source_target_pairs={{0,24},{4,28},{8,16},{12,20},{16,8},{20,12},{24,0},{28,4},{1,25},{... | collective-permute-start | bytes 1572872 | tf_op jit(solution)/shard_map/ppermute | solution.py:416
  44.0 1.8 %collective-permute-done.4.refs_3_.refs_8_ = bf16[256,1024]{1,0:T(8,128)(2,1)} collective-permute-done((bf16[256,1024]{1,0:T(8,128)(2,1)S(1)}, bf16[256,1024]{1,0:T(8,128)(2,1)}, u32[]{:S(2)}, u32[]{:S(2)}) %collective-permute-start.4) | collective-permute-done | bytes 524320 | tf_op jit(solution)/shard_map/ppermute | solution.py:413
  45.8 1.3 %all-to-all-done = bf16[32,24,128]{2,1,0:T(8,128)(2,1)S(1)} async-done(((bf16[32,24,128]{2,1,0:T(8,128)(2,1)}), bf16[32,24,128]{2,1,0:T(8,128)(2,1)S(1)}, u32[]{:S(2)}, u32[]{:S(2)}) %all-to-all-start) | async-done | bytes 196640 | tf_op jit(solution)/shard_map/all_to_all | solution.py:451
  47.1 11.1 %shard_map.90 = (bf16[1792,128]{1,0:T(8,128)(2,1)}, f32[8,128]{1,0:T(8,128)S(1)}) custom-call(s32[1]{0:T(128)S(6)} %copy.18.seed_ref, bf16[768,128]{1,0:T(8,128)(2,1)S(1)} %bitcast.22, f32[8,128]{1,0:T(8,128)S(1)} %get-tuple-element.16.after_ref), custom_call_target="tpu_custom_call" | custom-call | flops 99999997952 | tf_op jit(solution)/shard_map/pallas_call | solution.py:378
  58.2 3.3 %all-to-all-start.1 = ((bf16[32,56,128]{2,1,0:T(8,128)(2,1)}), bf16[32,56,128]{2,1,0:T(8,128)(2,1)}, u32[]{:S(2)}, u32[]{:S(2)}) async-start(bf16[32,56,128]{2,1,0:T(8,128)(2,1)} %bitcast.4), calls=%async_computation.1 | async-start | bytes 917504 | tf_op jit(solution)/shard_map/all_to_all | solution.py:486
  61.5 3.1 %shard_map.91 = (bf16[256,512]{1,0:T(8,128)(2,1)}, bf16[256,512]{1,0:T(8,128)(2,1)}, bf16[256,512]{1,0:T(8,128)(2,1)}, f32[8,128]{1,0:T(8,128)S(1)}) custom-call(bf16[256,1024]{1,0:T(8,128)(2,1)S(1)} %collective-permute-done.refs_1_.refs_0_, bf16[256,1024]{1,0:T(8,128)(2,1)S(1)} %collective-permute-done.1.refs_2_.refs_1_, ...), custom_call_target="tpu_custom_call" | custom-call | tf_op jit(solution)/shard_map/pallas_call | solution.py:190
  64.6 1.6 %collective-permute-start.9 = (bf16[256,512]{1,0:T(8,128)(2,1)}, bf16[256,512]{1,0:T(8,128)(2,1)S(1)}, u32[]{:S(2)}, u32[]{:S(2)}) collective-permute-start(bf16[256,512]{1,0:T(8,128)(2,1)} %get-tuple-element.18), channel_id=1, source_target_pairs={{0,8},{4,12},{8,0},{12,4},{16,24},{20,28},{24,16},{28,20},{1,9},{5... | collective-permute-start | bytes 786440 | tf_op jit(solution)/shard_map/ppermute | solution.py:416
  66.2 1.5 %collective-permute-start.10 = (bf16[256,512]{1,0:T(8,128)(2,1)}, bf16[256,512]{1,0:T(8,128)(2,1)S(1)}, u32[]{:S(2)}, u32[]{:S(2)}) collective-permute-start(bf16[256,512]{1,0:T(8,128)(2,1)} %get-tuple-element.19), channel_id=1, source_target_pairs={{0,16},{4,20},{8,24},{12,28},{16,0},{20,4},{24,8},{28,12},{1,17},{... | collective-permute-start | bytes 786440 | tf_op jit(solution)/shard_map/ppermute | solution.py:416
  68.1 1.3 %collective-permute-done.13.refs_1_ = bf16[256,1024]{1,0:T(8,128)(2,1)} collective-permute-done((bf16[256,1024]{1,0:T(8,128)(2,1)}, bf16[256,1024]{1,0:T(8,128)(2,1)}, u32[]{:S(2)}, u32[]{:S(2)}) %collective-permute-start.13) | collective-permute-done | bytes 524320 | tf_op jit(solution)/shard_map/ppermute | solution.py:416
  71.5 3.9 %shard_map.92.refs_3_ = bf16[256,8192]{1,0:T(8,128)(2,1)} custom-call(bf16[256,1024]{1,0:T(8,128)(2,1)} %collective-permute-done.12.refs_0_, bf16[256,1024]{1,0:T(8,128)(2,1)} %collective-permute-done.13.refs_1_, bf16[256,1024]{1,0:T(8,128)(2,1)} %collective-permute-done.14.refs_2_, ...), custom_call_target="tpu_custom_call", output_to_operand_aliasing={{}: (12, {})} | custom-call | flops 99999997952 | tf_op jit(solution)/shard_map/pallas_call | solution.py:260
  80.3 2.7 %collective-permute-done.10.refs_1_ = bf16[256,512]{1,0:T(8,128)(2,1)S(1)} collective-permute-done((bf16[256,512]{1,0:T(8,128)(2,1)}, bf16[256,512]{1,0:T(8,128)(2,1)S(1)}, u32[]{:S(2)}, u32[]{:S(2)}) %collective-permute-start.10) | collective-permute-done | bytes 262176 | tf_op jit(solution)/shard_map/ppermute | solution.py:416
  83.1 1.8 %shard_map.93 = bf16[256,8192]{1,0:T(8,128)(2,1)} custom-call(bf16[256,512]{1,0:T(8,128)(2,1)S(1)} %collective-permute-done.9.refs_0_, bf16[256,512]{1,0:T(8,128)(2,1)S(1)} %collective-permute-done.10.refs_1_, bf16[256,512]{1,0:T(8,128)(2,1)} %collective-permute-done.11.refs_2_, ...), custom_call_target="tpu_custom_call", output_to_operand_aliasing={{}: (3, {})} | custom-call | tf_op jit(solution)/shard_map/pallas_call | solution.py:260
  (49 shorter events, 11.4 us)
Async XLA Ops:
  0.6 7.2 %copy-start.1 = (bf16[256,1024]{1,0:T(8,128)(2,1)S(1)}, bf16[256,1024]{1,0:T(8,128)(2,1)}, u32[]{:S(2)}) copy-start(bf16[256,1024]{1,0:T(8,128)(2,1)} %refs_3_.1) | copy-start | bytes 1572868
  0.6 20.8 %copy-start.2 = (bf16[256,1024]{1,0:T(8,128)(2,1)S(1)}, bf16[256,1024]{1,0:T(8,128)(2,1)}, u32[]{:S(2)}) copy-start(bf16[256,1024]{1,0:T(8,128)(2,1)} %refs_3_.1) | copy-start | bytes 1572868
  0.7 20.8 %copy-start.9 = (bf16[8,1024]{1,0:T(8,128)(2,1)S(1)}, bf16[8,1024]{1,0:T(8,128)(2,1)}, u32[]{:S(2)}) copy-start(bf16[8,1024]{1,0:T(8,128)(2,1)} %refs_4_.1) | copy-start | bytes 49156
  0.7 20.8 %copy-start.3 = (bf16[8192,8]{0,1:T(8,128)(2,1)S(1)}, bf16[8192,8]{0,1:T(8,128)(2,1)}, u32[]{:S(2)}) copy-start(bf16[8192,8]{0,1:T(8,128)(2,1)} %param.9) | copy-start | bytes 393220
  2.6 25.0 %collective-permute-start.3 = (bf16[256,1024]{1,0:T(8,128)(2,1)}, bf16[256,1024]{1,0:T(8,128)(2,1)S(1)}, u32[]{:S(2)}, u32[]{:S(2)}) collective-permute-start(bf16[256,1024]{1,0:T(8,128)(2,1)} %shard_map.85), channel_id=1, source_target_pairs={{0,1},{1,2},{2,3},{3,0},{4,5},{5,6},{6,7},{7,4},{8,9},{9,10},{10,1... | collective-permute-start | bytes 1572872 | tf_op jit(solution)/shard_map/ppermute | solution.py:413
  5.7 25.6 %collective-permute-start.7 = (bf16[256,1024]{1,0:T(8,128)(2,1)}, bf16[256,1024]{1,0:T(8,128)(2,1)}, u32[]{:S(2)}, u32[]{:S(2)}) collective-permute-start(bf16[256,1024]{1,0:T(8,128)(2,1)} %shard_map.85), channel_id=1, source_target_pairs={{0,3},{1,0},{2,1},{3,2},{4,7},{5,4},{6,5},{7,6},{8,11},{9,8},{10,9... | collective-permute-start | bytes 1572872 | tf_op jit(solution)/shard_map/ppermute | solution.py:413
  7.8 24.5 %collective-permute-start.2 = (bf16[256,1024]{1,0:T(8,128)(2,1)S(1)}, bf16[256,1024]{1,0:T(8,128)(2,1)S(1)}, u32[]{:S(2)}, u32[]{:S(2)}) collective-permute-start(bf16[256,1024]{1,0:T(8,128)(2,1)S(1)} %copy-done.1), channel_id=1, source_target_pairs={{0,24},{4,28},{8,16},{12,20},{16,8},{20,12},{24,0},{28,4},{1,25},{... | collective-permute-start | bytes 1572872 | tf_op jit(solution)/shard_map/ppermute | solution.py:416
  10.4 24.4 %collective-permute-start.1 = (bf16[256,1024]{1,0:T(8,128)(2,1)S(1)}, bf16[256,1024]{1,0:T(8,128)(2,1)S(1)}, u32[]{:S(2)}, u32[]{:S(2)}) collective-permute-start(bf16[256,1024]{1,0:T(8,128)(2,1)S(1)} %copy-done.1), channel_id=1, source_target_pairs={{0,16},{4,20},{8,24},{12,28},{16,0},{20,4},{24,8},{28,12},{1,17},{... | collective-permute-start | bytes 1572872 | tf_op jit(solution)/shard_map/ppermute | solution.py:416
  10.9 24.1 %collective-permute-start = (bf16[256,1024]{1,0:T(8,128)(2,1)S(1)}, bf16[256,1024]{1,0:T(8,128)(2,1)S(1)}, u32[]{:S(2)}, u32[]{:S(2)}) collective-permute-start(bf16[256,1024]{1,0:T(8,128)(2,1)S(1)} %copy-done.1), channel_id=1, source_target_pairs={{0,8},{4,12},{8,0},{12,4},{16,24},{20,28},{24,16},{28,20},{1,9},{5... | collective-permute-start | bytes 1572872 | tf_op jit(solution)/shard_map/ppermute | solution.py:416
  16.6 30.5 %all-to-all-start = ((bf16[32,24,128]{2,1,0:T(8,128)(2,1)}), bf16[32,24,128]{2,1,0:T(8,128)(2,1)S(1)}, u32[]{:S(2)}, u32[]{:S(2)}) async-start(bf16[32,24,128]{2,1,0:T(8,128)(2,1)} %bitcast.21), calls=%async_computation | async-start | bytes 393216 | tf_op jit(solution)/shard_map/all_to_all | solution.py:451
  27.7 8.1 %collective-permute-start.6 = (bf16[256,1024]{1,0:T(8,128)(2,1)S(1)}, bf16[256,1024]{1,0:T(8,128)(2,1)S(1)}, u32[]{:S(2)}, u32[]{:S(2)}) collective-permute-start(bf16[256,1024]{1,0:T(8,128)(2,1)S(1)} %collective-permute-done.3.refs_3_.refs_4_), channel_id=1, source_target_pairs={{0,4},{4,0},{8,12},{12,8},{16,20},{20,16},{24,28},{28,24},{1,5},{5... | collective-permute-start | bytes 1572872 | tf_op jit(solution)/shard_map/ppermute | solution.py:416
  31.3 14.5 %collective-permute-start.4 = (bf16[256,1024]{1,0:T(8,128)(2,1)S(1)}, bf16[256,1024]{1,0:T(8,128)(2,1)}, u32[]{:S(2)}, u32[]{:S(2)}) collective-permute-start(bf16[256,1024]{1,0:T(8,128)(2,1)S(1)} %collective-permute-done.3.refs_3_.refs_4_), channel_id=1, source_target_pairs={{0,1},{1,2},{2,3},{3,0},{4,5},{5,6},{6,7},{7,4},{8,9},{9,10},{10,1... | collective-permute-start | bytes 1572872 | tf_op jit(solution)/shard_map/ppermute | solution.py:413
  32.4 3.4 %collective-permute-start.8 = (bf16[256,1024]{1,0:T(8,128)(2,1)}, bf16[256,1024]{1,0:T(8,128)(2,1)S(1)}, u32[]{:S(2)}, u32[]{:S(2)}) collective-permute-start(bf16[256,1024]{1,0:T(8,128)(2,1)} %collective-permute-done.7.refs_5_.refs_6_), channel_id=1, source_target_pairs={{0,4},{4,0},{8,12},{12,8},{16,20},{20,16},{24,28},{28,24},{1,5},{5... | collective-permute-start | bytes 1572872 | tf_op jit(solution)/shard_map/ppermute | solution.py:416
  35.7 10.0 %copy-start.7 = (bf16[256,1024]{1,0:T(8,128)(2,1)}, bf16[256,1024]{1,0:T(8,128)(2,1)S(1)}, u32[]{:S(2)}) copy-start(bf16[256,1024]{1,0:T(8,128)(2,1)S(1)} %collective-permute-done.8.refs_6_.refs_7_) | copy-start | bytes 1572868
  35.8 10.0 %copy-start.5 = (bf16[256,1024]{1,0:T(8,128)(2,1)}, bf16[256,1024]{1,0:T(8,128)(2,1)S(1)}, u32[]{:S(2)}) copy-start(bf16[256,1024]{1,0:T(8,128)(2,1)S(1)} %collective-permute-done.6.refs_4_.refs_5_) | copy-start | bytes 1572868
  40.5 27.2 %collective-permute-start.12 = (bf16[256,1024]{1,0:T(8,128)(2,1)}, bf16[256,1024]{1,0:T(8,128)(2,1)}, u32[]{:S(2)}, u32[]{:S(2)}) collective-permute-start(bf16[256,1024]{1,0:T(8,128)(2,1)} %get-tuple-element.21), channel_id=1, source_target_pairs={{0,8},{4,12},{8,0},{12,4},{16,24},{20,28},{24,16},{28,20},{1,9},{5... | collective-permute-start | bytes 1572872 | tf_op jit(solution)/shard_map/ppermute | solution.py:416
  42.1 27.3 %collective-permute-start.13 = (bf16[256,1024]{1,0:T(8,128)(2,1)}, bf16[256,1024]{1,0:T(8,128)(2,1)}, u32[]{:S(2)}, u32[]{:S(2)}) collective-permute-start(bf16[256,1024]{1,0:T(8,128)(2,1)} %get-tuple-element.22), channel_id=1, source_target_pairs={{0,16},{4,20},{8,24},{12,28},{16,0},{20,4},{24,8},{28,12},{1,17},{... | collective-permute-start | bytes 1572872 | tf_op jit(solution)/shard_map/ppermute | solution.py:416
  42.7 26.7 %collective-permute-start.14 = (bf16[256,1024]{1,0:T(8,128)(2,1)}, bf16[256,1024]{1,0:T(8,128)(2,1)}, u32[]{:S(2)}, u32[]{:S(2)}) collective-permute-start(bf16[256,1024]{1,0:T(8,128)(2,1)} %get-tuple-element.23), channel_id=1, source_target_pairs={{0,24},{4,28},{8,16},{12,20},{16,8},{20,12},{24,0},{28,4},{1,25},{... | collective-permute-start | bytes 1572872 | tf_op jit(solution)/shard_map/ppermute | solution.py:416
  45.8 15.7 %collective-permute-start.5 = (bf16[256,1024]{1,0:T(8,128)(2,1)}, bf16[256,1024]{1,0:T(8,128)(2,1)}, u32[]{:S(2)}, u32[]{:S(2)}) collective-permute-start(bf16[256,1024]{1,0:T(8,128)(2,1)} %collective-permute-done.4.refs_3_.refs_8_), channel_id=1, source_target_pairs={{0,4},{4,0},{8,12},{12,8},{16,20},{20,16},{24,28},{28,24},{1,5},{5... | collective-permute-start | bytes 1572872 | tf_op jit(solution)/shard_map/ppermute | solution.py:416
  58.2 17.2 %all-to-all-start.1 = ((bf16[32,56,128]{2,1,0:T(8,128)(2,1)}), bf16[32,56,128]{2,1,0:T(8,128)(2,1)}, u32[]{:S(2)}, u32[]{:S(2)}) async-start(bf16[32,56,128]{2,1,0:T(8,128)(2,1)} %bitcast.4), calls=%async_computation.1 | async-start | bytes 917504 | tf_op jit(solution)/shard_map/all_to_all | solution.py:486
  64.6 15.6 %collective-permute-start.9 = (bf16[256,512]{1,0:T(8,128)(2,1)}, bf16[256,512]{1,0:T(8,128)(2,1)S(1)}, u32[]{:S(2)}, u32[]{:S(2)}) collective-permute-start(bf16[256,512]{1,0:T(8,128)(2,1)} %get-tuple-element.18), channel_id=1, source_target_pairs={{0,8},{4,12},{8,0},{12,4},{16,24},{20,28},{24,16},{28,20},{1,9},{5... | collective-permute-start | bytes 786440 | tf_op jit(solution)/shard_map/ppermute | solution.py:416
  66.2 16.8 %collective-permute-start.10 = (bf16[256,512]{1,0:T(8,128)(2,1)}, bf16[256,512]{1,0:T(8,128)(2,1)S(1)}, u32[]{:S(2)}, u32[]{:S(2)}) collective-permute-start(bf16[256,512]{1,0:T(8,128)(2,1)} %get-tuple-element.19), channel_id=1, source_target_pairs={{0,16},{4,20},{8,24},{12,28},{16,0},{20,4},{24,8},{28,12},{1,17},{... | collective-permute-start | bytes 786440 | tf_op jit(solution)/shard_map/ppermute | solution.py:416
  67.7 15.4 %collective-permute-start.11 = (bf16[256,512]{1,0:T(8,128)(2,1)}, bf16[256,512]{1,0:T(8,128)(2,1)}, u32[]{:S(2)}, u32[]{:S(2)}) collective-permute-start(bf16[256,512]{1,0:T(8,128)(2,1)} %get-tuple-element.20), channel_id=1, source_target_pairs={{0,24},{4,28},{8,16},{12,20},{16,8},{20,12},{24,0},{28,4},{1,25},{... | collective-permute-start | bytes 786440 | tf_op jit(solution)/shard_map/ppermute | solution.py:416
  80.3 4.7 %copy-start.10 = (f32[32,128]{1,0:T(8,128)}, f32[32,128]{1,0:T(8,128)S(1)}, u32[]{:S(2)}) copy-start(f32[32,128]{1,0:T(8,128)S(1)} %broadcast_multiply_fusion) | copy-start | bytes 49156
  (4 other events, 5.2 us)

commit v7 on v6

--- a/solution.py
+++ b/solution.py
@@ -57,20 +57,36 @@
     return [member, place, lax.div(member, 2)] + [lax.rem(place + groups - s, groups) for s in range(groups)]
 
 
-def slice_kernel(width, weight_ref, out_ref, sem):
-    at = pl.multiple_of(lax.axis_index("grp") * width, width)
-    copy = pltpu.make_async_copy(weight_ref.at[pl.ds(at, width)], out_ref, sem)
-    copy.start()
-    copy.wait()
+def slice_kernel(width, weight_ref, out_ref, held_ref, sems):
+    start = lax.axis_index("grp") * width
+    rows = held_ref.shape[1]
+    parts = held_ref.shape[0]
+    taken, sent = [], []
+    for part in range(parts):
+        at = pl.multiple_of(start + part * rows, rows)
+        taken.append(pltpu.make_async_copy(weight_ref.at[pl.ds(at, rows)], held_ref.at[part], sems.at[0, part]))
+        taken[-1].start()
+    for part in range(parts):
+        taken[part].wait()
+        sent.append(
+            pltpu.make_async_copy(held_ref.at[part], out_ref.at[pl.ds(part * rows, rows)], sems.at[1, part])
+        )
+        sent[-1].start()
+    for copy in sent:
+        copy.wait()
 
 
 def member_slice(weight, width):
+    parts = 4 if width % 128 == 0 else 1
     return pl.pallas_call(
         functools.partial(slice_kernel, width),
         in_specs=[ANYWHERE],
-        out_specs=IN_VMEM,
+        out_specs=ANYWHERE,
         out_shape=jax.ShapeDtypeStruct((width, weight.shape[1]), weight.dtype),
-        scratch_shapes=[pltpu.SemaphoreType.DMA],
+        scratch_shapes=[
+            pltpu.VMEM((parts, width // parts, weight.shape[1]), weight.dtype),
+            pltpu.SemaphoreType.DMA((2, parts)),
+        ],
         cost_estimate=CHEAP,
     )(weight)
 
@@ -390,7 +406,6 @@
         ),
         out_shape=[jax.ShapeDtypeStruct((devices * tiles, 128), jnp.bfloat16), TOKEN],
         cost_estimate=DEAR,
-        compiler_params=pltpu.CompilerParams(vmem_limit_bytes=VMEM_BYTES),
     )(seed, part, after)
     return feats.reshape(devices, tiles, 128), token
 

time: 85.7 us -> 85.7 us (level)
  waiting for transfers between devices: 13.2 us -> 11.8 us
  local copies, waits for them, and re-layouts: 7.71 us -> 9.06 us
    unnamed x23 -> x29, local copies, waits for them, and re-layouts: 5.24 us -> 6.6 us
    ppermute x12, waiting for transfers between devices: 6.69 us -> 5.39 us  [across(): return lax.ppermute(array, 'grp', [(i, i ^ mask) for i in range(members)])]
    pallas_call x2, Pallas kernels: 5.78 us -> 4.83 us  [place_columns(): pl.pallas_call(functools.partial(place_kernel, shifts, chips, mine, lax.a...]
    pallas_call x1, Pallas kernels: 11.1 us -> 12.1 us  [project(): pl.pallas_call(functools.partial(project_kernel, stride, 256, width, chun...]
  transfers between devices with their start and end apart: 17 -> 17, of which waited for: 8 -> 7; matrix products, arithmetic and copies ran while one was open for 5% -> 5% of each run, Pallas kernels for 38% -> 39%
where the time goes in v7:
time: 85.7 us; the launch traced here: 85 us
  Pallas kernels  35.6 us (42%)
  starting transfers between devices  24.5 us (29%)
  waiting for transfers between devices  11.8 us (14%)
  local copies, waits for them, and re-layouts  9.06 us (11%)
  between operations  2.39 us (3%)
  other arithmetic  1.63 us (2%)
    pallas_call x1, Pallas kernels, project(): pl.pallas_call(functools.partial(project_kernel, stride, 256, width, chun...  12.1 us
    ppermute x12, starting transfers between devices, across(): return lax.ppermute(array, 'grp', [(i, i ^ mask) for i in range(members)])  10.8 us
    pallas_call x2, Pallas kernels, piece_columns(): pl.pallas_call(functools.partial(piece_kernel, shifts, chips, lax.axis_si...  7.73 us
    unnamed x29, local copies, waits for them, and re-layouts  6.6 us
    ppermute x3, starting transfers between devices, along(): lax.ppermute(array, 'fsdp', [(i, (i + shift) % groups) for i in range(gro...  6.21 us
    ppermute x12, waiting for transfers between devices, across(): return lax.ppermute(array, 'grp', [(i, i ^ mask) for i in range(members)])  5.39 us
    pallas_call x1, Pallas kernels, pair_gradient(): pl.pallas_call(functools.partial(flat_kernel, rank, groups, chunk_rows),...  5.31 us
    ppermute x3, waiting for transfers between devices, along(): lax.ppermute(array, 'fsdp', [(i, (i + shift) % groups) for i in range(gro...  5.23 us
  transfers between devices with their start and end apart: 17, of which 7 were waited for; matrix products, arithmetic and copies ran while one was open for 5% of the time, Pallas kernels for 39%

profile of v7, /device:TPU:0, one launch (start us, length us, event | category | flops | bytes accessed | tf_op | source)
XLA Modules:
  0.0 85.0 jit_solution(651289369053771043)
XLA Ops:
  0.7 1.9 %shard_map.85 = bf16[256,1024]{1,0:T(8,128)(2,1)} custom-call(bf16[2048,1024]{1,0:T(8,128)(2,1)} %weight_ref.3), custom_call_target="tpu_custom_call" | custom-call | tf_op jit(solution)/shard_map/pallas_call | solution.py:81
  2.6 3.1 %collective-permute-start.3 = (bf16[256,1024]{1,0:T(8,128)(2,1)}, bf16[256,1024]{1,0:T(8,128)(2,1)S(1)}, u32[]{:S(2)}, u32[]{:S(2)}) collective-permute-start(bf16[256,1024]{1,0:T(8,128)(2,1)} %shard_map.85), channel_id=1, source_target_pairs={{0,1},{1,2},{2,3},{3,0},{4,5},{5,6},{6,7},{7,4},{8,9},{9,10},{10,1... | collective-permute-start | bytes 1572872 | tf_op jit(solution)/shard_map/ppermute | solution.py:428
  5.7 2.1 %collective-permute-start.7 = (bf16[256,1024]{1,0:T(8,128)(2,1)}, bf16[256,1024]{1,0:T(8,128)(2,1)}, u32[]{:S(2)}, u32[]{:S(2)}) collective-permute-start(bf16[256,1024]{1,0:T(8,128)(2,1)} %shard_map.85), channel_id=1, source_target_pairs={{0,3},{1,0},{2,1},{3,2},{4,7},{5,4},{6,5},{7,6},{8,11},{9,8},{10,9... | collective-permute-start | bytes 1572872 | tf_op jit(solution)/shard_map/ppermute | solution.py:428
  7.8 2.6 %collective-permute-start.2 = (bf16[256,1024]{1,0:T(8,128)(2,1)S(1)}, bf16[256,1024]{1,0:T(8,128)(2,1)S(1)}, u32[]{:S(2)}, u32[]{:S(2)}) collective-permute-start(bf16[256,1024]{1,0:T(8,128)(2,1)S(1)} %copy-done.1), channel_id=1, source_target_pairs={{0,24},{4,28},{8,16},{12,20},{16,8},{20,12},{24,0},{28,4},{1,25},{... | collective-permute-start | bytes 1572872 | tf_op jit(solution)/shard_map/ppermute | solution.py:431
  11.3 5.3 %shard_map.86.after_ref = bf16[768,128]{1,0:T(8,128)(2,1)} custom-call(bf16[256,8192]{1,0:T(8,128)(2,1)} %in_ref.1, bf16[256,1024]{1,0:T(8,128)(2,1)} %refs_3_.1, bf16[8,8192]{1,0:T(8,128)(2,1)} %bitcast.16, bf16[8,1024]{1,0:T(8,128)(2,1)} %refs_4_.1), custom_call_target="tpu_custom_call" | custom-call | tf_op jit(solution)/shard_map/pallas_call | solution.py:333
  16.6 4.2 %all-to-all-start = ((bf16[32,24,128]{2,1,0:T(8,128)(2,1)}), bf16[32,24,128]{2,1,0:T(8,128)(2,1)S(1)}, u32[]{:S(2)}, u32[]{:S(2)}) async-start(bf16[32,24,128]{2,1,0:T(8,128)(2,1)} %bitcast.21), calls=%async_computation | async-start | bytes 393216 | tf_op jit(solution)/shard_map/all_to_all | solution.py:466
  21.5 2.2 %copy-done = bf16[2048,1024]{1,0:T(8,128)(2,1)S(1)} copy-done((bf16[2048,1024]{1,0:T(8,128)(2,1)S(1)}, bf16[2048,1024]{1,0:T(8,128)(2,1)}, u32[]{:S(2)}) %copy-start) | copy-done | bytes 4194328
  24.6 3.0 %shard_map.87 = (bf16[256,8192]{1,0:T(8,128)(2,1)}, f32[8,128]{1,0:T(8,128)S(1)}) custom-call(s32[1]{0:T(128)} %bitcast.1.info_ref, bf16[256,1024]{1,0:T(8,128)(2,1)S(1)} %copy-done.2, bf16[2048,1024]{1,0:T(8,128)(2,1)S(1)} %copy-done, bf16[8,8192]{1,0:T(8,128)(2,1)S(1)} %bitcast.17, bf16[8,1024]{1,0:T(8,128)(2,1)S(1)} %copy-done.9, ...), custom_call_target="tpu_custom_call" | custom-call | tf_op jit(solution)/shard_map/pallas_call | solution.py:112
  27.9 3.4 %collective-permute-done.7.refs_5_.refs_6_ = bf16[256,1024]{1,0:T(8,128)(2,1)} collective-permute-done((bf16[256,1024]{1,0:T(8,128)(2,1)}, bf16[256,1024]{1,0:T(8,128)(2,1)}, u32[]{:S(2)}, u32[]{:S(2)}) %collective-permute-start.7) | collective-permute-done | bytes 524320 | tf_op jit(solution)/shard_map/ppermute | solution.py:428
  32.3 2.4 %collective-permute-done.1.refs_2_.refs_1_ = bf16[256,1024]{1,0:T(8,128)(2,1)S(1)} collective-permute-done((bf16[256,1024]{1,0:T(8,128)(2,1)S(1)}, bf16[256,1024]{1,0:T(8,128)(2,1)S(1)}, u32[]{:S(2)}, u32[]{:S(2)}) %collective-permute-start.1) | collective-permute-done | bytes 524320 | tf_op jit(solution)/shard_map/ppermute | solution.py:431
  35.7 4.7 %shard_map.89 = (bf16[256,1024]{1,0:T(8,128)(2,1)}, bf16[256,1024]{1,0:T(8,128)(2,1)}, bf16[256,1024]{1,0:T(8,128)(2,1)}, f32[8,128]{1,0:T(8,128)S(1)}) custom-call(bf16[256,1024]{1,0:T(8,128)(2,1)S(1)} %collective-permute-done.refs_1_.refs_0_, bf16[256,1024]{1,0:T(8,128)(2,1)S(1)} %collective-permute-done.1.refs_2_.refs_1_, ...), custom_call_target="tpu_custom_call" | custom-call | tf_op jit(solution)/shard_map/pallas_call | solution.py:206
  40.4 1.6 %collective-permute-start.12 = (bf16[256,1024]{1,0:T(8,128)(2,1)}, bf16[256,1024]{1,0:T(8,128)(2,1)}, u32[]{:S(2)}, u32[]{:S(2)}) collective-permute-start(bf16[256,1024]{1,0:T(8,128)(2,1)} %get-tuple-element.21), channel_id=1, source_target_pairs={{0,8},{4,12},{8,0},{12,4},{16,24},{20,28},{24,16},{28,20},{1,9},{5... | collective-permute-start | bytes 1572872 | tf_op jit(solution)/shard_map/ppermute | solution.py:431
  42.7 1.2 %collective-permute-start.14 = (bf16[256,1024]{1,0:T(8,128)(2,1)}, bf16[256,1024]{1,0:T(8,128)(2,1)}, u32[]{:S(2)}, u32[]{:S(2)}) collective-permute-start(bf16[256,1024]{1,0:T(8,128)(2,1)} %get-tuple-element.23), channel_id=1, source_target_pairs={{0,24},{4,28},{8,16},{12,20},{16,8},{20,12},{24,0},{28,4},{1,25},{... | collective-permute-start | bytes 1572872 | tf_op jit(solution)/shard_map/ppermute | solution.py:431
  43.9 1.8 %collective-permute-done.4.refs_3_.refs_8_ = bf16[256,1024]{1,0:T(8,128)(2,1)} collective-permute-done((bf16[256,1024]{1,0:T(8,128)(2,1)S(1)}, bf16[256,1024]{1,0:T(8,128)(2,1)}, u32[]{:S(2)}, u32[]{:S(2)}) %collective-permute-start.4) | collective-permute-done | bytes 524320 | tf_op jit(solution)/shard_map/ppermute | solution.py:428
  45.8 1.2 %all-to-all-done = bf16[32,24,128]{2,1,0:T(8,128)(2,1)S(1)} async-done(((bf16[32,24,128]{2,1,0:T(8,128)(2,1)}), bf16[32,24,128]{2,1,0:T(8,128)(2,1)S(1)}, u32[]{:S(2)}, u32[]{:S(2)}) %all-to-all-start) | async-done | bytes 196640 | tf_op jit(solution)/shard_map/all_to_all | solution.py:466
  47.7 12.1 %shard_map.90 = (bf16[1792,128]{1,0:T(8,128)(2,1)}, f32[8,128]{1,0:T(8,128)}) custom-call(s32[1]{0:T(128)S(6)} %copy.18.seed_ref, bf16[768,128]{1,0:T(8,128)(2,1)} %bitcast.26, f32[8,128]{1,0:T(8,128)} %copy-done.12), custom_call_target="tpu_custom_call" | custom-call | flops 99999997952 | tf_op jit(solution)/shard_map/pallas_call | solution.py:394
  59.8 3.3 %all-to-all-start.1 = ((bf16[32,56,128]{2,1,0:T(8,128)(2,1)}), bf16[32,56,128]{2,1,0:T(8,128)(2,1)}, u32[]{:S(2)}, u32[]{:S(2)}) async-start(bf16[32,56,128]{2,1,0:T(8,128)(2,1)} %bitcast.24), calls=%async_computation.1 | async-start | bytes 917504 | tf_op jit(solution)/shard_map/all_to_all | solution.py:501
  63.8 3.0 %shard_map.91 = (bf16[256,512]{1,0:T(8,128)(2,1)}, bf16[256,512]{1,0:T(8,128)(2,1)}, bf16[256,512]{1,0:T(8,128)(2,1)S(1)}, f32[8,128]{1,0:T(8,128)S(1)}) custom-call(bf16[256,1024]{1,0:T(8,128)(2,1)S(1)} %collective-permute-done.refs_1_.refs_0_, bf16[256,1024]{1,0:T(8,128)(2,1)S(1)} %collective-permute-done.1.refs_2_.refs_1_, ...), custom_call_target="tpu_custom_call" | custom-call | tf_op jit(solution)/shard_map/pallas_call | solution.py:206
  66.8 1.6 %collective-permute-start.9 = (bf16[256,512]{1,0:T(8,128)(2,1)}, bf16[256,512]{1,0:T(8,128)(2,1)S(1)}, u32[]{:S(2)}, u32[]{:S(2)}) collective-permute-start(bf16[256,512]{1,0:T(8,128)(2,1)} %get-tuple-element.18), channel_id=1, source_target_pairs={{0,8},{4,12},{8,0},{12,4},{16,24},{20,28},{24,16},{28,20},{1,9},{5... | collective-permute-start | bytes 786440 | tf_op jit(solution)/shard_map/ppermute | solution.py:431
  68.4 1.5 %collective-permute-start.10 = (bf16[256,512]{1,0:T(8,128)(2,1)}, bf16[256,512]{1,0:T(8,128)(2,1)S(1)}, u32[]{:S(2)}, u32[]{:S(2)}) collective-permute-start(bf16[256,512]{1,0:T(8,128)(2,1)} %get-tuple-element.19), channel_id=1, source_target_pairs={{0,16},{4,20},{8,24},{12,28},{16,0},{20,4},{24,8},{28,12},{1,17},{... | collective-permute-start | bytes 786440 | tf_op jit(solution)/shard_map/ppermute | solution.py:431
  72.4 3.9 %shard_map.92.refs_3_ = bf16[256,8192]{1,0:T(8,128)(2,1)} custom-call(bf16[256,1024]{1,0:T(8,128)(2,1)} %collective-permute-done.12.refs_0_, bf16[256,1024]{1,0:T(8,128)(2,1)} %collective-permute-done.13.refs_1_, bf16[256,1024]{1,0:T(8,128)(2,1)} %collective-permute-done.14.refs_2_, ...), custom_call_target="tpu_custom_call", output_to_operand_aliasing={{}: (12, {})} | custom-call | flops 99999997952 | tf_op jit(solution)/shard_map/pallas_call | solution.py:276
  80.0 1.1 %reshape.52 = f32[18432]{0:T(1024)} reshape(f32[2304,8]{1,0:T(8,128)S(1)} %copy.12) | data formatting | bytes 147456 | tf_op jit(solution)/shard_map/reshape | solution.py:513
  81.2 1.7 %collective-permute-done.10.refs_1_ = bf16[256,512]{1,0:T(8,128)(2,1)S(1)} collective-permute-done((bf16[256,512]{1,0:T(8,128)(2,1)}, bf16[256,512]{1,0:T(8,128)(2,1)S(1)}, u32[]{:S(2)}, u32[]{:S(2)}) %collective-permute-start.10) | collective-permute-done | bytes 262176 | tf_op jit(solution)/shard_map/ppermute | solution.py:431
  82.9 1.1 %collective-permute-done.11.refs_2_ = bf16[256,512]{1,0:T(8,128)(2,1)S(1)} collective-permute-done((bf16[256,512]{1,0:T(8,128)(2,1)S(1)}, bf16[256,512]{1,0:T(8,128)(2,1)S(1)}, u32[]{:S(2)}, u32[]{:S(2)}) %collective-permute-start.11) | collective-permute-done | bytes 262176 | tf_op jit(solution)/shard_map/ppermute | solution.py:431
  (55 shorter events, 12.5 us)
Async XLA Ops:
  0.6 7.1 %copy-start.1 = (bf16[256,1024]{1,0:T(8,128)(2,1)S(1)}, bf16[256,1024]{1,0:T(8,128)(2,1)}, u32[]{:S(2)}) copy-start(bf16[256,1024]{1,0:T(8,128)(2,1)} %refs_3_.1) | copy-start | bytes 1572868
  0.6 20.8 %copy-start.2 = (bf16[256,1024]{1,0:T(8,128)(2,1)S(1)}, bf16[256,1024]{1,0:T(8,128)(2,1)}, u32[]{:S(2)}) copy-start(bf16[256,1024]{1,0:T(8,128)(2,1)} %refs_3_.1) | copy-start | bytes 1572868
  0.7 20.8 %copy-start.9 = (bf16[8,1024]{1,0:T(8,128)(2,1)S(1)}, bf16[8,1024]{1,0:T(8,128)(2,1)}, u32[]{:S(2)}) copy-start(bf16[8,1024]{1,0:T(8,128)(2,1)} %refs_4_.1) | copy-start | bytes 49156
  0.7 20.8 %copy-start.3 = (bf16[8192,8]{0,1:T(8,128)(2,1)S(1)}, bf16[8192,8]{0,1:T(8,128)(2,1)}, u32[]{:S(2)}) copy-start(bf16[8192,8]{0,1:T(8,128)(2,1)} %param.9) | copy-start | bytes 393220
  2.6 25.0 %collective-permute-start.3 = (bf16[256,1024]{1,0:T(8,128)(2,1)}, bf16[256,1024]{1,0:T(8,128)(2,1)S(1)}, u32[]{:S(2)}, u32[]{:S(2)}) collective-permute-start(bf16[256,1024]{1,0:T(8,128)(2,1)} %shard_map.85), channel_id=1, source_target_pairs={{0,1},{1,2},{2,3},{3,0},{4,5},{5,6},{6,7},{7,4},{8,9},{9,10},{10,1... | collective-permute-start | bytes 1572872 | tf_op jit(solution)/shard_map/ppermute | solution.py:428
  5.7 25.6 %collective-permute-start.7 = (bf16[256,1024]{1,0:T(8,128)(2,1)}, bf16[256,1024]{1,0:T(8,128)(2,1)}, u32[]{:S(2)}, u32[]{:S(2)}) collective-permute-start(bf16[256,1024]{1,0:T(8,128)(2,1)} %shard_map.85), channel_id=1, source_target_pairs={{0,3},{1,0},{2,1},{3,2},{4,7},{5,4},{6,5},{7,6},{8,11},{9,8},{10,9... | collective-permute-start | bytes 1572872 | tf_op jit(solution)/shard_map/ppermute | solution.py:428
  7.8 24.5 %collective-permute-start.2 = (bf16[256,1024]{1,0:T(8,128)(2,1)S(1)}, bf16[256,1024]{1,0:T(8,128)(2,1)S(1)}, u32[]{:S(2)}, u32[]{:S(2)}) collective-permute-start(bf16[256,1024]{1,0:T(8,128)(2,1)S(1)} %copy-done.1), channel_id=1, source_target_pairs={{0,24},{4,28},{8,16},{12,20},{16,8},{20,12},{24,0},{28,4},{1,25},{... | collective-permute-start | bytes 1572872 | tf_op jit(solution)/shard_map/ppermute | solution.py:431
  10.4 24.4 %collective-permute-start.1 = (bf16[256,1024]{1,0:T(8,128)(2,1)S(1)}, bf16[256,1024]{1,0:T(8,128)(2,1)S(1)}, u32[]{:S(2)}, u32[]{:S(2)}) collective-permute-start(bf16[256,1024]{1,0:T(8,128)(2,1)S(1)} %copy-done.1), channel_id=1, source_target_pairs={{0,16},{4,20},{8,24},{12,28},{16,0},{20,4},{24,8},{28,12},{1,17},{... | collective-permute-start | bytes 1572872 | tf_op jit(solution)/shard_map/ppermute | solution.py:431
  10.9 24.1 %collective-permute-start = (bf16[256,1024]{1,0:T(8,128)(2,1)S(1)}, bf16[256,1024]{1,0:T(8,128)(2,1)S(1)}, u32[]{:S(2)}, u32[]{:S(2)}) collective-permute-start(bf16[256,1024]{1,0:T(8,128)(2,1)S(1)} %copy-done.1), channel_id=1, source_target_pairs={{0,8},{4,12},{8,0},{12,4},{16,24},{20,28},{24,16},{28,20},{1,9},{5... | collective-permute-start | bytes 1572872 | tf_op jit(solution)/shard_map/ppermute | solution.py:431
  16.6 30.5 %all-to-all-start = ((bf16[32,24,128]{2,1,0:T(8,128)(2,1)}), bf16[32,24,128]{2,1,0:T(8,128)(2,1)S(1)}, u32[]{:S(2)}, u32[]{:S(2)}) async-start(bf16[32,24,128]{2,1,0:T(8,128)(2,1)} %bitcast.21), calls=%async_computation | async-start | bytes 393216 | tf_op jit(solution)/shard_map/all_to_all | solution.py:466
  27.6 8.1 %collective-permute-start.6 = (bf16[256,1024]{1,0:T(8,128)(2,1)S(1)}, bf16[256,1024]{1,0:T(8,128)(2,1)S(1)}, u32[]{:S(2)}, u32[]{:S(2)}) collective-permute-start(bf16[256,1024]{1,0:T(8,128)(2,1)S(1)} %collective-permute-done.3.refs_3_.refs_4_), channel_id=1, source_target_pairs={{0,4},{4,0},{8,12},{12,8},{16,20},{20,16},{24,28},{28,24},{1,5},{5... | collective-permute-start | bytes 1572872 | tf_op jit(solution)/shard_map/ppermute | solution.py:431
  31.3 14.5 %collective-permute-start.4 = (bf16[256,1024]{1,0:T(8,128)(2,1)S(1)}, bf16[256,1024]{1,0:T(8,128)(2,1)}, u32[]{:S(2)}, u32[]{:S(2)}) collective-permute-start(bf16[256,1024]{1,0:T(8,128)(2,1)S(1)} %collective-permute-done.3.refs_3_.refs_4_), channel_id=1, source_target_pairs={{0,1},{1,2},{2,3},{3,0},{4,5},{5,6},{6,7},{7,4},{8,9},{9,10},{10,1... | collective-permute-start | bytes 1572872 | tf_op jit(solution)/shard_map/ppermute | solution.py:428
  32.3 3.4 %collective-permute-start.8 = (bf16[256,1024]{1,0:T(8,128)(2,1)}, bf16[256,1024]{1,0:T(8,128)(2,1)S(1)}, u32[]{:S(2)}, u32[]{:S(2)}) collective-permute-start(bf16[256,1024]{1,0:T(8,128)(2,1)} %collective-permute-done.7.refs_5_.refs_6_), channel_id=1, source_target_pairs={{0,4},{4,0},{8,12},{12,8},{16,20},{20,16},{24,28},{28,24},{1,5},{5... | collective-permute-start | bytes 1572872 | tf_op jit(solution)/shard_map/ppermute | solution.py:431
  35.7 10.0 %copy-start.7 = (bf16[256,1024]{1,0:T(8,128)(2,1)}, bf16[256,1024]{1,0:T(8,128)(2,1)S(1)}, u32[]{:S(2)}) copy-start(bf16[256,1024]{1,0:T(8,128)(2,1)S(1)} %collective-permute-done.8.refs_6_.refs_7_) | copy-start | bytes 1572868
  35.7 10.0 %copy-start.5 = (bf16[256,1024]{1,0:T(8,128)(2,1)}, bf16[256,1024]{1,0:T(8,128)(2,1)S(1)}, u32[]{:S(2)}) copy-start(bf16[256,1024]{1,0:T(8,128)(2,1)S(1)} %collective-permute-done.6.refs_4_.refs_5_) | copy-start | bytes 1572868
  40.4 5.3 %copy-start.12 = (f32[8,128]{1,0:T(8,128)}, f32[8,128]{1,0:T(8,128)S(1)}, u32[]{:S(2)}) copy-start(f32[8,128]{1,0:T(8,128)S(1)} %get-tuple-element.16.after_ref) | copy-start | bytes 12292
  40.4 29.4 %collective-permute-start.12 = (bf16[256,1024]{1,0:T(8,128)(2,1)}, bf16[256,1024]{1,0:T(8,128)(2,1)}, u32[]{:S(2)}, u32[]{:S(2)}) collective-permute-start(bf16[256,1024]{1,0:T(8,128)(2,1)} %get-tuple-element.21), channel_id=1, source_target_pairs={{0,8},{4,12},{8,0},{12,4},{16,24},{20,28},{24,16},{28,20},{1,9},{5... | collective-permute-start | bytes 1572872 | tf_op jit(solution)/shard_map/ppermute | solution.py:431
  42.0 28.3 %collective-permute-start.13 = (bf16[256,1024]{1,0:T(8,128)(2,1)}, bf16[256,1024]{1,0:T(8,128)(2,1)}, u32[]{:S(2)}, u32[]{:S(2)}) collective-permute-start(bf16[256,1024]{1,0:T(8,128)(2,1)} %get-tuple-element.22), channel_id=1, source_target_pairs={{0,16},{4,20},{8,24},{12,28},{16,0},{20,4},{24,8},{28,12},{1,17},{... | collective-permute-start | bytes 1572872 | tf_op jit(solution)/shard_map/ppermute | solution.py:431
  42.7 27.6 %collective-permute-start.14 = (bf16[256,1024]{1,0:T(8,128)(2,1)}, bf16[256,1024]{1,0:T(8,128)(2,1)}, u32[]{:S(2)}, u32[]{:S(2)}) collective-permute-start(bf16[256,1024]{1,0:T(8,128)(2,1)} %get-tuple-element.23), channel_id=1, source_target_pairs={{0,24},{4,28},{8,16},{12,20},{16,8},{20,12},{24,0},{28,4},{1,25},{... | collective-permute-start | bytes 1572872 | tf_op jit(solution)/shard_map/ppermute | solution.py:431
  45.7 17.3 %collective-permute-start.5 = (bf16[256,1024]{1,0:T(8,128)(2,1)}, bf16[256,1024]{1,0:T(8,128)(2,1)}, u32[]{:S(2)}, u32[]{:S(2)}) collective-permute-start(bf16[256,1024]{1,0:T(8,128)(2,1)} %collective-permute-done.4.refs_3_.refs_8_), channel_id=1, source_target_pairs={{0,4},{4,0},{8,12},{12,8},{16,20},{20,16},{24,28},{28,24},{1,5},{5... | collective-permute-start | bytes 1572872 | tf_op jit(solution)/shard_map/ppermute | solution.py:431
  59.8 16.6 %all-to-all-start.1 = ((bf16[32,56,128]{2,1,0:T(8,128)(2,1)}), bf16[32,56,128]{2,1,0:T(8,128)(2,1)}, u32[]{:S(2)}, u32[]{:S(2)}) async-start(bf16[32,56,128]{2,1,0:T(8,128)(2,1)} %bitcast.24), calls=%async_computation.1 | async-start | bytes 917504 | tf_op jit(solution)/shard_map/all_to_all | solution.py:501
  66.8 14.4 %collective-permute-start.9 = (bf16[256,512]{1,0:T(8,128)(2,1)}, bf16[256,512]{1,0:T(8,128)(2,1)S(1)}, u32[]{:S(2)}, u32[]{:S(2)}) collective-permute-start(bf16[256,512]{1,0:T(8,128)(2,1)} %get-tuple-element.18), channel_id=1, source_target_pairs={{0,8},{4,12},{8,0},{12,4},{16,24},{20,28},{24,16},{28,20},{1,9},{5... | collective-permute-start | bytes 786440 | tf_op jit(solution)/shard_map/ppermute | solution.py:431
  68.4 14.5 %collective-permute-start.10 = (bf16[256,512]{1,0:T(8,128)(2,1)}, bf16[256,512]{1,0:T(8,128)(2,1)S(1)}, u32[]{:S(2)}, u32[]{:S(2)}) collective-permute-start(bf16[256,512]{1,0:T(8,128)(2,1)} %get-tuple-element.19), channel_id=1, source_target_pairs={{0,16},{4,20},{8,24},{12,28},{16,0},{20,4},{24,8},{28,12},{1,17},{... | collective-permute-start | bytes 786440 | tf_op jit(solution)/shard_map/ppermute | solution.py:431
  69.9 14.1 %collective-permute-start.11 = (bf16[256,512]{1,0:T(8,128)(2,1)S(1)}, bf16[256,512]{1,0:T(8,128)(2,1)S(1)}, u32[]{:S(2)}, u32[]{:S(2)}) collective-permute-start(bf16[256,512]{1,0:T(8,128)(2,1)S(1)} %get-tuple-element.20), channel_id=1, source_target_pairs={{0,24},{4,28},{8,16},{12,20},{16,8},{20,12},{24,0},{28,4},{1,25},{... | collective-permute-start | bytes 786440 | tf_op jit(solution)/shard_map/ppermute | solution.py:431
  (7 other events, 10.2 us)
